TPU v7x, 32 devices: a whole 2x2x4 slice. The times are simulated.
32 devices in a mesh: dp: 4 (over z), ctx: 8 (over y, x, core).
Axes of the slice: x: 2, y: 2, z: 4, core: 2. Of those that a mesh axis runs over, the one named last changes fastest.
Arguments:
- block_in: bfloat16 [8192, 2048], P(('dp', 'ctx')), may hold values from -6 to 6
- gain_attn: bfloat16 [2048], P(('dp', 'ctx')), may hold values from 0.5 to 1.5
- qkv_weight: bfloat16 [2048, 2560], P(('dp', 'ctx')), may hold values from -0.125 to 0.125
- out_weight: bfloat16 [2048, 2048], P(('dp', 'ctx')), may hold values from -0.5 to 0.5
- gain_ffn: bfloat16 [2048], P(('dp', 'ctx')), may hold values from 0.5 to 1.5
- gate_up_weight: bfloat16 [2048, 11264], P(('dp', 'ctx')), may hold values from -0.125 to 0.125
- down_weight: bfloat16 [5632, 2048], P(('dp', 'ctx')), may hold values from -0.078125 to 0.078125
- doc_lengths: int32 [4, 4], P('dp'), may hold values from 1 to 2045, as said below
- out_grad: bfloat16 [8192, 2048], P(('dp', 'ctx')), may hold values from -6 to 6
Outputs:
- block_out: bfloat16 [8192, 2048], P(('dp', 'ctx'))
- input_grad: float32 [8192, 2048], P(('dp', 'ctx'))
- gain_attn_grad: float32 [2048], P(('dp', 'ctx'))
- qkv_weight_grad: float32 [2048, 2560], P(('dp', 'ctx'))
- out_weight_grad: float32 [2048, 2048], P(('dp', 'ctx'))
- gain_ffn_grad: float32 [2048], P(('dp', 'ctx'))
- gate_up_weight_grad: float32 [2048, 11264], P(('dp', 'ctx'))
- down_weight_grad: float32 [5632, 2048], P(('dp', 'ctx'))
Inputs may be any that keep to these rules, and one draw needn't show every extreme that they name: `doc_lengths`: each sequence holds 4 documents; the second starts within the sequence's first 256 tokens and ends within its last 256; the others have 1 to 127 tokens each, and the lengths of a sequence add up to 2048; in one sequence the others have 1 token each.
All inputs are finite; a program needn't handle non-finite values.
Results may differ from a plain program's by a relative error of at most 0.015.
Values may be sent and summed in bfloat16 or wider, within the bound.
No kernel may reach another device: no remote copies, remote signals or barrier semaphores. Data moves between devices by JAX's collectives and lax.ppermute only.
A program may use at most 384 MiB of HBM per device.

v0:
```python
import jax
import jax.numpy as jnp
import numpy as np
from jax import lax
from jax.experimental import pallas as pl
from jax.experimental.pallas import tpu as pltpu
from jax.sharding import PartitionSpec as P

D = 2048
H = 32
KVH = 4
HD = 64
FF = 5632
HALF = HD // 2

EPS = 1e-05
MASKED = -1e30
BF = jnp.bfloat16
F32 = jnp.float32
VMEM_LIMIT = 60 << 20
SHORT = pl.CostEstimate(flops=1 << 20, bytes_accessed=1 << 20, transcendentals=0)
MEDIUM = pl.CostEstimate(flops=2 * 10**10, bytes_accessed=1 << 20, transcendentals=0)
LONG = pl.CostEstimate(flops=10**11, bytes_accessed=1 << 20, transcendentals=0)


def nt(a, b):
    return lax.dot_general(a, b, (((1,), (1,)), ((), ())), preferred_element_type=F32)


def nn(a, b):
    return jnp.dot(a, b, preferred_element_type=F32)


def after(x, *earlier):
    return lax.optimization_barrier((x, *earlier))[0]


def after_each(values, *earlier):
    count = len(values)
    return lax.optimization_barrier((*values, *earlier))[:count]


def walk(n_ctx, parity):
    bits = []
    bit = 2
    while bit < n_ctx:
        bits.append(bit)
        bit *= 2
    return bits if parity == 0 else bits[::-1]


def swap_stage(x, n_ctx, stage):
    pairs = [(c, c ^ walk(n_ctx, c % 2)[stage]) for c in range(n_ctx)]
    return lax.ppermute(x, "ctx", pairs)


def swap_core(x, n_ctx):
    return lax.ppermute(x, "ctx", [(c, c ^ 1) for c in range(n_ctx)])


def slot_table(n_ctx):
    lists = []
    for parity in (0, 1):
        row = [0]
        for bit in walk(n_ctx, parity):
            row = row + [v ^ bit for v in row]
        lists.append(row)
    return np.array(
        [lists[p] + [v ^ 1 for v in lists[1 - p]] for p in (0, 1)], dtype=np.int32
    )


def gather_direct(x, n_ctx):
    return [x] + [swap_stage(x, n_ctx, stage) for stage in range(len(walk(n_ctx, 0)))]


def gather_rest(direct, n_ctx, earlier=(), last=()):
    have = direct[:1]
    for stage in range(len(walk(n_ctx, 0))):
        passed = [after(block, *earlier) if earlier else block for block in have[1:]]
        have = have + [direct[stage + 1]] + [swap_stage(block, n_ctx, stage) for block in passed]
    return have + [swap_core(after(block, *last) if last else block, n_ctx) for block in have]


def gather_at_once(x, n_ctx):
    have = [x]
    table = slot_table(n_ctx)
    for slot in range(1, n_ctx // 2):
        pairs = [(c, c ^ int(table[c % 2][slot])) for c in range(n_ctx)]
        have.append(lax.ppermute(x, "ctx", pairs))
    return have, [swap_core(block, n_ctx) for block in have]


def gather_slots(x, n_ctx):
    return gather_rest(gather_direct(x, n_ctx), n_ctx)


def scatter_pairs(term, tok, n_ctx):
    mine = n_ctx // 2
    cut = mine // 2
    sums, arrivals = [], []
    for lo, hi in ((cut, mine), (0, cut)):
        arrivals.append(swap_core(term(mine + lo, mine + hi).astype(BF), n_ctx))
        sums.append(term(lo, hi) + arrivals[-1].astype(F32))
    return sums, arrivals


def scatter_chips(upper, lower, stages, n_ctx, *earlier):
    for stage in stages:
        if earlier and stage == 0:
            upper = after(upper.astype(BF), *earlier)
        lower = lower + swap_stage(upper.astype(BF), n_ctx, stage).astype(F32)
        if stage:
            half = lower.shape[0] // 2
            upper, lower = lower[half:], lower[:half]
    return lower if stages[-1] == 0 else (upper, lower)


def scatter_rest(lower, arrived, stages, n_ctx):
    sums = lower + arrived.astype(F32)
    if len(stages) == 1:
        return sums
    half = sums.shape[0] // 2
    return scatter_chips(sums[half:], sums[:half], stages[1:], n_ctx)


def exchange(x):
    return lax.all_to_all(x, "ctx", split_axis=0, concat_axis=0, tiled=False)


def gather_dp(x):
    return lax.all_gather(x, "dp", axis=0, tiled=True)


def scatter_dp(x):
    return lax.psum_scatter(x, "dp", scatter_dimension=0, tiled=True)


def fetch_piece(pieces, buffer, semaphores, count=1):
    step = pl.program_id(0)

    @pl.when(step == 0)
    def _():
        for i, piece in enumerate(pieces):
            pltpu.make_async_copy(piece, buffer.at[i], semaphores.at[i]).start()

    for i in range(count):
        at = step * count + i
        pltpu.make_async_copy(pieces[0], buffer.at[at], semaphores.at[at]).wait()
    if count == 1:
        return buffer[step]
    return buffer[pl.ds(step * count, count)].reshape(count * buffer.shape[1], buffer.shape[2])


def keep_pieces(buffer, target, semaphores, count=1):
    step = pl.program_id(0)
    total, tok = buffer.shape[0], buffer.shape[1]

    def copy(at):
        rows = pl.ds(pl.multiple_of(at * tok, tok), tok)
        return pltpu.make_async_copy(buffer.at[at], target.at[rows], semaphores.at[at])

    for i in range(count):
        copy(step * count + i).start()

    @pl.when(step == total // count - 1)
    def _():
        for i in range(total):
            copy(i).wait()


def store_rows(source, target, semaphores):
    count = semaphores.shape[0]
    rows = source.shape[0] // count
    copies = [
        pltpu.make_async_copy(
            source.at[pl.ds(i * rows, rows)], target.at[pl.ds(i * rows, rows)], semaphores.at[i]
        )
        for i in range(count)
    ]
    for copy in copies:
        copy.start()
    return copies


def chunks(rows):
    return next(count for count in (8, 4, 2, 1) if rows % (16 * count) == 0)


def fetch_rows(source, buffer, semaphores):
    count = semaphores.shape[0]
    rows = source.shape[0] // count

    @pl.when(pl.program_id(0) == 0)
    def _():
        copies = [
            pltpu.make_async_copy(
                source.at[pl.ds(i * rows, rows)], buffer.at[pl.ds(i * rows, rows)], semaphores.at[i]
            )
            for i in range(count)
        ]
        for copy in copies:
            copy.start()
        for copy in copies:
            copy.wait()


def swap_halves(x):
    return pltpu.roll(x, x.shape[1] // 2, axis=1)


def turn_tables(cosine, sine, width):
    times = width // 128
    cosine = jnp.concatenate([cosine] * times, axis=1) if times > 1 else cosine
    sine = jnp.concatenate([sine] * times, axis=1) if times > 1 else sine
    lane = lax.broadcasted_iota(jnp.int32, sine.shape, 1)
    return cosine, jnp.where(lane < width // 2, -sine, sine)


def any_specs(pieces):
    return [pl.BlockSpec(memory_space=pltpu.HBM) for _ in pieces]


def project_qkv(order, pieces, weight, spread, widen, cosine, sine, width, tok):
    n = len(pieces)
    seq = n * tok

    def kernel(order_ref, *refs):
        parts = refs[:n]
        w_hbm, spread_ref, widen_ref, cos_ref, sin_ref = refs[n : n + 5]
        (
            q_ref, k_ref, v_ref, kt_ref, vt_ref, all_hbm, wide, buffer, semaphores, keep_semaphores, w_ref, w_semaphores
        ) = refs[n + 5 :]
        fetch_rows(w_hbm, w_ref, w_semaphores)

        @pl.when(pl.program_id(0) == 0)
        def _():
            wide[...] = nn(w_ref[...], spread_ref[...]).astype(BF)

        x = fetch_piece(parts, buffer, semaphores)
        keep_pieces(buffer, all_hbm, keep_semaphores)
        mixed = nn(x, wide[...])
        cos, sin = turn_tables(cos_ref[...], sin_ref[...], width)
        q = mixed[:, :width]
        q_ref[...] = (q * cos + swap_halves(q) * sin).astype(BF) * (HD**-0.5)
        lane = lax.broadcasted_iota(jnp.int32, (tok, 128), 1)
        key_sine = jnp.where(lane < HALF, -sin_ref[...], sin_ref[...])
        both = jnp.where(
            lane < HD,
            mixed[:, width : width + 128] * cos_ref[...] + mixed[:, width + 128 :] * key_sine,
            mixed[:, width : width + 128],
        ).astype(BF)
        repeated = nn(both, widen_ref[...]).astype(BF)
        k_ref[...] = repeated[:, :width]
        v_ref[...] = repeated[:, width:]
        turned = both.T
        kt_ref[...] = turned[:HD]
        vt_ref[...] = turned[HD:]

    rows = lambda s, order: (order[s], 0)
    lanes = lambda s, order: (0, order[s])
    whole = lambda s, order: (0, 0)
    return pl.pallas_call(
        kernel,
        grid_spec=pltpu.PrefetchScalarGridSpec(
            num_scalar_prefetch=1,
            grid=(n,),
            in_specs=any_specs(pieces)
            + [
                pl.BlockSpec(memory_space=pltpu.HBM),
                pl.BlockSpec(spread.shape, whole),
                pl.BlockSpec(widen.shape, whole),
                pl.BlockSpec((tok, 128), rows),
                pl.BlockSpec((tok, 128), rows),
            ],
            out_specs=[
                pl.BlockSpec((tok, width), rows),
                pl.BlockSpec((tok, width), rows),
                pl.BlockSpec((tok, width), rows),
                pl.BlockSpec((HD, tok), lanes),
                pl.BlockSpec((HD, tok), lanes),
                pl.BlockSpec(memory_space=pltpu.HBM),
            ],
            scratch_shapes=[
                pltpu.VMEM((D, width + 256), BF),
                pltpu.VMEM((n, tok, D), BF),
                pltpu.SemaphoreType.DMA((n,)),
                pltpu.SemaphoreType.DMA((n,)),
                pltpu.VMEM(weight.shape, BF),
                pltpu.SemaphoreType.DMA((chunks(D),)),
            ],
        ),
        out_shape=[
            jax.ShapeDtypeStruct((seq, width), BF),
            jax.ShapeDtypeStruct((seq, width), BF),
            jax.ShapeDtypeStruct((seq, width), BF),
            jax.ShapeDtypeStruct((HD, seq), BF),
            jax.ShapeDtypeStruct((HD, seq), BF),
            jax.ShapeDtypeStruct((seq, D), BF),
        ],
        compiler_params=pltpu.CompilerParams(vmem_limit_bytes=VMEM_LIMIT),
        cost_estimate=LONG,
        name="project_qkv",
    )(order, *pieces, weight, spread, widen, cosine, sine)


def project_out(order, heads_in, pieces, residual):
    n, tok, width = heads_in.shape

    def kernel(order_ref, a_ref, *refs):
        parts = refs[:n]
        x_ref, state_hbm, norm_hbm, buffer, semaphores, state_ref, norm_ref, out_semaphores = refs[n:]
        step = pl.program_id(0)
        w = fetch_piece(parts, buffer, semaphores)

        @pl.when(step == 0)
        def _():
            state_ref[...] = x_ref[...].astype(F32)

        state_ref[...] += nn(a_ref[0], w)

        @pl.when(step == n - 1)
        def _():
            state = state_ref[...]
            scale = lax.rsqrt(jnp.mean(state * state, axis=-1, keepdims=True) + EPS)
            copies = store_rows(state_ref, state_hbm, out_semaphores.at[0])
            norm_ref[...] = (state * scale).astype(BF)
            copies += store_rows(norm_ref, norm_hbm, out_semaphores.at[1])
            for copy in copies:
                copy.wait()

    whole = lambda s, order: (0, 0)
    return pl.pallas_call(
        kernel,
        grid_spec=pltpu.PrefetchScalarGridSpec(
            num_scalar_prefetch=1,
            grid=(n,),
            in_specs=[pl.BlockSpec((1, tok, width), lambda s, order: (order[s], 0, 0))]
            + any_specs(pieces)
            + [pl.BlockSpec((tok, D), whole)],
            out_specs=[pl.BlockSpec(memory_space=pltpu.HBM)] * 2,
            scratch_shapes=[
                pltpu.VMEM((n, width, D), BF),
                pltpu.SemaphoreType.DMA((n,)),
                pltpu.VMEM((tok, D), F32),
                pltpu.VMEM((tok, D), BF),
                pltpu.SemaphoreType.DMA((2, 4)),
            ],
        ),
        out_shape=[
            jax.ShapeDtypeStruct((tok, D), F32),
            jax.ShapeDtypeStruct((tok, D), BF),
        ],
        compiler_params=pltpu.CompilerParams(vmem_limit_bytes=VMEM_LIMIT),
        cost_estimate=SHORT,
        name="project_out",
    )(order, heads_in, *pieces, residual)


def feed_forward(pieces, weight):
    n = len(pieces)
    tok = 2 * pieces[0].shape[0]
    seq = n * tok // 2
    ff = weight.shape[1] // 2

    def kernel(*refs):
        parts = refs[:n]
        w_hbm, hidden_ref, factor_ref, all_hbm, buffer, semaphores, keep_semaphores, w_ref, w_semaphores = refs[n:]
        fetch_rows(w_hbm, w_ref, w_semaphores)
        x = fetch_piece(parts, buffer, semaphores, 2)
        keep_pieces(buffer, all_hbm, keep_semaphores, 2)
        both = nn(x, w_ref[...])
        gate = both[:, :ff]
        up = both[:, ff:]
        sig = jax.nn.sigmoid(gate)
        silu = gate * sig
        hidden_ref[...] = (silu * up).astype(BF)
        factor_ref[:, :ff] = (up * sig * (1.0 + gate * (1.0 - sig))).astype(BF)
        factor_ref[:, ff:] = silu.astype(BF)

    rows = lambda s: (s, 0)
    return pl.pallas_call(
        kernel,
        grid=(n // 2,),
        in_specs=any_specs(pieces) + [pl.BlockSpec(memory_space=pltpu.HBM)],
        out_specs=[
            pl.BlockSpec((tok, ff), rows),
            pl.BlockSpec((tok, 2 * ff), rows),
            pl.BlockSpec(memory_space=pltpu.HBM),
        ],
        scratch_shapes=[
            pltpu.VMEM((n, tok // 2, D), BF),
            pltpu.SemaphoreType.DMA((n,)),
            pltpu.SemaphoreType.DMA((n,)),
            pltpu.VMEM(weight.shape, BF),
            pltpu.SemaphoreType.DMA((chunks(D),)),
        ],
        out_shape=[
            jax.ShapeDtypeStruct((seq, ff), BF),
            jax.ShapeDtypeStruct((seq, 2 * ff), BF),
            jax.ShapeDtypeStruct((seq, D), BF),
        ],
        compiler_params=pltpu.CompilerParams(vmem_limit_bytes=VMEM_LIMIT),
        cost_estimate=LONG,
        name="feed_forward",
    )(*pieces, weight)


def feed_backward(factors, grads, weight):
    seq = factors.shape[0]
    ff = weight.shape[0]
    tok = 512

    def kernel(factor_ref, g_ref, w_hbm, out_ref, w_ref, w_semaphores, turned):
        fetch_rows(w_hbm, w_ref, w_semaphores)

        @pl.when(pl.program_id(0) == 0)
        def _():
            turned[...] = w_ref[...].T

        grad_hidden = nn(g_ref[...], turned[...])
        factor = factor_ref[...].astype(F32)
        out_ref[:, :ff] = (grad_hidden * factor[:, :ff]).astype(BF)
        out_ref[:, ff:] = (grad_hidden * factor[:, ff:]).astype(BF)

    rows = lambda s: (s, 0)
    return pl.pallas_call(
        kernel,
        grid=(seq // tok,),
        in_specs=[
            pl.BlockSpec((tok, 2 * ff), rows),
            pl.BlockSpec((tok, D), rows),
            pl.BlockSpec(memory_space=pltpu.HBM),
        ],
        out_specs=pl.BlockSpec((tok, 2 * ff), rows),
        scratch_shapes=[
            pltpu.VMEM(weight.shape, BF),
            pltpu.SemaphoreType.DMA((chunks(ff),)),
            pltpu.VMEM((D, ff), BF),
        ],
        out_shape=jax.ShapeDtypeStruct((seq, 2 * ff), BF),
        compiler_params=pltpu.CompilerParams(vmem_limit_bytes=VMEM_LIMIT),
        cost_estimate=LONG,
        name="feed_backward",
    )(factors, grads, weight)


def lay_out(pieces):
    n = len(pieces)
    tok = pieces[0].shape[0]

    def kernel(*refs):
        parts = refs[:n]
        out_ref, buffer, in_semaphores, out_semaphores = refs[n:]
        arrive = [
            pltpu.make_async_copy(part, buffer.at[i], in_semaphores.at[i])
            for i, part in enumerate(parts)
        ]
        leave = [
            pltpu.make_async_copy(buffer.at[i], out_ref.at[pl.ds(i * tok, tok)], out_semaphores.at[i])
            for i in range(n)
        ]
        for copy in arrive:
            copy.start()
        for i in range(n):
            arrive[i].wait()
            leave[i].start()
        for copy in leave:
            copy.wait()

    return pl.pallas_call(
        kernel,
        in_specs=any_specs(pieces),
        out_specs=pl.BlockSpec(memory_space=pltpu.HBM),
        scratch_shapes=[
            pltpu.VMEM((n, tok, D), BF),
            pltpu.SemaphoreType.DMA((n,)),
            pltpu.SemaphoreType.DMA((n,)),
        ],
        out_shape=jax.ShapeDtypeStruct((n * tok, D), BF),
        compiler_params=pltpu.CompilerParams(vmem_limit_bytes=VMEM_LIMIT),
        cost_estimate=SHORT,
        name="lay_out",
    )(*pieces)


def branch_back(order, d_two, state, out_grad, pieces):
    n = len(pieces)
    tok = d_two.shape[0]
    width = pieces[0].shape[0]

    def kernel(order_ref, d_ref, state_ref, g_ref, *refs):
        parts = refs[:n]
        grad_hbm, branch_hbm, heads_ref, buffer, semaphores, grad_ref, branch_ref, out_semaphores = refs[n:]

        @pl.when(pl.program_id(0) == 0)
        def _():
            state = state_ref[...]
            scale = lax.rsqrt(jnp.mean(state * state, axis=-1, keepdims=True) + EPS)
            norm = state * scale
            d = d_ref[...]
            grad = g_ref[...].astype(F32) + scale * (
                d - norm * jnp.mean(d * norm, axis=-1, keepdims=True)
            )
            grad_ref[...] = grad
            branch_ref[...] = grad.astype(BF)
            store_rows(grad_ref, grad_hbm, out_semaphores.at[0])
            store_rows(branch_ref, branch_hbm, out_semaphores.at[1])

        w = fetch_piece(parts, buffer, semaphores)
        heads_ref[0] = nt(branch_ref[...], w).astype(BF)

        @pl.when(pl.program_id(0) == n - 1)
        def _():
            for source, target, at in ((grad_ref, grad_hbm, 0), (branch_ref, branch_hbm, 1)):
                rows = tok // 4
                for i in range(4):
                    cut = pl.ds(i * rows, rows)
                    pltpu.make_async_copy(source.at[cut], target.at[cut], out_semaphores.at[at, i]).wait()

    whole = lambda s, order: (0, 0)
    return pl.pallas_call(
        kernel,
        grid_spec=pltpu.PrefetchScalarGridSpec(
            num_scalar_prefetch=1,
            grid=(n,),
            in_specs=[
                pl.BlockSpec((tok, D), whole),
                pl.BlockSpec((tok, D), whole),
                pl.BlockSpec((tok, D), whole),
            ]
            + any_specs(pieces),
            out_specs=[
                pl.BlockSpec(memory_space=pltpu.HBM),
                pl.BlockSpec(memory_space=pltpu.HBM),
                pl.BlockSpec((1, tok, width), lambda s, order: (order[s], 0, 0)),
            ],
            scratch_shapes=[
                pltpu.VMEM((n, width, D), BF),
                pltpu.SemaphoreType.DMA((n,)),
                pltpu.VMEM((tok, D), F32),
                pltpu.VMEM((tok, D), BF),
                pltpu.SemaphoreType.DMA((2, 4)),
            ],
        ),
        out_shape=[
            jax.ShapeDtypeStruct((tok, D), F32),
            jax.ShapeDtypeStruct((tok, D), BF),
            jax.ShapeDtypeStruct((n, tok, width), BF),
        ],
        compiler_params=pltpu.CompilerParams(vmem_limit_bytes=VMEM_LIMIT),
        cost_estimate=SHORT,
        name="branch_back",
    )(order, d_two, state, out_grad, *pieces)


def split_columns(weight, gain, n_ctx, n_dp, ff_rows):
    rows = weight.shape[0]
    ff = ff_rows * n_dp

    def kernel(w_ref, gain_ref, out_ref):
        gains = gain_ref[...]
        for part in range(2):
            for d in range(n_dp):
                for c in range(n_ctx):
                    at = part * FF + (d * n_ctx + c) * ff_rows
                    to = part * ff + d * ff_rows
                    values = w_ref[:, at : at + ff_rows].astype(F32) * gains
                    out_ref[c, :, to : to + ff_rows] = values.astype(BF)

    return pl.pallas_call(
        kernel,
        in_specs=[pl.BlockSpec(memory_space=pltpu.VMEM)] * 2,
        out_specs=pl.BlockSpec(memory_space=pltpu.VMEM),
        out_shape=jax.ShapeDtypeStruct((n_ctx, rows, 2 * ff), BF),
        compiler_params=pltpu.CompilerParams(vmem_limit_bytes=VMEM_LIMIT),
        cost_estimate=LONG,
        name="split_columns",
    )(weight, gain)


def join_columns(sums, weight, gain, n_dp, ff_rows):
    n_ctx, rows, both = sums.shape
    ff = both // 2

    def kernel(s_ref, w_ref, gain_ref, out_ref, gain_out_ref):
        gains = gain_ref[...]
        total = jnp.zeros((rows, ff_rows), F32)
        for part in range(2):
            for d in range(n_dp):
                for c in range(n_ctx):
                    at = part * ff + d * ff_rows
                    to = part * FF + (d * n_ctx + c) * ff_rows
                    values = s_ref[c, :, at : at + ff_rows].astype(F32)
                    total = total + values * w_ref[:, to : to + ff_rows].astype(F32)
                    out_ref[:, to : to + ff_rows] = values * gains
        gain_out_ref[...] = jnp.sum(total, axis=1, keepdims=True)

    return pl.pallas_call(
        kernel,
        in_specs=[pl.BlockSpec(memory_space=pltpu.VMEM)] * 3,
        out_specs=[pl.BlockSpec(memory_space=pltpu.VMEM)] * 2,
        out_shape=[
            jax.ShapeDtypeStruct((rows, 2 * FF), F32),
            jax.ShapeDtypeStruct((rows, 1), F32),
        ],
        compiler_params=pltpu.CompilerParams(vmem_limit_bytes=VMEM_LIMIT),
        cost_estimate=LONG,
        name="join_columns",
    )(sums, weight, gain)


def lane_heads(rows, width):
    lane = lax.broadcasted_iota(jnp.int32, (rows, width), 1)
    return (lane % (width // 2)) // HALF


def attend_forward(slot_of, starts, queries, keys, values_t, heads, tok, first, count, before):
    seq, width = queries.shape
    blocks = seq // tok
    span = 2 * tok

    def kernel(slot_ref, start_ref, q_ref, k_ref, v_ref, *refs):
        attn_ref, slot_attn_ref, full_ref, lse_ref, scores = refs[len(before) :]
        block = first + pl.program_id(0)
        steps = (block + 2) // 2
        start = start_ref[...]
        here = block * tok + lax.broadcasted_iota(jnp.int32, (1, tok), 1)
        head_of = lane_heads(tok, width)
        q = q_ref[...]
        q_heads = [jnp.where(head_of == h, q, jnp.zeros_like(q)) for h in range(heads)]

        def score(i, peaks):
            rows = pl.ds(pl.multiple_of(i * span, span), span)
            k = k_ref[rows, :]
            there = i * span + lax.broadcasted_iota(jnp.int32, (span, tok), 0)
            visible = (there >= start) & (there <= here)
            out = []
            for h in range(heads):
                s = jnp.where(visible, nt(k, q_heads[h]), MASKED)
                scores[h, rows, :] = s
                out.append(jnp.maximum(peaks[h], jnp.max(s.reshape(span // 8, 8, tok), axis=0)))
            return tuple(out)

        peaks = lax.fori_loop(
            0, steps, score, tuple(jnp.full((8, tok), MASKED, F32) for _ in range(heads))
        )
        peaks = [jnp.max(peak, axis=0, keepdims=True) for peak in peaks]

        def weigh(i, running):
            rows = pl.ds(pl.multiple_of(i * span, span), span)
            v = v_ref[:, rows]
            out = []
            for h in range(heads):
                total, acc = running[h]
                p = jnp.exp(scores[h, rows, :] - peaks[h])
                total = total + jnp.sum(p.reshape(span // 8, 8, tok), axis=0)
                out.append((total, acc + nn(v, p.astype(BF))))
            return tuple(out)

        result = lax.fori_loop(
            0,
            steps,
            weigh,
            tuple((jnp.zeros((8, tok), F32), jnp.zeros((HD, tok), F32)) for _ in range(heads)),
        )
        rows = []
        for h in range(heads):
            total, acc = result[h]
            total = jnp.sum(total, axis=0, keepdims=True)
            rows.append(acc / total)
            lse_ref[0, h : h + 1, :] = peaks[h] + jnp.log(total)
        full = jnp.concatenate(rows, axis=0).T
        full_ref[...] = full
        attn_ref[...] = full.astype(BF)
        slot_attn_ref[...] = full.astype(BF)

    return pl.pallas_call(
        kernel,
        grid_spec=pltpu.PrefetchScalarGridSpec(
            num_scalar_prefetch=1,
            grid=(count,),
            in_specs=[
                pl.BlockSpec((1, tok), lambda j, slot: (0, first + j)),
                pl.BlockSpec((tok, width), lambda j, slot: (first + j, 0)),
                pl.BlockSpec((seq, width), lambda j, slot: (0, 0)),
                pl.BlockSpec((HD, seq), lambda j, slot: (0, 0)),
            ]
            + [pl.BlockSpec(memory_space=pltpu.HBM)] * len(before),
            out_specs=[
                pl.BlockSpec((tok, width), lambda j, slot: (first + j, 0)),
                pl.BlockSpec((tok, width), lambda j, slot: (slot[first + j], 0)),
                pl.BlockSpec((tok, width), lambda j, slot: (first + j, 0)),
                pl.BlockSpec((1, heads, tok), lambda j, slot: (first + j, 0, 0)),
            ],
            scratch_shapes=[pltpu.VMEM((heads, seq, tok), F32)],
        ),
        out_shape=[
            jax.ShapeDtypeStruct((seq, width), BF),
            jax.ShapeDtypeStruct((seq, width), BF),
            jax.ShapeDtypeStruct((seq, width), F32),
            jax.ShapeDtypeStruct((blocks, heads, tok), F32),
        ],
        input_output_aliases={5 + i: i for i in range(len(before))},
        compiler_params=pltpu.CompilerParams(vmem_limit_bytes=VMEM_LIMIT),
        cost_estimate=LONG,
        name="attend_forward",
    )(slot_of, starts, queries, keys, values_t, *before)


def attend_backward(
    slot_of, starts, queries, keys, keys_t, values, grads, full, lse, cosine, sine, unsplit, heads, tok
):
    seq, width = queries.shape
    blocks = seq // tok
    span = 2 * tok
    half = width // 2

    def kernel(
        slot_ref, start_ref, q_ref, k_ref, kt_ref, v_ref, g_ref, full_ref, lse_ref, cos_ref, sin_ref, unsplit_ref,
        out_ref, dk, dv,
    ):
        block = pl.program_id(0)
        steps = (block + 2) // 2

        @pl.when(block == 0)
        def _():
            dk[...] = jnp.zeros_like(dk)
            dv[...] = jnp.zeros_like(dv)

        start = start_ref[...]
        here = block * tok + lax.broadcasted_iota(jnp.int32, (1, tok), 1)
        head_of = lane_heads(tok, width)
        wide = lax.broadcasted_iota(jnp.int32, (tok, width), 1) // HD
        q = q_ref[...]
        g = g_ref[...]
        q_heads = [jnp.where(head_of == h, q, jnp.zeros_like(q)) for h in range(heads)]
        g_heads = [jnp.where(wide == h, g, jnp.zeros_like(g)) for h in range(heads)]
        q_stack = jnp.concatenate(q_heads, axis=0)
        g_stack = jnp.concatenate(g_heads, axis=0)
        picks = (
            lax.broadcasted_iota(jnp.int32, (8, width), 1) // HD
            == lax.broadcasted_iota(jnp.int32, (8, width), 0)
        ).astype(F32)
        deltas = lax.dot_general(
            picks,
            g.astype(F32) * full_ref[...],
            (((1,), (1,)), ((), ())),
            preferred_element_type=F32,
            precision=lax.Precision.HIGHEST,
        )

        def step(i, dq):
            rows = pl.ds(pl.multiple_of(i * span, span), span)
            k = k_ref[rows, :]
            v = v_ref[rows, :]
            kt = kt_ref[:, rows]
            there = i * span + lax.broadcasted_iota(jnp.int32, (span, tok), 0)
            visible = (there >= start) & (there <= here)
            probs, grad_scores, out = [], [], []
            for h in range(heads):
                s = jnp.where(visible, nt(k, q_heads[h]), MASKED)
                p = jnp.exp(s - lse_ref[0, h : h + 1, :])
                ds = (p * (nt(v, g_heads[h]) - deltas[h : h + 1, :])).astype(BF)
                probs.append(p.astype(BF))
                grad_scores.append(ds)
                out.append(dq[h] + nn(kt, ds))
            dv[rows, :] += nn(jnp.concatenate(probs, axis=1), g_stack)
            dk[rows, :] += nn(jnp.concatenate(grad_scores, axis=1), q_stack)
            return tuple(out)

        dq = lax.fori_loop(
            0, steps, step, tuple(jnp.zeros((HD, tok), F32) for _ in range(heads))
        )
        dq = jnp.concatenate([x[:HALF] for x in dq] + [x[HALF:] for x in dq], axis=0).T
        here_rows = pl.ds(pl.multiple_of(block * tok, tok), tok)
        cos, sin = turn_tables(cos_ref[here_rows, :], sin_ref[here_rows, :], width)
        dq = (dq * cos - swap_halves(dq) * sin) * (HD**-0.5)
        slot_rows = pl.ds(pl.multiple_of(slot_ref[block] * tok, tok), tok)
        out_ref[slot_rows, :width] = nn(dq.astype(BF), unsplit_ref[...]).astype(BF)

        @pl.when(block == blocks - 1)
        def _():
            lane = lax.broadcasted_iota(jnp.int32, (width, 128), 0)
            column = lax.broadcasted_iota(jnp.int32, (width, 128), 1)
            fold_k = ((lane // half) * HALF + lane % HALF == column).astype(BF)
            fold_v = (lane % HD + HD == column).astype(BF)

            def fold(i, unused):
                rows = pl.ds(pl.multiple_of(i * tok, tok), tok)
                cos, sin = turn_tables(cos_ref[rows, :], sin_ref[rows, :], width)
                a = dk[rows, :]
                a = a * cos - swap_halves(a) * sin
                b = dv[rows, :]
                a_high = a.astype(BF)
                b_high = b.astype(BF)
                terms = (
                    nn(a_high, fold_k)
                    + nn((a - a_high.astype(F32)).astype(BF), fold_k)
                    + nn(b_high, fold_v)
                    + nn((b - b_high.astype(F32)).astype(BF), fold_v)
                )
                slot_rows = pl.ds(pl.multiple_of(slot_ref[i] * tok, tok), tok)
                out_ref[slot_rows, width:] = terms.astype(BF)
                return unused

            lax.fori_loop(0, blocks, fold, 0)

    whole = lambda shape: pl.BlockSpec(shape, lambda j, *_: (0, 0))
    return pl.pallas_call(
        kernel,
        grid_spec=pltpu.PrefetchScalarGridSpec(
            num_scalar_prefetch=1,
            grid=(blocks,),
            in_specs=[
                pl.BlockSpec((1, tok), lambda j, *_: (0, j)),
                pl.BlockSpec((tok, width), lambda j, *_: (j, 0)),
                whole((seq, width)),
                whole((HD, seq)),
                whole((seq, width)),
                pl.BlockSpec((tok, width), lambda j, *_: (j, 0)),
                pl.BlockSpec((tok, width), lambda j, *_: (j, 0)),
                pl.BlockSpec((1, heads, tok), lambda j, *_: (j, 0, 0)),
                whole((seq, 128)),
                whole((seq, 128)),
                whole((width, width)),
            ],
            out_specs=whole((seq, width + 128)),
            scratch_shapes=[pltpu.VMEM((seq, width), F32), pltpu.VMEM((seq, width), F32)],
        ),
        out_shape=jax.ShapeDtypeStruct((seq, width + 128), BF),
        compiler_params=pltpu.CompilerParams(vmem_limit_bytes=VMEM_LIMIT),
        cost_estimate=MEDIUM,
        name="attend_backward",
    )(slot_of, starts, queries, keys, keys_t, values, grads, full, lse, cosine, sine, unsplit)


def outer_rows(activations, gradients):
    return lax.dot_general(
        activations, gradients, (((0,), (0,)), ((), ())), preferred_element_type=F32
    ).astype(BF)


def split_source(width):
    lane = np.arange(width)
    half = lane // (width // 2)
    head = (lane % (width // 2)) // HALF
    return head * HD + half * HALF + lane % HALF


def spread_matrix(width):
    matrix = np.zeros((width + 2 * HD, width + 256), np.float32)
    lane = np.arange(width)
    matrix[split_source(width), lane] = 1
    lane = np.arange(2 * HD)
    matrix[width + lane, width + lane] = 1
    lane = np.arange(HD)
    matrix[width + (lane + HALF) % HD, width + 128 + lane] = 1
    return jnp.asarray(matrix, BF)


def widen_matrix(width):
    matrix = np.zeros((2 * HD, 2 * width), np.float32)
    lane = np.arange(width)
    matrix[(lane // (width // 2)) * HALF + lane % HALF, lane] = 1
    matrix[HD + lane % HD, width + lane] = 1
    return jnp.asarray(matrix, BF)


def unsplit_matrix(width):
    matrix = np.zeros((width, width), np.float32)
    matrix[np.arange(width), split_source(width)] = 1
    return jnp.asarray(matrix, BF)


def on_device(
    block_in,
    gain_attn,
    qkv_weight,
    out_weight,
    gain_ffn,
    gate_up_weight,
    down_weight,
    doc_lengths,
    out_grad,
):
    n_ctx = lax.axis_size("ctx")
    n_dp = lax.axis_size("dp")
    me = lax.axis_index("ctx")
    tok = block_in.shape[0]
    seq = tok * n_ctx
    heads = H // n_ctx
    width = heads * HD
    sharers = n_ctx // KVH
    rows = qkv_weight.shape[0]
    ff_rows = down_weight.shape[0]
    ff = ff_rows * n_dp
    columns = width + 2 * HD

    order = me ^ jnp.where(me % 2 == 0, *[jnp.asarray(t) for t in slot_table(n_ctx)])
    slots = jnp.arange(n_ctx, dtype=jnp.int32)
    slot_of = jnp.sum(jnp.where(order[None, :] == slots[:, None], slots[None, :], 0), axis=1)
    index = jnp.arange(seq, dtype=jnp.int32)
    lengths = doc_lengths[0]
    ends = jnp.cumsum(lengths)
    starts = jnp.sum((index[:, None] >= ends[None, :]).astype(jnp.int32) * lengths[None, :], axis=1)
    lane = jnp.arange(128, dtype=F32) % HALF
    frequency = 10000.0 ** (-lane * 2.0 / HD)
    angles = (index - starts).astype(F32)[:, None] * frequency[None, :]
    cosine = jnp.cos(angles)
    sine = jnp.sin(angles)
    starts_row = starts[None, :]

    gain_one = gain_attn.astype(F32)[:, None]
    gain_two = gain_ffn.astype(F32)[:, None]
    qkv = (qkv_weight.astype(F32) * gain_one).astype(BF)
    q_cols = qkv[:, : H * HD].reshape(rows, n_ctx, width).transpose(1, 0, 2)
    k_cols = qkv[:, H * HD : (H + KVH) * HD].reshape(rows, KVH, HD).transpose(1, 0, 2)
    v_cols = qkv[:, (H + KVH) * HD :].reshape(rows, KVH, HD).transpose(1, 0, 2)
    kv_cols = jnp.repeat(jnp.concatenate([k_cols, v_cols], axis=2), sharers, axis=0)
    owner_pairs = [(b, b % n_dp * n_ctx + b // n_dp) for b in range(n_dp * n_ctx)]
    out_own = lax.ppermute(out_weight, ("dp", "ctx"), owner_pairs)
    out_part = gather_dp(out_own)
    qkv_own = exchange(after(jnp.concatenate([q_cols, kv_cols], axis=2), out_own)).reshape(
        n_ctx * rows, columns
    )
    qkv_part = gather_dp(qkv_own)

    hidden_in = block_in.astype(F32)
    rms_one = lax.rsqrt(jnp.mean(hidden_in * hidden_in, axis=-1, keepdims=True) + EPS)
    one_pieces = gather_slots(after((hidden_in * rms_one).astype(BF), qkv_own), n_ctx)

    gate_up_cols = split_columns(
        gate_up_weight, after(gain_two, cosine, sine), n_ctx, n_dp, ff_rows
    )
    gate_up_own = exchange(after(gate_up_cols, *one_pieces[: n_ctx // 2])).reshape(
        n_ctx * rows, 2 * ff
    )
    gate_up_part = gather_dp(gate_up_own)
    down_part = gather_dp(after(down_weight, gate_up_own))

    queries, keys, values, keys_t, values_t, all_one = project_qkv(
        order, one_pieces, qkv_part, spread_matrix(width), widen_matrix(width), cosine, sine, width, tok
    )
    out_pieces = gather_slots(out_part, n_ctx)
    attn, slot_attn, attended, lse = attend_forward(
        slot_of, starts_row, after(queries, gate_up_own), keys, values_t, heads, tok, 0, n_ctx, ()
    )
    attn_tokens = exchange(attn.reshape(n_ctx, tok, width))
    state, norm_two = project_out(order, attn_tokens, out_pieces, block_in)

    two_pieces = gather_slots(norm_two, n_ctx)
    grad_direct = gather_direct(after(out_grad, *two_pieces), n_ctx)
    hidden, factors, all_two = feed_forward(two_pieces, gate_up_part)
    grad_pieces = gather_rest(grad_direct, n_ctx, (hidden,))
    all_grad = lay_out(grad_pieces)
    down_terms = outer_rows(hidden, all_grad)
    down_sums = scatter_dp(down_terms)
    grad_gate_up = feed_backward(after(factors, down_terms), all_grad, down_part)

    def rows_of(x, lo, hi):
        return lax.slice_in_dim(x, lo * tok, hi * tok, axis=0)

    d_pairs, _ = scatter_pairs(
        lambda lo, hi: nt(rows_of(grad_gate_up, lo, hi), gate_up_part), tok, n_ctx
    )
    stages = tuple(reversed(range(len(walk(n_ctx, 0)))))
    d_two = scatter_chips(*d_pairs, stages, n_ctx)
    hidden_pairs, _ = scatter_pairs(
        lambda lo, hi: nn(rows_of(after(hidden, *d_pairs), lo, hi), down_part), tok, n_ctx
    )
    gate_up_terms = outer_rows(after(all_two, *d_pairs), grad_gate_up)
    gate_up_sums = scatter_dp(gate_up_terms)

    grad_state, grad_branch, grad_heads = branch_back(
        order, after(d_two, gate_up_terms, *hidden_pairs), state, out_grad, out_pieces
    )
    grad_attn = exchange(grad_heads).reshape(seq, width)
    branch_here, branch_there = gather_at_once(after(grad_branch, grad_attn), n_ctx)
    hidden_upper, hidden_lower = hidden_pairs
    hidden_arrived = swap_stage(after(hidden_upper.astype(BF), grad_attn), n_ctx, stages[0])
    grad_mixed = attend_backward(
        slot_of,
        starts_row,
        queries,
        keys,
        keys_t,
        values,
        grad_attn,
        attended,
        lse,
        cosine,
        sine,
        unsplit_matrix(width),
        heads,
        tok,
    )
    qkv_terms = outer_rows(all_one, grad_mixed)
    qkv_sums = scatter_dp(after(qkv_terms, gate_up_sums))
    one_pairs, _ = scatter_pairs(
        lambda lo, hi: nt(
            rows_of(after(grad_mixed, qkv_terms, hidden_arrived, *branch_here), lo, hi), qkv_part
        ),
        tok,
        n_ctx,
    )
    d_one = scatter_chips(*one_pairs, stages, n_ctx)
    hidden_sums = scatter_rest(hidden_lower, hidden_arrived, stages, n_ctx)
    block_out = (state + hidden_sums).astype(BF)
    out_terms = outer_rows(slot_attn, after(lay_out(branch_here + branch_there), qkv_terms))
    out_sums = scatter_dp(after(out_terms, qkv_sums))
    norm_one = hidden_in * rms_one
    input_grad = grad_state + rms_one * (
        d_one - norm_one * jnp.mean(d_one * norm_one, axis=-1, keepdims=True)
    )

    down_weight_grad = after(down_sums, grad_mixed).astype(F32)
    out_weight_grad = lax.ppermute(
        out_sums, ("dp", "ctx"), [(b, a) for a, b in owner_pairs]
    ).astype(F32)
    gate_up_weight_grad, gain_ffn_grad = join_columns(
        exchange(after(gate_up_sums, grad_mixed).reshape(n_ctx, rows, 2 * ff)), gate_up_weight, gain_two, n_dp, ff_rows
    )
    qkv_back = exchange(qkv_sums.reshape(n_ctx, rows, columns)).astype(F32)
    q_back = qkv_back[:, :, :width].transpose(1, 0, 2).reshape(rows, H * HD)
    kv_back = jnp.sum(qkv_back[:, :, width:].reshape(KVH, sharers, rows, 2 * HD), axis=1)
    k_back = kv_back[:, :, :HD].transpose(1, 0, 2).reshape(rows, KVH * HD)
    v_back = kv_back[:, :, HD:].transpose(1, 0, 2).reshape(rows, KVH * HD)
    qkv_back = jnp.concatenate([q_back, k_back, v_back], axis=1)
    qkv_weight_grad = qkv_back * gain_one
    gain_attn_grad = jnp.sum(qkv_back * qkv_weight.astype(F32), axis=1)
    return (
        block_out,
        input_grad,
        gain_attn_grad,
        qkv_weight_grad,
        out_weight_grad,
        gain_ffn_grad[:, 0],
        gate_up_weight_grad,
        down_weight_grad,
    )


def solution(mesh):
    rows = P(("dp", "ctx"), None)
    entries = P(("dp", "ctx"))
    return jax.shard_map(
        on_device,
        mesh=mesh,
        in_specs=(rows, entries, rows, rows, entries, rows, rows, P("dp", None), rows),
        out_specs=(rows, rows, entries, rows, rows, entries, rows, rows),
        check_vma=False,
    )
```

profile of v0, /device:TPU:1, one launch (start us, length us, event | category | flops | bytes accessed | tf_op | source)
XLA Modules:
  0.0 620.0 jit_solution(3166374443066136251)
XLA Ops:
  16.5 13.4 %all-to-all-start = ((bf16[8,64,384]{2,1,0:T(8,128)(2,1)}), bf16[8,64,384]{2,1,0:T(8,128)(2,1)S(1)}, u32[]{:S(2)}, u32[]{:S(2)}) async-start(bf16[8,64,384]{2,1,0:T(8,128)(2,1)} %pad_maximum_fusion), calls=%async_computation | async-start | bytes 786432 | tf_op jit(solution)/shard_map/all_to_all | solution.py:128
  39.8 17.5 %collective-permute-done.1.refs_1_ = bf16[256,2048]{1,0:T(8,128)(2,1)} collective-permute-done((bf16[256,2048]{1,0:T(8,128)(2,1)S(1)}, bf16[256,2048]{1,0:T(8,128)(2,1)}, u32[]{:S(2)}, u32[]{:S(2)}) %collective-permute-start.1) | collective-permute-done | bytes 1048608 | tf_op jit(solution)/shard_map/ppermute | solution.py:54
  73.6 8.6 %collective-permute-start.7 = (bf16[256,2048]{1,0:T(8,128)(2,1)}, bf16[256,2048]{1,0:T(8,128)(2,1)}, u32[]{:S(2)}, u32[]{:S(2)}) collective-permute-start(bf16[256,2048]{1,0:T(8,128)(2,1)} %collective-permute-done.3.refs_3_), channel_id=1, source_target_pairs={{0,1},{1,0},{2,3},{3,2},{4,5},{5,4},{6,7},{7,6},{8,9},{9,8},{10,11... | collective-permute-start | bytes 3145736 | tf_op jit(solution)/shard_map/ppermute | solution.py:58
  90.1 6.8 %collective-permute-done.8.refs_1_ = bf16[256,2048]{1,0:T(8,128)(2,1)} collective-permute-done((bf16[256,2048]{1,0:T(8,128)(2,1)}, bf16[256,2048]{1,0:T(8,128)(2,1)}, u32[]{:S(2)}, u32[]{:S(2)}) %collective-permute-start.8) | collective-permute-done | bytes 1048608 | tf_op jit(solution)/shard_map/ppermute | solution.py:54
  98.2 9.8 %collective-permute-start.13 = (bf16[256,2048]{1,0:T(8,128)(2,1)}, bf16[256,2048]{1,0:T(8,128)(2,1)}, u32[]{:S(2)}, u32[]{:S(2)}) collective-permute-start(bf16[256,2048]{1,0:T(8,128)(2,1)} %collective-permute-done.9.refs_2_), channel_id=1, source_target_pairs={{0,1},{1,0},{2,3},{3,2},{4,5},{5,4},{6,7},{7,6},{8,9},{9,8},{10,11... | collective-permute-start | bytes 3145736 | tf_op jit(solution)/shard_map/ppermute | solution.py:58
  107.9 16.3 %project_qkv.1 = (bf16[2048,256]{1,0:T(8,128)(2,1)}, bf16[2048,256]{1,0:T(8,128)(2,1)}, bf16[2048,256]{1,0:T(8,128)(2,1)}, bf16[64,2048]{1,0:T(8,128)(2,1)}, bf1...) custom-call(s32[8]{0:T(128)} %copy-done.29, bf16[256,2048]{1,0:T(8,128)(2,1)} %copy-done.24, ...), custom_call_target="tpu_custom_call" | custom-call | flops 99999997952 | bytes 1048576 | tf_op jit(solution)/shard_map/project_qkv/pallas_call | solution.py:263
  128.4 24.6 %attend_forward.1 = (bf16[2048,256]{1,0:T(8,128)(2,1)}, bf16[2048,256]{1,0:T(8,128)(2,1)}, f32[2048,256]{1,0:T(8,128)}, f32[8,4,256]{2,1,0:T(4,128)}) custom-call(s32[8]{0:T(128)} %select_reduce_fusion.1.slot_ref, s32[1,2048]{1,0:T(1,128)} %bitcast.64, bf16[2048,256]{1,0:T(8,128)(2,1)} %get-tuple-element.53.q_ref, ...), custom_call_target="tpu_custom_call" | custom-call | flops 99999997952 | bytes 1048576 | tf_op jit(solution)/shard_map/attend_forward/pallas_call | solution.py:678
  157.9 11.9 %all-to-all-done.2.a_ref = bf16[8,256,256]{2,1,0:T(8,128)(2,1)S(1)} async-done(((bf16[8,256,256]{2,1,0:T(8,128)(2,1)}), bf16[8,256,256]{2,1,0:T(8,128)(2,1)S(1)}, u32[]{:S(2)}, u32[]{:S(2)}) %all-to-all-start.2) | async-done | bytes 1048608 | tf_op jit(solution)/shard_map/all_to_all | solution.py:128
  170.8 11.1 %project_out.1 = (f32[256,2048]{1,0:T(8,128)}, bf16[256,2048]{1,0:T(8,128)(2,1)}) custom-call(s32[8]{0:T(128)} %copy-done.29, bf16[8,256,256]{2,1,0:T(8,128)(2,1)} %copy-done.10, bf16[256,2048]{1,0:T(8,128)(2,1)} %all-gather.7.cloned.1.call-done.refs_0_, bf16[256,2048]{1,0:T(8,128)(2,1)} %collective-permute-done.8.refs_1_, ...), custom_call_target="tpu_custom_call" | custom-call | flops 1048576 | bytes 1048576 | tf_op jit(solution)/shard_map/project_out/pallas_call | solution.py:333
  185.5 17.5 %collective-permute-done.15.refs_1_ = bf16[256,2048]{1,0:T(8,128)(2,1)S(1)} collective-permute-done((bf16[256,2048]{1,0:T(8,128)(2,1)}, bf16[256,2048]{1,0:T(8,128)(2,1)S(1)}, u32[]{:S(2)}, u32[]{:S(2)}) %collective-permute-start.15) | collective-permute-done | bytes 1048608 | tf_op jit(solution)/shard_map/ppermute | solution.py:54
  212.9 8.2 %collective-permute-done.17.refs_3_ = bf16[256,2048]{1,0:T(8,128)(2,1)} collective-permute-done((bf16[256,2048]{1,0:T(8,128)(2,1)S(1)}, bf16[256,2048]{1,0:T(8,128)(2,1)}, u32[]{:S(2)}, u32[]{:S(2)}) %collective-permute-start.17) | collective-permute-done | bytes 1048608 | tf_op jit(solution)/shard_map/ppermute | solution.py:54
  229.7 6.1 all-gather.9.cloned.1.call-done.refs_8_
  235.8 23.9 %feed_forward.1 = (bf16[2048,704]{1,0:T(8,128)(2,1)}, bf16[2048,1408]{1,0:T(8,128)(2,1)}, bf16[2048,2048]{1,0:T(8,128)(2,1)}) custom-call(bf16[256,2048]{1,0:T(8,128)(2,1)} %get-tuple-element.58.refs_0_, bf16[256,2048]{1,0:T(8,128)(2,1)} %copy-done.40, bf16[256,2048]{1,0:T(8,128)(2,1)} %copy-done.41, bf16[256,2048]{1,0:T(8,128)(2,1)} %collective-permute-done.17.refs_3_, ...), custom_call_target="tpu_custom_call" | custom-call | flops 99999997952 | bytes 1048576 | tf_op jit(solution)/shard_map/feed_forward/pallas_call | solution.py:382
  262.2 11.6 %collective-permute-done.24.refs_3_ = bf16[256,2048]{1,0:T(8,128)(2,1)S(1)} collective-permute-done((bf16[256,2048]{1,0:T(8,128)(2,1)S(1)}, bf16[256,2048]{1,0:T(8,128)(2,1)S(1)}, u32[]{:S(2)}, u32[]{:S(2)}) %collective-permute-start.24) | collective-permute-done | bytes 1048608 | tf_op jit(solution)/shard_map/ppermute | solution.py:54
  277.5 6.5 %lay_out.2.g_ref = bf16[2048,2048]{1,0:T(8,128)(2,1)} custom-call(bf16[256,2048]{1,0:T(8,128)(2,1)} %g_ref.1, bf16[256,2048]{1,0:T(8,128)(2,1)} %copy-done.17, bf16[256,2048]{1,0:T(8,128)(2,1)} %copy-done.18, bf16[256,2048]{1,0:T(8,128)(2,1)} %copy-done.19, bf16[256,2048]{1,0:T(8,128)(2,1)} %copy-done.21, bf16[256,2048]{1,0:T(8,128)(2,1)} %copy-done.22, ...), custom_call_target="tpu_custom_call" | custom-call | flops 1048576 | bytes 1048576 | tf_op jit(solution)/shard_map/lay_out/pallas_call | solution.py:471
  284.0 10.7 %convolution_convert_fusion.1 = bf16[704,2048]{1,0:T(8,128)(2,1)} fusion(bf16[2048,704]{1,0:T(8,128)(2,1)} %get-tuple-element.65, bf16[2048,2048]{1,0:T(8,128)(2,1)} %lay_out.2.g_ref), kind=kOutput, calls=%fused_computation.9 | convolution fusion | flops 5907021824 | bytes 14155776 | tf_op jit(solution)/shard_map/dot_general | solution.py:839
  294.7 15.2 %feed_backward.1 = bf16[2048,1408]{1,0:T(8,128)(2,1)} custom-call(bf16[2048,1408]{1,0:T(8,128)(2,1)} %get-tuple-element.63.factor_ref, bf16[2048,2048]{1,0:T(8,128)(2,1)} %lay_out.2.g_ref, bf16[704,2048]{1,0:T(8,128)(2,1)} %all-gather.11.cloned.1.call-done.w_hbm), custom_call_target="tpu_custom_call" | custom-call | flops 99999997952 | bytes 1048576 | tf_op jit(solution)/shard_map/feed_backward/pallas_call | solution.py:427
  309.9 7.8 %convolution_convert_fusion.7 = bf16[512,2048]{1,0:T(8,128)(2,1)} fusion(bf16[2048,1408]{1,0:T(8,128)(2,1)} %all-gather.9.cloned.1.call-done.refs_8_, bf16[2048,1408]{1,0:T(8,128)(2,1)} %feed_backward.1), kind=kOutput, calls=%fused_computation.15 | convolution fusion | flops 2953838592 | bytes 9306112 | tf_op jit(solution)/shard_map/dot_general | solution.py:27
  318.2 7.8 %convolution_convert_fusion.6 = bf16[512,2048]{1,0:T(8,128)(2,1)} fusion(bf16[2048,1408]{1,0:T(8,128)(2,1)} %all-gather.9.cloned.1.call-done.refs_8_, bf16[2048,1408]{1,0:T(8,128)(2,1)} %feed_backward.1), kind=kOutput, calls=%fused_computation.14 | convolution fusion | flops 2953838592 | bytes 9306112 | tf_op jit(solution)/shard_map/dot_general | solution.py:27
  326.2 8.0 %convert_add_fusion.6 = bf16[512,2048]{1,0:T(8,128)(2,1)} fusion(bf16[512,2048]{1,0:T(8,128)(2,1)S(1)} %collective-permute-done.29, bf16[2048,1408]{1,0:T(8,128)(2,1)} %all-gather.9.cloned.1.call-done.refs_8_, bf16[2048,1408]{1,0:T(8,128)(2,1)} %feed_backward.1), kind=kOutput, calls=%fused_computation.8 | convolution fusion | flops 2955935744 | bytes 11403264 | tf_op jit(solution)/shard_map/dot_general | solution.py:27
  335.4 9.7 %convert_add_fusion.5 = f32[512,2048]{1,0:T(8,128)} fusion(bf16[512,2048]{1,0:T(8,128)(2,1)} %collective-permute-done.30, bf16[2048,1408]{1,0:T(8,128)(2,1)} %all-gather.9.cloned.1.call-done.refs_8_, bf16[2048,1408]{1,0:T(8,128)(2,1)} %feed_backward.1), kind=kOutput, calls=%fused_computation.7 | convolution fusion | flops 2954887168 | bytes 13500416 | tf_op jit(solution)/shard_map/dot_general | solution.py:27
  352.0 15.8 %convolution_convert_fusion = bf16[2048,1408]{1,0:T(8,128)(2,1)} fusion(bf16[2048,2048]{1,0:T(8,128)(2,1)S(1)} %bitcast.72, bf16[2048,1408]{1,0:T(8,128)(2,1)S(1)} %bitcast.70), kind=kOutput, calls=%fused_computation | convolution fusion | flops 11814043648 | bytes 19922944 | tf_op jit(solution)/shard_map/dot_general | solution.py:839
  386.8 10.9 %branch_back.1 = (f32[256,2048]{1,0:T(8,128)}, bf16[256,2048]{1,0:T(8,128)(2,1)}, bf16[8,256,256]{2,1,0:T(8,128)(2,1)}) custom-call(s32[8]{0:T(128)} %copy-done.29, f32[256,2048]{1,0:T(8,128)} %slice_add_fusion.2.d_ref, f32[256,2048]{1,0:T(8,128)} %get-tuple-element.57.state_ref, bf16[256,2048]{1,0:T(8,128)(2,1)} %g_ref.1, ...), custom_call_target="tpu_custom_call" | custom-call | flops 1048576 | bytes 1048576 | tf_op jit(solution)/shard_map/branch_back/pallas_call | solution.py:522
  397.7 19.8 %all_to_all.30 = bf16[8,256,256]{2,1,0:T(8,128)(2,1)} all-to-all(bf16[8,256,256]{2,1,0:T(8,128)(2,1)} %get-tuple-element.69), channel_id=1, replica_groups=mesh['dp'=4,'ctx'=8] {'ctx'}, dimensions={0} | all-to-all | bytes 2097152 | tf_op jit(solution)/shard_map/all_to_all | solution.py:128
  421.1 56.0 %attend_backward.1 = bf16[2048,384]{1,0:T(8,128)(2,1)} custom-call(s32[8]{0:T(128)} %select_reduce_fusion.1.slot_ref, s32[1,2048]{1,0:T(1,128)} %bitcast.65, bf16[2048,256]{1,0:T(8,128)(2,1)} %get-tuple-element.53.q_ref, bf16[2048,256]{1,0:T(8,128)(2,1)} %get-tuple-element.54.k_ref, bf16[64,2048]{1,0:T(8,128)(2,1)} %get-tuple-element.72.kt_ref, ...), custom_call_target="tpu_custom_call" | custom-call | flops 20000000000 | bytes 1048576 | tf_op jit(solution)/shard_map/attend_backward/pallas_call | solution.py:810
  477.2 9.7 %convolution_convert_fusion.8 = bf16[2048,384]{1,0:T(8,128)(2,1)} fusion(bf16[2048,2048]{1,0:T(8,128)(2,1)} %get-tuple-element.76, bf16[2048,384]{1,0:T(8,128)(2,1)} %attend_backward.1), kind=kOutput, calls=%fused_computation.16 | convolution fusion | flops 3222011904 | bytes 11534336 | tf_op jit(solution)/shard_map/dot_general | solution.py:839
  513.2 6.5 %lay_out.3 = bf16[2048,2048]{1,0:T(8,128)(2,1)} custom-call(bf16[256,2048]{1,0:T(8,128)(2,1)} %get-tuple-element.78.refs_0_, bf16[256,2048]{1,0:T(8,128)(2,1)} %collective-permute-done.37.refs_1_, bf16[256,2048]{1,0:T(8,128)(2,1)} %collective-permute-done.38.refs_2_, bf16[256,2048]{1,0:T(8,128)(2,1)} %collective-permute-done.39.refs_3_, ...), custom_call_target="tpu_custom_call" | custom-call | flops 1048576 | bytes 1048576 | tf_op jit(solution)/shard_map/lay_out/pallas_call | solution.py:471
  519.8 11.8 %collective-permute-done.42 = bf16[512,2048]{1,0:T(8,128)(2,1)} collective-permute-done((bf16[512,2048]{1,0:T(8,128)(2,1)}, bf16[512,2048]{1,0:T(8,128)(2,1)}, u32[]{:S(2)}, u32[]{:S(2)}) %collective-permute-start.42) | collective-permute-done | bytes 2097184 | tf_op jit(solution)/shard_map/ppermute | solution.py:54
  559.9 10.0 %all-to-all-done.5.s_ref = bf16[8,64,1408]{2,1,0:T(8,128)(2,1)} async-done(((bf16[8,64,1408]{2,1,0:T(8,128)(2,1)}), bf16[8,64,1408]{2,1,0:T(8,128)(2,1)}, u32[]{:S(2)}, u32[]{:S(2)}) %all-to-all-start.5) | async-done | bytes 1441824 | tf_op jit(solution)/shard_map/all_to_all | solution.py:128
  569.9 7.7 %all-to-all-start.4 = ((bf16[8,64,384]{2,1,0:T(8,128)(2,1)}), bf16[8,64,384]{2,1,0:T(8,128)(2,1)S(1)}, u32[]{:S(2)}, u32[]{:S(2)}) async-start(bf16[8,64,384]{2,1,0:T(8,128)(2,1)} %bitcast.61), calls=%async_computation.6 | async-start | bytes 786432 | tf_op jit(solution)/shard_map/all_to_all | solution.py:128
  577.6 9.2 %join_columns.1 = (f32[64,11264]{1,0:T(8,128)}, f32[64,1]{1,0:T(8,128)}) custom-call(bf16[8,64,1408]{2,1,0:T(8,128)(2,1)} %all-to-all-done.5.s_ref, bf16[64,11264]{1,0:T(8,128)(2,1)} %w_ref.3, f32[64,1]{1,0:T(8,128)} %copy.50.gain_ref), custom_call_target="tpu_custom_call" | custom-call | flops 99999997952 | bytes 1048576 | tf_op jit(solution)/shard_map/join_columns/pallas_call | solution.py:599
  595.7 16.2 %collective-permute-done.48 = bf16[64,2048]{1,0:T(8,128)(2,1)S(1)} collective-permute-done((bf16[64,2048]{1,0:T(8,128)(2,1)}, bf16[64,2048]{1,0:T(8,128)(2,1)S(1)}, u32[]{:S(2)}, u32[]{:S(2)}) %collective-permute-start.48) | collective-permute-done | bytes 262176 | tf_op jit(solution)/shard_map/ppermute | solution.py:1018
  (279 shorter events, 178.0 us)
Async XLA Ops:
  29.8 41.6 %all-gather.7.cloned.1.call-start = ((), (), s32[]{:S(2)}) async-start(), calls=%async_computation.11 | async-start | bytes 1310720 | tf_op jit(solution)/shard_map/all_gather | solution.py:132
  36.2 71.7 %all-gather.5.cloned.1.call-start = ((), (), s32[]{:S(2)}) async-start(), calls=%async_computation.10 | async-start | bytes 1966080 | tf_op jit(solution)/shard_map/all_gather | solution.py:132
  36.5 34.8 %collective-permute-start.2 = (bf16[256,2048]{1,0:T(8,128)(2,1)S(1)}, bf16[256,2048]{1,0:T(8,128)(2,1)}, u32[]{:S(2)}, u32[]{:S(2)}) collective-permute-start(bf16[256,2048]{1,0:T(8,128)(2,1)S(1)} %fusion.2.refs_0_), channel_id=1, source_target_pairs={{0,4},{1,3},{2,6},{3,1},{4,0},{5,7},{6,2},{7,5},{8,12},{9,11},{10,... | collective-permute-start | bytes 3145736 | tf_op jit(solution)/shard_map/ppermute | solution.py:54
  38.6 32.9 %collective-permute-start.4 = (bf16[256,2048]{1,0:T(8,128)(2,1)S(1)}, bf16[256,2048]{1,0:T(8,128)(2,1)S(1)}, u32[]{:S(2)}, u32[]{:S(2)}) collective-permute-start(bf16[256,2048]{1,0:T(8,128)(2,1)S(1)} %fusion.2.refs_0_), channel_id=1, source_target_pairs={{0,1},{1,0},{2,3},{3,2},{4,5},{5,4},{6,7},{7,6},{8,9},{9,8},{10,11... | collective-permute-start | bytes 3145736 | tf_op jit(solution)/shard_map/ppermute | solution.py:58
  71.3 25.7 %collective-permute-start.6 = (bf16[256,2048]{1,0:T(8,128)(2,1)}, bf16[256,2048]{1,0:T(8,128)(2,1)}, u32[]{:S(2)}, u32[]{:S(2)}) collective-permute-start(bf16[256,2048]{1,0:T(8,128)(2,1)} %collective-permute-done.2.refs_2_), channel_id=1, source_target_pairs={{0,1},{1,0},{2,3},{3,2},{4,5},{5,4},{6,7},{7,6},{8,9},{9,8},{10,11... | collective-permute-start | bytes 3145736 | tf_op jit(solution)/shard_map/ppermute | solution.py:58
  71.4 25.6 %collective-permute-start.8 = (bf16[256,2048]{1,0:T(8,128)(2,1)}, bf16[256,2048]{1,0:T(8,128)(2,1)}, u32[]{:S(2)}, u32[]{:S(2)}) collective-permute-start(bf16[256,2048]{1,0:T(8,128)(2,1)} %all-gather.7.cloned.1.call-done.refs_0_), channel_id=1, source_target_pairs={{0,2},{1,5},{2,0},{3,7},{4,6},{5,1},{6,4},{7,3},{8,10},{9,13},{10,... | collective-permute-start | bytes 3145736 | tf_op jit(solution)/shard_map/ppermute | solution.py:54
  71.4 26.7 %collective-permute-start.9 = (bf16[256,2048]{1,0:T(8,128)(2,1)}, bf16[256,2048]{1,0:T(8,128)(2,1)}, u32[]{:S(2)}, u32[]{:S(2)}) collective-permute-start(bf16[256,2048]{1,0:T(8,128)(2,1)} %all-gather.7.cloned.1.call-done.refs_0_), channel_id=1, source_target_pairs={{0,4},{1,3},{2,6},{3,1},{4,0},{5,7},{6,2},{7,5},{8,12},{9,11},{10,... | collective-permute-start | bytes 3145736 | tf_op jit(solution)/shard_map/ppermute | solution.py:54
  73.6 34.3 %collective-permute-start.7 = (bf16[256,2048]{1,0:T(8,128)(2,1)}, bf16[256,2048]{1,0:T(8,128)(2,1)}, u32[]{:S(2)}, u32[]{:S(2)}) collective-permute-start(bf16[256,2048]{1,0:T(8,128)(2,1)} %collective-permute-done.3.refs_3_), channel_id=1, source_target_pairs={{0,1},{1,0},{2,3},{3,2},{4,5},{5,4},{6,7},{7,6},{8,9},{9,8},{10,11... | collective-permute-start | bytes 3145736 | tf_op jit(solution)/shard_map/ppermute | solution.py:58
  86.1 41.2 %all-to-all-start.1 = ((bf16[8,64,1408]{2,1,0:T(8,128)(2,1)}), bf16[8,64,1408]{2,1,0:T(8,128)(2,1)S(1)}, u32[]{:S(2)}, u32[]{:S(2)}) async-start(bf16[8,64,1408]{2,1,0:T(8,128)(2,1)} %split_columns.1), calls=%async_computation.1 | async-start | bytes 2883584 | tf_op jit(solution)/shard_map/all_to_all | solution.py:128
  90.0 145.8 %all-gather.9.cloned.1.call-start = ((), (), s32[]{:S(2)}) async-start(), calls=%async_computation.12 | async-start | bytes 7208960 | tf_op jit(solution)/shard_map/all_gather | solution.py:132
  90.0 67.9 %collective-permute-start.11 = (bf16[256,2048]{1,0:T(8,128)(2,1)}, bf16[256,2048]{1,0:T(8,128)(2,1)}, u32[]{:S(2)}, u32[]{:S(2)}) collective-permute-start(bf16[256,2048]{1,0:T(8,128)(2,1)} %all-gather.7.cloned.1.call-done.refs_0_), channel_id=1, source_target_pairs={{0,1},{1,0},{2,3},{3,2},{4,5},{5,4},{6,7},{7,6},{8,9},{9,8},{10,11... | collective-permute-start | bytes 3145736 | tf_op jit(solution)/shard_map/ppermute | solution.py:58
  97.0 27.3 %collective-permute-start.10 = (bf16[256,2048]{1,0:T(8,128)(2,1)}, bf16[256,2048]{1,0:T(8,128)(2,1)S(1)}, u32[]{:S(2)}, u32[]{:S(2)}) collective-permute-start(bf16[256,2048]{1,0:T(8,128)(2,1)} %collective-permute-done.8.refs_1_), channel_id=1, source_target_pairs={{0,4},{1,3},{2,6},{3,1},{4,0},{5,7},{6,2},{7,5},{8,12},{9,11},{10,... | collective-permute-start | bytes 3145736 | tf_op jit(solution)/shard_map/ppermute | solution.py:54
  97.0 60.9 %collective-permute-start.12 = (bf16[256,2048]{1,0:T(8,128)(2,1)}, bf16[256,2048]{1,0:T(8,128)(2,1)}, u32[]{:S(2)}, u32[]{:S(2)}) collective-permute-start(bf16[256,2048]{1,0:T(8,128)(2,1)} %collective-permute-done.8.refs_1_), channel_id=1, source_target_pairs={{0,1},{1,0},{2,3},{3,2},{4,5},{5,4},{6,7},{7,6},{8,9},{9,8},{10,11... | collective-permute-start | bytes 3145736 | tf_op jit(solution)/shard_map/ppermute | solution.py:58
  98.2 59.8 %collective-permute-start.13 = (bf16[256,2048]{1,0:T(8,128)(2,1)}, bf16[256,2048]{1,0:T(8,128)(2,1)}, u32[]{:S(2)}, u32[]{:S(2)}) collective-permute-start(bf16[256,2048]{1,0:T(8,128)(2,1)} %collective-permute-done.9.refs_2_), channel_id=1, source_target_pairs={{0,1},{1,0},{2,3},{3,2},{4,5},{5,4},{6,7},{7,6},{8,9},{9,8},{10,11... | collective-permute-start | bytes 3145736 | tf_op jit(solution)/shard_map/ppermute | solution.py:58
  124.2 45.6 %collective-permute-start.14 = (bf16[256,2048]{1,0:T(8,128)(2,1)S(1)}, bf16[256,2048]{1,0:T(8,128)(2,1)}, u32[]{:S(2)}, u32[]{:S(2)}) collective-permute-start(bf16[256,2048]{1,0:T(8,128)(2,1)S(1)} %collective-permute-done.10.refs_3_), channel_id=1, source_target_pairs={{0,1},{1,0},{2,3},{3,2},{4,5},{5,4},{6,7},{7,6},{8,9},{9,8},{10,11... | collective-permute-start | bytes 3145736 | tf_op jit(solution)/shard_map/ppermute | solution.py:58
  157.9 136.8 %all-gather.11.cloned.1.call-start = ((), (), s32[]{:S(2)}) async-start(), calls=%async_computation.13 | async-start | bytes 3604480 | tf_op jit(solution)/shard_map/all_gather | solution.py:132
  183.1 29.3 %collective-permute-start.16 = (bf16[256,2048]{1,0:T(8,128)(2,1)}, bf16[256,2048]{1,0:T(8,128)(2,1)S(1)}, u32[]{:S(2)}, u32[]{:S(2)}) collective-permute-start(bf16[256,2048]{1,0:T(8,128)(2,1)} %get-tuple-element.58.refs_0_), channel_id=1, source_target_pairs={{0,4},{1,3},{2,6},{3,1},{4,0},{5,7},{6,2},{7,5},{8,12},{9,11},{10,... | collective-permute-start | bytes 3145736 | tf_op jit(solution)/shard_map/ppermute | solution.py:54
  225.3 274.3 %reduce-scatter.11.cloned.1.call-start = ((), (), s32[]{:S(2)}) async-start(), calls=%async_computation.17 | async-start | bytes 3604480 | tf_op jit(solution)/shard_map/reduce_scatter | solution.py:136
  227.9 31.8 %collective-permute-start.22 = (bf16[256,2048]{1,0:T(8,128)(2,1)S(1)}, bf16[256,2048]{1,0:T(8,128)(2,1)S(1)}, u32[]{:S(2)}, u32[]{:S(2)}) collective-permute-start(bf16[256,2048]{1,0:T(8,128)(2,1)S(1)} %copy-done.9), channel_id=1, source_target_pairs={{0,2},{1,5},{2,0},{3,7},{4,6},{5,1},{6,4},{7,3},{8,10},{9,13},{10,... | collective-permute-start | bytes 3145736 | tf_op jit(solution)/shard_map/ppermute | solution.py:54
  229.7 32.0 %collective-permute-start.23 = (bf16[256,2048]{1,0:T(8,128)(2,1)S(1)}, bf16[256,2048]{1,0:T(8,128)(2,1)S(1)}, u32[]{:S(2)}, u32[]{:S(2)}) collective-permute-start(bf16[256,2048]{1,0:T(8,128)(2,1)S(1)} %copy-done.9), channel_id=1, source_target_pairs={{0,4},{1,3},{2,6},{3,1},{4,0},{5,7},{6,2},{7,5},{8,12},{9,11},{10,... | collective-permute-start | bytes 3145736 | tf_op jit(solution)/shard_map/ppermute | solution.py:54
  326.1 193.7 %reduce-scatter.5.cloned.1.call-start = ((), (), s32[]{:S(2)}) async-start(), calls=%async_computation.14 | async-start | bytes 7208960 | tf_op jit(solution)/shard_map/reduce_scatter | solution.py:136
  334.2 33.7 %collective-permute-start.33 = (bf16[512,2048]{1,0:T(8,128)(2,1)}, bf16[512,2048]{1,0:T(8,128)(2,1)S(1)}, u32[]{:S(2)}, u32[]{:S(2)}) collective-permute-start(bf16[512,2048]{1,0:T(8,128)(2,1)} %convert_add_fusion.6), channel_id=1, source_target_pairs={{0,4},{1,3},{2,6},{3,1},{4,0},{5,7},{6,2},{7,5},{8,12},{9,11},{10,... | collective-permute-start | bytes 6291464 | tf_op jit(solution)/shard_map/ppermute | solution.py:54
  351.9 25.9 %collective-permute-start.32 = (bf16[512,2048]{1,0:T(8,128)(2,1)}, bf16[512,2048]{1,0:T(8,128)(2,1)}, u32[]{:S(2)}, u32[]{:S(2)}) collective-permute-start(bf16[512,2048]{1,0:T(8,128)(2,1)} %convolution_convert_fusion.4), channel_id=1, source_target_pairs={{0,1},{1,0},{2,3},{3,2},{4,5},{5,4},{6,7},{7,6},{8,9},{9,8},{10,11... | collective-permute-start | bytes 6291464 | tf_op jit(solution)/shard_map/ppermute | solution.py:58
  367.8 192.0 %reduce-scatter.7.cloned.1.call-start = ((), (), s32[]{:S(2)}) async-start(), calls=%async_computation.15 | async-start | bytes 1966080 | tf_op jit(solution)/shard_map/reduce_scatter | solution.py:136
  417.4 69.4 %collective-permute-start.37 = (bf16[256,2048]{1,0:T(8,128)(2,1)}, bf16[256,2048]{1,0:T(8,128)(2,1)}, u32[]{:S(2)}, u32[]{:S(2)}) collective-permute-start(bf16[256,2048]{1,0:T(8,128)(2,1)} %get-tuple-element.78.refs_0_), channel_id=1, source_target_pairs={{0,2},{1,5},{2,0},{3,7},{4,6},{5,1},{6,4},{7,3},{8,10},{9,13},{10,... | collective-permute-start | bytes 3145736 | tf_op jit(solution)/shard_map/ppermute | solution.py:90
  417.7 69.1 %collective-permute-start.38 = (bf16[256,2048]{1,0:T(8,128)(2,1)}, bf16[256,2048]{1,0:T(8,128)(2,1)}, u32[]{:S(2)}, u32[]{:S(2)}) collective-permute-start(bf16[256,2048]{1,0:T(8,128)(2,1)} %get-tuple-element.78.refs_0_), channel_id=1, source_target_pairs={{0,4},{1,3},{2,6},{3,1},{4,0},{5,7},{6,2},{7,5},{8,12},{9,11},{10,... | collective-permute-start | bytes 3145736 | tf_op jit(solution)/shard_map/ppermute | solution.py:90
  418.6 68.2 %collective-permute-start.39 = (bf16[256,2048]{1,0:T(8,128)(2,1)}, bf16[256,2048]{1,0:T(8,128)(2,1)}, u32[]{:S(2)}, u32[]{:S(2)}) collective-permute-start(bf16[256,2048]{1,0:T(8,128)(2,1)} %get-tuple-element.78.refs_0_), channel_id=1, source_target_pairs={{0,6},{1,7},{2,4},{3,5},{4,2},{5,3},{6,0},{7,1},{8,14},{9,15},{10,... | collective-permute-start | bytes 3145736 | tf_op jit(solution)/shard_map/ppermute | solution.py:90
  420.1 67.8 %collective-permute-start.35 = (bf16[512,2048]{1,0:T(8,128)(2,1)}, bf16[512,2048]{1,0:T(8,128)(2,1)}, u32[]{:S(2)}, u32[]{:S(2)}) collective-permute-start(bf16[512,2048]{1,0:T(8,128)(2,1)} %convert_add_fusion.3), channel_id=1, source_target_pairs={{0,4},{1,3},{2,6},{3,1},{4,0},{5,7},{6,2},{7,5},{8,12},{9,11},{10,... | collective-permute-start | bytes 6291464 | tf_op jit(solution)/shard_map/ppermute | solution.py:54
  492.7 27.1 %collective-permute-start.40 = (bf16[512,2048]{1,0:T(8,128)(2,1)}, bf16[512,2048]{1,0:T(8,128)(2,1)}, u32[]{:S(2)}, u32[]{:S(2)}) collective-permute-start(bf16[512,2048]{1,0:T(8,128)(2,1)} %convolution_convert_fusion.3), channel_id=1, source_target_pairs={{0,1},{1,0},{2,3},{3,2},{4,5},{5,4},{6,7},{7,6},{8,9},{9,8},{10,11... | collective-permute-start | bytes 6291464 | tf_op jit(solution)/shard_map/ppermute | solution.py:58
  498.5 33.0 %collective-permute-start.42 = (bf16[512,2048]{1,0:T(8,128)(2,1)}, bf16[512,2048]{1,0:T(8,128)(2,1)}, u32[]{:S(2)}, u32[]{:S(2)}) collective-permute-start(bf16[512,2048]{1,0:T(8,128)(2,1)} %add_convert_fusion), channel_id=1, source_target_pairs={{0,4},{1,3},{2,6},{3,1},{4,0},{5,7},{6,2},{7,5},{8,12},{9,11},{10,... | collective-permute-start | bytes 6291464 | tf_op jit(solution)/shard_map/ppermute | solution.py:54
  512.9 37.9 %collective-permute-start.36 = (bf16[256,2048]{1,0:T(8,128)(2,1)}, bf16[256,2048]{1,0:T(8,128)(2,1)}, u32[]{:S(2)}, u32[]{:S(2)}) collective-permute-start(bf16[256,2048]{1,0:T(8,128)(2,1)} %slice.167), channel_id=1, source_target_pairs={{0,2},{1,5},{2,0},{3,7},{4,6},{5,1},{6,4},{7,3},{8,10},{9,13},{10,... | collective-permute-start | bytes 3145736 | tf_op jit(solution)/shard_map/ppermute | solution.py:54
  550.7 39.6 %reduce-scatter.9.cloned.1.call-start = ((), (), s32[]{:S(2)}) async-start(), calls=%async_computation.16 | async-start | bytes 1310720 | tf_op jit(solution)/shard_map/reduce_scatter | solution.py:136
  (79 other events, 1178.8 us)
Sparse Core Ops, SparseCore 0:
  36.3 28.5 all-gather.6
  67.1 39.3 all-gather.4
  128.5 107.2 all-gather.8
  237.2 57.1 all-gather.10
  326.2 54.4 reduce-scatter.10
  382.9 102.3 reduce-scatter.4
  519.9 32.1 reduce-scatter.6
  560.0 30.2 reduce-scatter.8
where the time goes:
time: 628 us; the launch traced here: 620 us
  Pallas kernels  183 us (29%)
  waiting for transfers between devices  135 us (21%)
  starting transfers between devices  116 us (18%)
  matrix products  99.6 us (16%)
  other arithmetic  38.4 us (6%)
  blocking collectives  19.8 us (3%)
  between operations  15.4 us (2%)
  local copies, waits for them, and re-layouts  12.4 us (2%)
    ppermute x18, waiting for transfers between devices, swap_stage(): return lax.ppermute(x, 'ctx', pairs)  78.4 us
    pallas_call x1, Pallas kernels, attend_backward(): pl.pallas_call(kernel, grid_spec=pltpu.PrefetchScalarGridSpec(num_scalar_...  56 us
    ppermute x26, starting transfers between devices, swap_core(): return lax.ppermute(x, 'ctx', [(c, c ^ 1) for c in range(n_ctx)])  43.7 us
    dot_general x8, matrix products, nt(): lax.dot_general(a, b, (((1,), (1,)), ((), ())), preferred_element_type=F32)  43.3 us
    dot_general x4, matrix products, outer_rows(): lax.dot_general(activations, gradients, (((0,), (0,)), ((), ())), preferr...  39.8 us
    all_to_all x5, starting transfers between devices, exchange(): return lax.all_to_all(x, 'ctx', split_axis=0, concat_axis=0, tiled=False)  35.7 us
    all_to_all x5, waiting for transfers between devices, exchange(): return lax.all_to_all(x, 'ctx', split_axis=0, concat_axis=0, tiled=False)  27.7 us
    ppermute x18, starting transfers between devices, swap_stage(): return lax.ppermute(x, 'ctx', pairs)  25 us
  transfers between devices with their start and end apart: 62, of which 19 were waited for; matrix products, arithmetic and copies ran while one was open for 22% of the time, Pallas kernels for 27%

commit v1 on v0

--- a/solution.py
+++ b/solution.py
@@ -304,59 +304,6 @@
     )(order, *pieces, weight, spread, widen, cosine, sine)
 
 
-def project_out(order, heads_in, pieces, residual):
-    n, tok, width = heads_in.shape
-
-    def kernel(order_ref, a_ref, *refs):
-        parts = refs[:n]
-        x_ref, state_hbm, norm_hbm, buffer, semaphores, state_ref, norm_ref, out_semaphores = refs[n:]
-        step = pl.program_id(0)
-        w = fetch_piece(parts, buffer, semaphores)
-
-        @pl.when(step == 0)
-        def _():
-            state_ref[...] = x_ref[...].astype(F32)
-
-        state_ref[...] += nn(a_ref[0], w)
-
-        @pl.when(step == n - 1)
-        def _():
-            state = state_ref[...]
-            scale = lax.rsqrt(jnp.mean(state * state, axis=-1, keepdims=True) + EPS)
-            copies = store_rows(state_ref, state_hbm, out_semaphores.at[0])
-            norm_ref[...] = (state * scale).astype(BF)
-            copies += store_rows(norm_ref, norm_hbm, out_semaphores.at[1])
-            for copy in copies:
-                copy.wait()
-
-    whole = lambda s, order: (0, 0)
-    return pl.pallas_call(
-        kernel,
-        grid_spec=pltpu.PrefetchScalarGridSpec(
-            num_scalar_prefetch=1,
-            grid=(n,),
-            in_specs=[pl.BlockSpec((1, tok, width), lambda s, order: (order[s], 0, 0))]
-            + any_specs(pieces)
-            + [pl.BlockSpec((tok, D), whole)],
-            out_specs=[pl.BlockSpec(memory_space=pltpu.HBM)] * 2,
-            scratch_shapes=[
-                pltpu.VMEM((n, width, D), BF),
-                pltpu.SemaphoreType.DMA((n,)),
-                pltpu.VMEM((tok, D), F32),
-                pltpu.VMEM((tok, D), BF),
-                pltpu.SemaphoreType.DMA((2, 4)),
-            ],
-        ),
-        out_shape=[
-            jax.ShapeDtypeStruct((tok, D), F32),
-            jax.ShapeDtypeStruct((tok, D), BF),
-        ],
-        compiler_params=pltpu.CompilerParams(vmem_limit_bytes=VMEM_LIMIT),
-        cost_estimate=SHORT,
-        name="project_out",
-    )(order, heads_in, *pieces, residual)
-
-
 def feed_forward(pieces, weight):
     n = len(pieces)
     tok = 2 * pieces[0].shape[0]
@@ -615,14 +562,13 @@
     return (lane % (width // 2)) // HALF
 
 
-def attend_forward(slot_of, starts, queries, keys, values_t, heads, tok, first, count, before):
+def attend_forward(slot_of, starts, queries, keys, values_t, heads, tok):
     seq, width = queries.shape
     blocks = seq // tok
     span = 2 * tok
 
-    def kernel(slot_ref, start_ref, q_ref, k_ref, v_ref, *refs):
-        attn_ref, slot_attn_ref, full_ref, lse_ref, scores = refs[len(before) :]
-        block = first + pl.program_id(0)
+    def kernel(slot_ref, start_ref, q_ref, k_ref, v_ref, slot_attn_ref, full_ref, lse_ref, scores):
+        block = pl.program_id(0)
         steps = (block + 2) // 2
         start = start_ref[...]
         here = block * tok + lax.broadcasted_iota(jnp.int32, (1, tok), 1)
@@ -672,40 +618,35 @@
             lse_ref[0, h : h + 1, :] = peaks[h] + jnp.log(total)
         full = jnp.concatenate(rows, axis=0).T
         full_ref[...] = full
-        attn_ref[...] = full.astype(BF)
         slot_attn_ref[...] = full.astype(BF)
 
     return pl.pallas_call(
         kernel,
         grid_spec=pltpu.PrefetchScalarGridSpec(
             num_scalar_prefetch=1,
-            grid=(count,),
+            grid=(blocks,),
             in_specs=[
-                pl.BlockSpec((1, tok), lambda j, slot: (0, first + j)),
-                pl.BlockSpec((tok, width), lambda j, slot: (first + j, 0)),
+                pl.BlockSpec((1, tok), lambda j, slot: (0, j)),
+                pl.BlockSpec((tok, width), lambda j, slot: (j, 0)),
                 pl.BlockSpec((seq, width), lambda j, slot: (0, 0)),
                 pl.BlockSpec((HD, seq), lambda j, slot: (0, 0)),
-            ]
-            + [pl.BlockSpec(memory_space=pltpu.HBM)] * len(before),
+            ],
             out_specs=[
-                pl.BlockSpec((tok, width), lambda j, slot: (first + j, 0)),
-                pl.BlockSpec((tok, width), lambda j, slot: (slot[first + j], 0)),
-                pl.BlockSpec((tok, width), lambda j, slot: (first + j, 0)),
-                pl.BlockSpec((1, heads, tok), lambda j, slot: (first + j, 0, 0)),
+                pl.BlockSpec((tok, width), lambda j, slot: (slot[j], 0)),
+                pl.BlockSpec((tok, width), lambda j, slot: (j, 0)),
+                pl.BlockSpec((1, heads, tok), lambda j, slot: (j, 0, 0)),
             ],
             scratch_shapes=[pltpu.VMEM((heads, seq, tok), F32)],
         ),
         out_shape=[
             jax.ShapeDtypeStruct((seq, width), BF),
-            jax.ShapeDtypeStruct((seq, width), BF),
             jax.ShapeDtypeStruct((seq, width), F32),
             jax.ShapeDtypeStruct((blocks, heads, tok), F32),
         ],
-        input_output_aliases={5 + i: i for i in range(len(before))},
         compiler_params=pltpu.CompilerParams(vmem_limit_bytes=VMEM_LIMIT),
-        cost_estimate=LONG,
+        cost_estimate=SHORT,
         name="attend_forward",
-    )(slot_of, starts, queries, keys, values_t, *before)
+    )(slot_of, starts, queries, keys, values_t)
 
 
 def attend_backward(
@@ -918,21 +859,20 @@
     k_cols = qkv[:, H * HD : (H + KVH) * HD].reshape(rows, KVH, HD).transpose(1, 0, 2)
     v_cols = qkv[:, (H + KVH) * HD :].reshape(rows, KVH, HD).transpose(1, 0, 2)
     kv_cols = jnp.repeat(jnp.concatenate([k_cols, v_cols], axis=2), sharers, axis=0)
-    owner_pairs = [(b, b % n_dp * n_ctx + b // n_dp) for b in range(n_dp * n_ctx)]
-    out_own = lax.ppermute(out_weight, ("dp", "ctx"), owner_pairs)
-    out_part = gather_dp(out_own)
-    qkv_own = exchange(after(jnp.concatenate([q_cols, kv_cols], axis=2), out_own)).reshape(
-        n_ctx * rows, columns
-    )
+    qkv_own = exchange(jnp.concatenate([q_cols, kv_cols], axis=2)).reshape(n_ctx * rows, columns)
     qkv_part = gather_dp(qkv_own)
 
     hidden_in = block_in.astype(F32)
     rms_one = lax.rsqrt(jnp.mean(hidden_in * hidden_in, axis=-1, keepdims=True) + EPS)
-    one_pieces = gather_slots(after((hidden_in * rms_one).astype(BF), qkv_own), n_ctx)
-
+    one_direct = gather_direct(after((hidden_in * rms_one).astype(BF), qkv_own), n_ctx)
     gate_up_cols = split_columns(
         gate_up_weight, after(gain_two, cosine, sine), n_ctx, n_dp, ff_rows
     )
+    one_pieces = gather_rest(one_direct, n_ctx, (), (qkv_part, gate_up_cols))
+    owner_pairs = [(b, b % n_dp * n_ctx + b // n_dp) for b in range(n_dp * n_ctx)]
+    out_own = lax.ppermute(after(out_weight, qkv_part), ("dp", "ctx"), owner_pairs)
+    out_part = gather_dp(out_own)
+
     gate_up_own = exchange(after(gate_up_cols, *one_pieces[: n_ctx // 2])).reshape(
         n_ctx * rows, 2 * ff
     )
@@ -942,29 +882,38 @@
     queries, keys, values, keys_t, values_t, all_one = project_qkv(
         order, one_pieces, qkv_part, spread_matrix(width), widen_matrix(width), cosine, sine, width, tok
     )
-    out_pieces = gather_slots(out_part, n_ctx)
-    attn, slot_attn, attended, lse = attend_forward(
-        slot_of, starts_row, after(queries, gate_up_own), keys, values_t, heads, tok, 0, n_ctx, ()
-    )
-    attn_tokens = exchange(attn.reshape(n_ctx, tok, width))
-    state, norm_two = project_out(order, attn_tokens, out_pieces, block_in)
+    slot_attn, attended, lse = attend_forward(
+        slot_of, starts_row, after(queries, gate_up_own), keys, values_t, heads, tok
+    )
+    stages = tuple(reversed(range(len(walk(n_ctx, 0)))))
+
+    def rows_of(x, lo, hi):
+        return lax.slice_in_dim(x, lo * tok, hi * tok, axis=0)
+
+    attn_pairs, _ = scatter_pairs(
+        lambda lo, hi: nn(rows_of(slot_attn, lo, hi), out_part), tok, n_ctx
+    )
+    state = hidden_in + scatter_chips(*attn_pairs, stages, n_ctx)
+    rms_two = lax.rsqrt(jnp.mean(state * state, axis=-1, keepdims=True) + EPS)
+    norm_two = (state * rms_two).astype(BF)
 
     two_pieces = gather_slots(norm_two, n_ctx)
     grad_direct = gather_direct(after(out_grad, *two_pieces), n_ctx)
     hidden, factors, all_two = feed_forward(two_pieces, gate_up_part)
     grad_pieces = gather_rest(grad_direct, n_ctx, (hidden,))
     all_grad = lay_out(grad_pieces)
+    out_direct = gather_direct(after(out_part, *grad_pieces[: n_ctx // 2]), n_ctx)
+    out_pieces = gather_rest(out_direct, n_ctx)
     down_terms = outer_rows(hidden, all_grad)
     down_sums = scatter_dp(down_terms)
-    grad_gate_up = feed_backward(after(factors, down_terms), all_grad, down_part)
-
-    def rows_of(x, lo, hi):
-        return lax.slice_in_dim(x, lo * tok, hi * tok, axis=0)
-
+    grad_gate_up = feed_backward(
+        after(factors, down_terms, *out_direct), all_grad, down_part
+    )
+
+    grad_gate_up = after(grad_gate_up, *out_pieces[: n_ctx // 2])
     d_pairs, _ = scatter_pairs(
         lambda lo, hi: nt(rows_of(grad_gate_up, lo, hi), gate_up_part), tok, n_ctx
     )
-    stages = tuple(reversed(range(len(walk(n_ctx, 0)))))
     d_two = scatter_chips(*d_pairs, stages, n_ctx)
     hidden_pairs, _ = scatter_pairs(
         lambda lo, hi: nn(rows_of(after(hidden, *d_pairs), lo, hi), down_part), tok, n_ctx

time: 628 us -> 638 us (1.016)
  waiting for transfers between devices: 135 us -> 177 us
  starting transfers between devices: 116 us -> 85.1 us
  Pallas kernels: 183 us -> 172 us
  matrix products: 99.6 us -> 107 us
    ppermute x18 -> x20, waiting for transfers between devices: 78.4 us -> 122 us  [swap_stage(): return lax.ppermute(x, 'ctx', pairs)]
    ppermute x26 -> x28, starting transfers between devices: 43.7 us -> 20.3 us  [swap_core(): return lax.ppermute(x, 'ctx', [(c, c ^ 1) for c in range(n_ctx)])]
    all_to_all x5 -> x4, waiting for transfers between devices: 27.7 us -> 15.4 us  [exchange(): return lax.all_to_all(x, 'ctx', split_axis=0, concat_axis=0, tiled=False)]
    pallas_call x1 -> x0, Pallas kernels: 11.1 us -> none  [project_out(): pl.pallas_call(kernel, grid_spec=pltpu.PrefetchScalarGridSpec(num_scalar_...]
    all_to_all x5 -> x4, starting transfers between devices: 35.7 us -> 25.5 us  [exchange(): return lax.all_to_all(x, 'ctx', split_axis=0, concat_axis=0, tiled=False)]
    all_gather x4, waiting for transfers between devices: 6.11 us -> 15.6 us  [gather_dp(): return lax.all_gather(x, 'dp', axis=0, tiled=True)]
    dot_general x4 -> x8, matrix products: 16.5 us -> 23.9 us  [nn(): return jnp.dot(a, b, preferred_element_type=F32)]
    ppermute x18 -> x20, starting transfers between devices: 25 us -> 29.8 us  [swap_stage(): return lax.ppermute(x, 'ctx', pairs)]
  transfers between devices with their start and end apart: 62 -> 65, of which waited for: 19 -> 23; matrix products, arithmetic and copies ran while one was open for 22% -> 22% of each run, Pallas kernels for 27% -> 27%
where the time goes in v1:
time: 638 us; the launch traced here: 631 us
  waiting for transfers between devices  177 us (28%)
  Pallas kernels  172 us (27%)
  matrix products  107 us (17%)
  starting transfers between devices  85.1 us (13%)
  other arithmetic  39.2 us (6%)
  blocking collectives  19.6 us (3%)
  between operations  15.5 us (2%)
  local copies, waits for them, and re-layouts  15.3 us (2%)
    ppermute x20, waiting for transfers between devices, swap_stage(): return lax.ppermute(x, 'ctx', pairs)  122 us
    pallas_call x1, Pallas kernels, attend_backward(): pl.pallas_call(kernel, grid_spec=pltpu.PrefetchScalarGridSpec(num_scalar_...  56.2 us
    dot_general x8, matrix products, nt(): lax.dot_general(a, b, (((1,), (1,)), ((), ())), preferred_element_type=F32)  43.6 us
    dot_general x4, matrix products, outer_rows(): lax.dot_general(activations, gradients, (((0,), (0,)), ((), ())), preferr...  39.9 us
    ppermute x20, starting transfers between devices, swap_stage(): return lax.ppermute(x, 'ctx', pairs)  29.8 us
    all_to_all x4, starting transfers between devices, exchange(): return lax.all_to_all(x, 'ctx', split_axis=0, concat_axis=0, tiled=False)  25.5 us
    pallas_call x1, Pallas kernels, attend_forward(): pl.pallas_call(kernel, grid_spec=pltpu.PrefetchScalarGridSpec(num_scalar_...  24.5 us
    pallas_call x1, Pallas kernels, feed_forward(): pl.pallas_call(kernel, grid=(n // 2,), in_specs=any_specs(pieces) + [pl.B...  23.9 us
  transfers between devices with their start and end apart: 65, of which 23 were waited for; matrix products, arithmetic and copies ran while one was open for 22% of the time, Pallas kernels for 27%

profile of v1, /device:TPU:1, one launch (start us, length us, event | category | flops | bytes accessed | tf_op | source)
XLA Modules:
  0.0 631.2 jit_solution(15104893538289966397)
XLA Ops:
  30.4 6.7 %collective-permute-done.refs_1_ = bf16[256,2048]{1,0:T(8,128)(2,1)} collective-permute-done((bf16[256,2048]{1,0:T(8,128)(2,1)S(1)}, bf16[256,2048]{1,0:T(8,128)(2,1)}, u32[]{:S(2)}, u32[]{:S(2)}) %collective-permute-start) | collective-permute-done | bytes 1048608 | tf_op jit(solution)/shard_map/ppermute | solution.py:54
  43.4 17.6 %collective-permute-done.2.refs_3_ = bf16[256,2048]{1,0:T(8,128)(2,1)} collective-permute-done((bf16[256,2048]{1,0:T(8,128)(2,1)}, bf16[256,2048]{1,0:T(8,128)(2,1)}, u32[]{:S(2)}, u32[]{:S(2)}) %collective-permute-start.2) | collective-permute-done | bytes 1048608 | tf_op jit(solution)/shard_map/ppermute | solution.py:54
  61.0 6.7 %all-gather.5.cloned.1.call-done.refs_8_ = bf16[2048,384]{1,0:T(8,128)(2,1)} async-done(((bf16[512,384]{1,0:T(8,128)(2,1)}), bf16[2048,384]{1,0:T(8,128)(2,1)}) %all-gather.5.cloned.1.call-update) | async-done | bytes 1572880 | tf_op jit(solution)/shard_map/all_gather | solution.py:132
  77.5 16.2 %project_qkv.1 = (bf16[2048,256]{1,0:T(8,128)(2,1)}, bf16[2048,256]{1,0:T(8,128)(2,1)}, bf16[2048,256]{1,0:T(8,128)(2,1)}, bf16[64,2048]{1,0:T(8,128)(2,1)}, bf1...) custom-call(s32[8]{0:T(128)} %copy-done.41, bf16[256,2048]{1,0:T(8,128)(2,1)} %copy-done.27, ...), custom_call_target="tpu_custom_call" | custom-call | flops 99999997952 | bytes 1048576 | tf_op jit(solution)/shard_map/project_qkv/pallas_call | solution.py:263
  95.7 24.5 %attend_forward.1 = (bf16[2048,256]{1,0:T(8,128)(2,1)}, f32[2048,256]{1,0:T(8,128)}, f32[8,4,256]{2,1,0:T(4,128)}) custom-call(s32[8]{0:T(128)} %select_reduce_fusion.1.slot_ref, s32[1,2048]{1,0:T(1,128)} %bitcast.66, bf16[2048,256]{1,0:T(8,128)(2,1)} %get-tuple-element.59.q_ref, bf16[2048,256]{1,0:T(8,128)(2,1)} %get-tuple-element.60.k_ref, ...), custom_call_target="tpu_custom_call" | custom-call | flops 1048576 | bytes 1048576 | tf_op jit(solution)/shard_map/attend_forward/pallas_call | solution.py:623
  133.7 23.1 %collective-permute-done.10 = bf16[512,2048]{1,0:T(8,128)(2,1)S(1)} collective-permute-done((bf16[512,2048]{1,0:T(8,128)(2,1)S(1)}, bf16[512,2048]{1,0:T(8,128)(2,1)S(1)}, u32[]{:S(2)}, u32[]{:S(2)}) %collective-permute-start.10) | collective-permute-done | bytes 2097184 | tf_op jit(solution)/shard_map/ppermute | solution.py:54
  158.1 10.1 %collective-permute-start.11 = (bf16[256,2048]{1,0:T(8,128)(2,1)S(1)}, bf16[256,2048]{1,0:T(8,128)(2,1)S(1)}, u32[]{:S(2)}, u32[]{:S(2)}) collective-permute-start(bf16[256,2048]{1,0:T(8,128)(2,1)S(1)} %slice.204), channel_id=1, source_target_pairs={{0,2},{1,5},{2,0},{3,7},{4,6},{5,1},{6,4},{7,3},{8,10},{9,13},{10,... | collective-permute-start | bytes 3145736 | tf_op jit(solution)/shard_map/ppermute | solution.py:54
  168.2 12.6 %collective-permute-done.11 = bf16[256,2048]{1,0:T(8,128)(2,1)S(1)} collective-permute-done((bf16[256,2048]{1,0:T(8,128)(2,1)S(1)}, bf16[256,2048]{1,0:T(8,128)(2,1)S(1)}, u32[]{:S(2)}, u32[]{:S(2)}) %collective-permute-start.11) | collective-permute-done | bytes 1048608 | tf_op jit(solution)/shard_map/ppermute | solution.py:54
  184.4 21.6 %collective-permute-done.12.refs_1_ = bf16[256,2048]{1,0:T(8,128)(2,1)} collective-permute-done((bf16[256,2048]{1,0:T(8,128)(2,1)S(1)}, bf16[256,2048]{1,0:T(8,128)(2,1)}, u32[]{:S(2)}, u32[]{:S(2)}) %collective-permute-start.12) | collective-permute-done | bytes 1048608 | tf_op jit(solution)/shard_map/ppermute | solution.py:54
  211.2 9.8 %collective-permute-done.14.refs_3_ = bf16[256,2048]{1,0:T(8,128)(2,1)} collective-permute-done((bf16[256,2048]{1,0:T(8,128)(2,1)}, bf16[256,2048]{1,0:T(8,128)(2,1)}, u32[]{:S(2)}, u32[]{:S(2)}) %collective-permute-start.14) | collective-permute-done | bytes 1048608 | tf_op jit(solution)/shard_map/ppermute | solution.py:54
  228.4 8.9 %all-gather.9.cloned.1.call-done.refs_8_ = bf16[2048,1408]{1,0:T(8,128)(2,1)} async-done(((bf16[512,1408]{1,0:T(8,128)(2,1)}), bf16[2048,1408]{1,0:T(8,128)(2,1)}) %all-gather.9.cloned.1.call-update) | async-done | bytes 5767184 | tf_op jit(solution)/shard_map/all_gather | solution.py:132
  237.4 23.9 %feed_forward.1 = (bf16[2048,704]{1,0:T(8,128)(2,1)}, bf16[2048,1408]{1,0:T(8,128)(2,1)}, bf16[2048,2048]{1,0:T(8,128)(2,1)}) custom-call(bf16[256,2048]{1,0:T(8,128)(2,1)} %copy-done.26, bf16[256,2048]{1,0:T(8,128)(2,1)} %collective-permute-done.12.refs_1_, bf16[256,2048]{1,0:T(8,128)(2,1)} %collective-permute-done.13.refs_2_, ...), custom_call_target="tpu_custom_call" | custom-call | flops 99999997952 | bytes 1048576 | tf_op jit(solution)/shard_map/feed_forward/pallas_call | solution.py:329
  263.8 11.6 %collective-permute-done.21.refs_3_ = bf16[256,2048]{1,0:T(8,128)(2,1)S(1)} collective-permute-done((bf16[256,2048]{1,0:T(8,128)(2,1)S(1)}, bf16[256,2048]{1,0:T(8,128)(2,1)S(1)}, u32[]{:S(2)}, u32[]{:S(2)}) %collective-permute-start.21) | collective-permute-done | bytes 1048608 | tf_op jit(solution)/shard_map/ppermute | solution.py:54
  281.0 6.5 %lay_out.2.g_ref = bf16[2048,2048]{1,0:T(8,128)(2,1)} custom-call(bf16[256,2048]{1,0:T(8,128)(2,1)} %g_ref.1, bf16[256,2048]{1,0:T(8,128)(2,1)} %copy-done.20, bf16[256,2048]{1,0:T(8,128)(2,1)} %collective-permute-done.20.refs_2_, bf16[256,2048]{1,0:T(8,128)(2,1)} %copy-done.21, bf16[256,2048]{1,0:T(8,128)(2,1)} %copy-done.22, bf16[256,2048]{1,0:T(8,128)(2,1)} %copy-done.23, ...), custom_call_target="tpu_custom_call" | custom-call | flops 1048576 | bytes 1048576 | tf_op jit(solution)/shard_map/lay_out/pallas_call | solution.py:418
  287.5 10.7 %convolution_convert_fusion.1 = bf16[704,2048]{1,0:T(8,128)(2,1)} fusion(bf16[2048,704]{1,0:T(8,128)(2,1)} %get-tuple-element.72, bf16[2048,2048]{1,0:T(8,128)(2,1)} %lay_out.2.g_ref), kind=kOutput, calls=%fused_computation.11 | convolution fusion | flops 5907021824 | bytes 14155776 | tf_op jit(solution)/shard_map/dot_general | solution.py:780
  303.1 15.2 %feed_backward.1 = bf16[2048,1408]{1,0:T(8,128)(2,1)} custom-call(bf16[2048,1408]{1,0:T(8,128)(2,1)} %get-tuple-element.69.factor_ref, bf16[2048,2048]{1,0:T(8,128)(2,1)} %lay_out.2.g_ref, bf16[704,2048]{1,0:T(8,128)(2,1)} %all-gather.11.cloned.1.call-done.w_hbm), custom_call_target="tpu_custom_call" | custom-call | flops 99999997952 | bytes 1048576 | tf_op jit(solution)/shard_map/feed_backward/pallas_call | solution.py:374
  318.4 8.2 %convolution_convert_fusion.9 = bf16[512,2048]{1,0:T(8,128)(2,1)} fusion(bf16[2048,1408]{1,0:T(8,128)(2,1)} %all-gather.9.cloned.1.call-done.refs_8_, bf16[2048,1408]{1,0:T(8,128)(2,1)} %feed_backward.1), kind=kOutput, calls=%fused_computation.22 | convolution fusion | flops 2953838592 | bytes 9306112 | tf_op jit(solution)/shard_map/dot_general | solution.py:27
  327.5 7.8 %convolution_convert_fusion.8 = bf16[512,2048]{1,0:T(8,128)(2,1)} fusion(bf16[2048,1408]{1,0:T(8,128)(2,1)} %all-gather.9.cloned.1.call-done.refs_8_, bf16[2048,1408]{1,0:T(8,128)(2,1)} %feed_backward.1), kind=kOutput, calls=%fused_computation.21 | convolution fusion | flops 2953838592 | bytes 9306112 | tf_op jit(solution)/shard_map/dot_general | solution.py:27
  335.4 8.0 %convert_add_fusion.6 = bf16[512,2048]{1,0:T(8,128)(2,1)} fusion(bf16[512,2048]{1,0:T(8,128)(2,1)S(1)} %collective-permute-done.29, bf16[2048,1408]{1,0:T(8,128)(2,1)} %all-gather.9.cloned.1.call-done.refs_8_, bf16[2048,1408]{1,0:T(8,128)(2,1)} %feed_backward.1), kind=kOutput, calls=%fused_computation.8 | convolution fusion | flops 2955935744 | bytes 11403264 | tf_op jit(solution)/shard_map/dot_general | solution.py:27
  344.6 9.7 %convert_add_fusion.5 = f32[512,2048]{1,0:T(8,128)} fusion(bf16[512,2048]{1,0:T(8,128)(2,1)} %collective-permute-done.30, bf16[2048,1408]{1,0:T(8,128)(2,1)} %all-gather.9.cloned.1.call-done.refs_8_, bf16[2048,1408]{1,0:T(8,128)(2,1)} %feed_backward.1), kind=kOutput, calls=%fused_computation.7 | convolution fusion | flops 2954887168 | bytes 13500416 | tf_op jit(solution)/shard_map/dot_general | solution.py:27
  361.3 15.8 %convolution_convert_fusion = bf16[2048,1408]{1,0:T(8,128)(2,1)} fusion(bf16[2048,2048]{1,0:T(8,128)(2,1)S(1)} %bitcast.74, bf16[2048,1408]{1,0:T(8,128)(2,1)S(1)} %bitcast.72), kind=kOutput, calls=%fused_computation | convolution fusion | flops 11814043648 | bytes 19922944 | tf_op jit(solution)/shard_map/dot_general | solution.py:780
  401.8 10.1 %branch_back.1 = (f32[256,2048]{1,0:T(8,128)}, bf16[256,2048]{1,0:T(8,128)(2,1)}, bf16[8,256,256]{2,1,0:T(8,128)(2,1)}) custom-call(s32[8]{0:T(128)} %copy-done.41, f32[256,2048]{1,0:T(8,128)} %slice_add_fusion.2.d_ref, f32[256,2048]{1,0:T(8,128)} %copy-done.1, bf16[256,2048]{1,0:T(8,128)(2,1)} %g_ref.1, ...), custom_call_target="tpu_custom_call" | custom-call | flops 1048576 | bytes 1048576 | tf_op jit(solution)/shard_map/branch_back/pallas_call | solution.py:469
  411.9 19.6 %all_to_all.25 = bf16[8,256,256]{2,1,0:T(8,128)(2,1)} all-to-all(bf16[8,256,256]{2,1,0:T(8,128)(2,1)} %get-tuple-element.76), channel_id=1, replica_groups=mesh['dp'=4,'ctx'=8] {'ctx'}, dimensions={0} | all-to-all | bytes 2097152 | tf_op jit(solution)/shard_map/all_to_all | solution.py:128
  435.1 56.2 %attend_backward.1 = bf16[2048,384]{1,0:T(8,128)(2,1)} custom-call(s32[8]{0:T(128)} %select_reduce_fusion.1.slot_ref, s32[1,2048]{1,0:T(1,128)} %bitcast.67, bf16[2048,256]{1,0:T(8,128)(2,1)} %get-tuple-element.59.q_ref, bf16[2048,256]{1,0:T(8,128)(2,1)} %get-tuple-element.60.k_ref, bf16[64,2048]{1,0:T(8,128)(2,1)} %get-tuple-element.79.kt_ref, ...), custom_call_target="tpu_custom_call" | custom-call | flops 20000000000 | bytes 1048576 | tf_op jit(solution)/shard_map/attend_backward/pallas_call | solution.py:751
  491.3 9.8 %convolution_convert_fusion.10 = bf16[2048,384]{1,0:T(8,128)(2,1)} fusion(bf16[2048,2048]{1,0:T(8,128)(2,1)} %get-tuple-element.83, bf16[2048,384]{1,0:T(8,128)(2,1)} %attend_backward.1), kind=kOutput, calls=%fused_computation.26 | convolution fusion | flops 3222011904 | bytes 11534336 | tf_op jit(solution)/shard_map/dot_general | solution.py:780
  527.4 6.5 %lay_out.3 = bf16[2048,2048]{1,0:T(8,128)(2,1)} custom-call(bf16[256,2048]{1,0:T(8,128)(2,1)} %get-tuple-element.85.refs_0_, bf16[256,2048]{1,0:T(8,128)(2,1)} %collective-permute-done.41.refs_1_, bf16[256,2048]{1,0:T(8,128)(2,1)} %collective-permute-done.42.refs_2_, bf16[256,2048]{1,0:T(8,128)(2,1)} %collective-permute-done.43.refs_3_, ...), custom_call_target="tpu_custom_call" | custom-call | flops 1048576 | bytes 1048576 | tf_op jit(solution)/shard_map/lay_out/pallas_call | solution.py:418
  534.0 11.7 %collective-permute-done.46 = bf16[512,2048]{1,0:T(8,128)(2,1)} collective-permute-done((bf16[512,2048]{1,0:T(8,128)(2,1)}, bf16[512,2048]{1,0:T(8,128)(2,1)}, u32[]{:S(2)}, u32[]{:S(2)}) %collective-permute-start.46) | collective-permute-done | bytes 2097184 | tf_op jit(solution)/shard_map/ppermute | solution.py:54
  557.2 6.8 %all-to-all-start.4 = ((bf16[8,64,1408]{2,1,0:T(8,128)(2,1)}), bf16[8,64,1408]{2,1,0:T(8,128)(2,1)}, u32[]{:S(2)}, u32[]{:S(2)}) async-start(bf16[8,64,1408]{2,1,0:T(8,128)(2,1)} %bitcast.17), calls=%async_computation.7 | async-start | bytes 2883584 | tf_op jit(solution)/shard_map/all_to_all | solution.py:128
  572.6 8.2 %all-to-all-done.4.s_ref = bf16[8,64,1408]{2,1,0:T(8,128)(2,1)} async-done(((bf16[8,64,1408]{2,1,0:T(8,128)(2,1)}), bf16[8,64,1408]{2,1,0:T(8,128)(2,1)}, u32[]{:S(2)}, u32[]{:S(2)}) %all-to-all-start.4) | async-done | bytes 1441824 | tf_op jit(solution)/shard_map/all_to_all | solution.py:128
  580.9 8.9 %all-to-all-start.3 = ((bf16[8,64,384]{2,1,0:T(8,128)(2,1)}), bf16[8,64,384]{2,1,0:T(8,128)(2,1)S(1)}, u32[]{:S(2)}, u32[]{:S(2)}) async-start(bf16[8,64,384]{2,1,0:T(8,128)(2,1)} %bitcast.63), calls=%async_computation.5 | async-start | bytes 786432 | tf_op jit(solution)/shard_map/all_to_all | solution.py:128
  589.8 9.2 %join_columns.1 = (f32[64,11264]{1,0:T(8,128)}, f32[64,1]{1,0:T(8,128)}) custom-call(bf16[8,64,1408]{2,1,0:T(8,128)(2,1)} %all-to-all-done.4.s_ref, bf16[64,11264]{1,0:T(8,128)(2,1)} %w_ref.3, f32[64,1]{1,0:T(8,128)} %copy.50.gain_ref), custom_call_target="tpu_custom_call" | custom-call | flops 99999997952 | bytes 1048576 | tf_op jit(solution)/shard_map/join_columns/pallas_call | solution.py:546
  606.9 16.2 %collective-permute-done.52 = bf16[64,2048]{1,0:T(8,128)(2,1)S(1)} collective-permute-done((bf16[64,2048]{1,0:T(8,128)(2,1)}, bf16[64,2048]{1,0:T(8,128)(2,1)S(1)}, u32[]{:S(2)}, u32[]{:S(2)}) %collective-permute-start.52) | collective-permute-done | bytes 262176 | tf_op jit(solution)/shard_map/ppermute | solution.py:967
  (309 shorter events, 177.3 us)
Async XLA Ops:
  15.6 52.0 %all-gather.5.cloned.1.call-start = ((), (), s32[]{:S(2)}) async-start(), calls=%async_computation.9 | async-start | bytes 1966080 | tf_op jit(solution)/shard_map/all_gather | solution.py:132
  28.3 40.1 %collective-permute-start.1 = (bf16[256,2048]{1,0:T(8,128)(2,1)S(1)}, bf16[256,2048]{1,0:T(8,128)(2,1)}, u32[]{:S(2)}, u32[]{:S(2)}) collective-permute-start(bf16[256,2048]{1,0:T(8,128)(2,1)S(1)} %fusion.2.refs_0_), channel_id=1, source_target_pairs={{0,4},{1,3},{2,6},{3,1},{4,0},{5,7},{6,2},{7,5},{8,12},{9,11},{10,... | collective-permute-start | bytes 3145736 | tf_op jit(solution)/shard_map/ppermute | solution.py:54
  37.1 23.9 %collective-permute-start.2 = (bf16[256,2048]{1,0:T(8,128)(2,1)}, bf16[256,2048]{1,0:T(8,128)(2,1)}, u32[]{:S(2)}, u32[]{:S(2)}) collective-permute-start(bf16[256,2048]{1,0:T(8,128)(2,1)} %collective-permute-done.refs_1_), channel_id=1, source_target_pairs={{0,4},{1,3},{2,6},{3,1},{4,0},{5,7},{6,2},{7,5},{8,12},{9,11},{10,... | collective-permute-start | bytes 3145736 | tf_op jit(solution)/shard_map/ppermute | solution.py:54
  72.1 23.6 %all-to-all-start.1 = ((bf16[8,64,1408]{2,1,0:T(8,128)(2,1)}), bf16[8,64,1408]{2,1,0:T(8,128)(2,1)S(1)}, u32[]{:S(2)}, u32[]{:S(2)}) async-start(bf16[8,64,1408]{2,1,0:T(8,128)(2,1)} %split_columns.1), calls=%async_computation.1 | async-start | bytes 2883584 | tf_op jit(solution)/shard_map/all_to_all | solution.py:128
  76.6 43.7 %all-gather.7.cloned.1.call-start = ((), (), s32[]{:S(2)}) async-start(), calls=%async_computation.10 | async-start | bytes 1310720 | tf_op jit(solution)/shard_map/all_gather | solution.py:132
  77.4 159.9 %all-gather.9.cloned.1.call-start = ((), (), s32[]{:S(2)}) async-start(), calls=%async_computation.11 | async-start | bytes 7208960 | tf_op jit(solution)/shard_map/all_gather | solution.py:132
  124.3 178.8 %all-gather.11.cloned.1.call-start = ((), (), s32[]{:S(2)}) async-start(), calls=%async_computation.12 | async-start | bytes 3604480 | tf_op jit(solution)/shard_map/all_gather | solution.py:132
  130.8 26.0 %collective-permute-start.10 = (bf16[512,2048]{1,0:T(8,128)(2,1)S(1)}, bf16[512,2048]{1,0:T(8,128)(2,1)S(1)}, u32[]{:S(2)}, u32[]{:S(2)}) collective-permute-start(bf16[512,2048]{1,0:T(8,128)(2,1)S(1)} %add_convert_fusion.1), channel_id=1, source_target_pairs={{0,4},{1,3},{2,6},{3,1},{4,0},{5,7},{6,2},{7,5},{8,12},{9,11},{10,... | collective-permute-start | bytes 6291464 | tf_op jit(solution)/shard_map/ppermute | solution.py:54
  158.1 22.6 %collective-permute-start.11 = (bf16[256,2048]{1,0:T(8,128)(2,1)S(1)}, bf16[256,2048]{1,0:T(8,128)(2,1)S(1)}, u32[]{:S(2)}, u32[]{:S(2)}) collective-permute-start(bf16[256,2048]{1,0:T(8,128)(2,1)S(1)} %slice.204), channel_id=1, source_target_pairs={{0,2},{1,5},{2,0},{3,7},{4,6},{5,1},{6,4},{7,3},{8,10},{9,13},{10,... | collective-permute-start | bytes 3145736 | tf_op jit(solution)/shard_map/ppermute | solution.py:54
  182.9 23.1 %collective-permute-start.12 = (bf16[256,2048]{1,0:T(8,128)(2,1)S(1)}, bf16[256,2048]{1,0:T(8,128)(2,1)}, u32[]{:S(2)}, u32[]{:S(2)}) collective-permute-start(bf16[256,2048]{1,0:T(8,128)(2,1)S(1)} %multiply_convert_fusion.refs_0_), channel_id=1, source_target_pairs={{0,2},{1,5},{2,0},{3,7},{4,6},{5,1},{6,4},{7,3},{8,10},{9,13},{10,... | collective-permute-start | bytes 3145736 | tf_op jit(solution)/shard_map/ppermute | solution.py:54
  184.4 26.2 %collective-permute-start.13 = (bf16[256,2048]{1,0:T(8,128)(2,1)S(1)}, bf16[256,2048]{1,0:T(8,128)(2,1)}, u32[]{:S(2)}, u32[]{:S(2)}) collective-permute-start(bf16[256,2048]{1,0:T(8,128)(2,1)S(1)} %multiply_convert_fusion.refs_0_), channel_id=1, source_target_pairs={{0,4},{1,3},{2,6},{3,1},{4,0},{5,7},{6,2},{7,5},{8,12},{9,11},{10,... | collective-permute-start | bytes 3145736 | tf_op jit(solution)/shard_map/ppermute | solution.py:54
  225.8 287.8 %reduce-scatter.11.cloned.1.call-start = ((), (), s32[]{:S(2)}) async-start(), calls=%async_computation.16 | async-start | bytes 3604480 | tf_op jit(solution)/shard_map/reduce_scatter | solution.py:136
  228.4 32.8 %collective-permute-start.19 = (bf16[256,2048]{1,0:T(8,128)(2,1)S(1)}, bf16[256,2048]{1,0:T(8,128)(2,1)S(1)}, u32[]{:S(2)}, u32[]{:S(2)}) collective-permute-start(bf16[256,2048]{1,0:T(8,128)(2,1)S(1)} %copy-done.15), channel_id=1, source_target_pairs={{0,2},{1,5},{2,0},{3,7},{4,6},{5,1},{6,4},{7,3},{8,10},{9,13},{10,... | collective-permute-start | bytes 3145736 | tf_op jit(solution)/shard_map/ppermute | solution.py:54
  228.4 34.9 %collective-permute-start.20 = (bf16[256,2048]{1,0:T(8,128)(2,1)S(1)}, bf16[256,2048]{1,0:T(8,128)(2,1)}, u32[]{:S(2)}, u32[]{:S(2)}) collective-permute-start(bf16[256,2048]{1,0:T(8,128)(2,1)S(1)} %copy-done.15), channel_id=1, source_target_pairs={{0,4},{1,3},{2,6},{3,1},{4,0},{5,7},{6,2},{7,5},{8,12},{9,11},{10,... | collective-permute-start | bytes 3145736 | tf_op jit(solution)/shard_map/ppermute | solution.py:54
  276.6 23.3 %collective-permute-start.26 = (bf16[256,2048]{1,0:T(8,128)(2,1)S(1)}, bf16[256,2048]{1,0:T(8,128)(2,1)}, u32[]{:S(2)}, u32[]{:S(2)}) collective-permute-start(bf16[256,2048]{1,0:T(8,128)(2,1)S(1)} %copy-done.6), channel_id=1, source_target_pairs={{0,2},{1,5},{2,0},{3,7},{4,6},{5,1},{6,4},{7,3},{8,10},{9,13},{10,... | collective-permute-start | bytes 3145736 | tf_op jit(solution)/shard_map/ppermute | solution.py:54
  277.8 24.1 %collective-permute-start.27 = (bf16[256,2048]{1,0:T(8,128)(2,1)S(1)}, bf16[256,2048]{1,0:T(8,128)(2,1)S(1)}, u32[]{:S(2)}, u32[]{:S(2)}) collective-permute-start(bf16[256,2048]{1,0:T(8,128)(2,1)S(1)} %copy-done.6), channel_id=1, source_target_pairs={{0,4},{1,3},{2,6},{3,1},{4,0},{5,7},{6,2},{7,5},{8,12},{9,11},{10,... | collective-permute-start | bytes 3145736 | tf_op jit(solution)/shard_map/ppermute | solution.py:54
  335.4 198.6 %reduce-scatter.5.cloned.1.call-start = ((), (), s32[]{:S(2)}) async-start(), calls=%async_computation.13 | async-start | bytes 7208960 | tf_op jit(solution)/shard_map/reduce_scatter | solution.py:136
  343.4 35.5 %collective-permute-start.33 = (bf16[512,2048]{1,0:T(8,128)(2,1)}, bf16[512,2048]{1,0:T(8,128)(2,1)S(1)}, u32[]{:S(2)}, u32[]{:S(2)}) collective-permute-start(bf16[512,2048]{1,0:T(8,128)(2,1)} %convert_add_fusion.6), channel_id=1, source_target_pairs={{0,4},{1,3},{2,6},{3,1},{4,0},{5,7},{6,2},{7,5},{8,12},{9,11},{10,... | collective-permute-start | bytes 6291464 | tf_op jit(solution)/shard_map/ppermute | solution.py:54
  357.6 24.5 %collective-permute-start.32 = (bf16[512,2048]{1,0:T(8,128)(2,1)}, bf16[512,2048]{1,0:T(8,128)(2,1)}, u32[]{:S(2)}, u32[]{:S(2)}) collective-permute-start(bf16[512,2048]{1,0:T(8,128)(2,1)} %convolution_convert_fusion.6), channel_id=1, source_target_pairs={{0,1},{1,0},{2,3},{3,2},{4,5},{5,4},{6,7},{7,6},{8,9},{9,8},{10,11... | collective-permute-start | bytes 6291464 | tf_op jit(solution)/shard_map/ppermute | solution.py:58
  360.8 27.0 %collective-permute-start.31 = (bf16[512,2048]{1,0:T(8,128)(2,1)}, bf16[512,2048]{1,0:T(8,128)(2,1)}, u32[]{:S(2)}, u32[]{:S(2)}) collective-permute-start(bf16[512,2048]{1,0:T(8,128)(2,1)} %convolution_convert_fusion.7), channel_id=1, source_target_pairs={{0,1},{1,0},{2,3},{3,2},{4,5},{5,4},{6,7},{7,6},{8,9},{9,8},{10,11... | collective-permute-start | bytes 6291464 | tf_op jit(solution)/shard_map/ppermute | solution.py:58
  377.2 195.4 %reduce-scatter.7.cloned.1.call-start = ((), (), s32[]{:S(2)}) async-start(), calls=%async_computation.14 | async-start | bytes 1966080 | tf_op jit(solution)/shard_map/reduce_scatter | solution.py:136
  378.9 20.9 %collective-permute-start.37 = (bf16[256,2048]{1,0:T(8,128)(2,1)}, bf16[256,2048]{1,0:T(8,128)(2,1)S(1)}, u32[]{:S(2)}, u32[]{:S(2)}) collective-permute-start(bf16[256,2048]{1,0:T(8,128)(2,1)} %copy-done.28), channel_id=1, source_target_pairs={{0,1},{1,0},{2,3},{3,2},{4,5},{5,4},{6,7},{7,6},{8,9},{9,8},{10,11... | collective-permute-start | bytes 3145736 | tf_op jit(solution)/shard_map/ppermute | solution.py:58
  431.5 69.6 %collective-permute-start.41 = (bf16[256,2048]{1,0:T(8,128)(2,1)}, bf16[256,2048]{1,0:T(8,128)(2,1)}, u32[]{:S(2)}, u32[]{:S(2)}) collective-permute-start(bf16[256,2048]{1,0:T(8,128)(2,1)} %get-tuple-element.85.refs_0_), channel_id=1, source_target_pairs={{0,2},{1,5},{2,0},{3,7},{4,6},{5,1},{6,4},{7,3},{8,10},{9,13},{10,... | collective-permute-start | bytes 3145736 | tf_op jit(solution)/shard_map/ppermute | solution.py:90
  431.7 69.4 %collective-permute-start.42 = (bf16[256,2048]{1,0:T(8,128)(2,1)}, bf16[256,2048]{1,0:T(8,128)(2,1)}, u32[]{:S(2)}, u32[]{:S(2)}) collective-permute-start(bf16[256,2048]{1,0:T(8,128)(2,1)} %get-tuple-element.85.refs_0_), channel_id=1, source_target_pairs={{0,4},{1,3},{2,6},{3,1},{4,0},{5,7},{6,2},{7,5},{8,12},{9,11},{10,... | collective-permute-start | bytes 3145736 | tf_op jit(solution)/shard_map/ppermute | solution.py:90
  432.6 68.5 %collective-permute-start.43 = (bf16[256,2048]{1,0:T(8,128)(2,1)}, bf16[256,2048]{1,0:T(8,128)(2,1)}, u32[]{:S(2)}, u32[]{:S(2)}) collective-permute-start(bf16[256,2048]{1,0:T(8,128)(2,1)} %get-tuple-element.85.refs_0_), channel_id=1, source_target_pairs={{0,6},{1,7},{2,4},{3,5},{4,2},{5,3},{6,0},{7,1},{8,14},{9,15},{10,... | collective-permute-start | bytes 3145736 | tf_op jit(solution)/shard_map/ppermute | solution.py:90
  434.1 67.8 %collective-permute-start.39 = (bf16[512,2048]{1,0:T(8,128)(2,1)}, bf16[512,2048]{1,0:T(8,128)(2,1)}, u32[]{:S(2)}, u32[]{:S(2)}) collective-permute-start(bf16[512,2048]{1,0:T(8,128)(2,1)} %convert_add_fusion.3), channel_id=1, source_target_pairs={{0,4},{1,3},{2,6},{3,1},{4,0},{5,7},{6,2},{7,5},{8,12},{9,11},{10,... | collective-permute-start | bytes 6291464 | tf_op jit(solution)/shard_map/ppermute | solution.py:54
  506.9 27.1 %collective-permute-start.44 = (bf16[512,2048]{1,0:T(8,128)(2,1)}, bf16[512,2048]{1,0:T(8,128)(2,1)}, u32[]{:S(2)}, u32[]{:S(2)}) collective-permute-start(bf16[512,2048]{1,0:T(8,128)(2,1)} %convolution_convert_fusion.5), channel_id=1, source_target_pairs={{0,1},{1,0},{2,3},{3,2},{4,5},{5,4},{6,7},{7,6},{8,9},{9,8},{10,11... | collective-permute-start | bytes 6291464 | tf_op jit(solution)/shard_map/ppermute | solution.py:58
  512.7 33.0 %collective-permute-start.46 = (bf16[512,2048]{1,0:T(8,128)(2,1)}, bf16[512,2048]{1,0:T(8,128)(2,1)}, u32[]{:S(2)}, u32[]{:S(2)}) collective-permute-start(bf16[512,2048]{1,0:T(8,128)(2,1)} %add_convert_fusion), channel_id=1, source_target_pairs={{0,4},{1,3},{2,6},{3,1},{4,0},{5,7},{6,2},{7,5},{8,12},{9,11},{10,... | collective-permute-start | bytes 6291464 | tf_op jit(solution)/shard_map/ppermute | solution.py:54
  527.1 37.0 %collective-permute-start.40 = (bf16[256,2048]{1,0:T(8,128)(2,1)}, bf16[256,2048]{1,0:T(8,128)(2,1)}, u32[]{:S(2)}, u32[]{:S(2)}) collective-permute-start(bf16[256,2048]{1,0:T(8,128)(2,1)} %slice.202), channel_id=1, source_target_pairs={{0,2},{1,5},{2,0},{3,7},{4,6},{5,1},{6,4},{7,3},{8,10},{9,13},{10,... | collective-permute-start | bytes 3145736 | tf_op jit(solution)/shard_map/ppermute | solution.py:54
  557.2 23.6 %all-to-all-start.4 = ((bf16[8,64,1408]{2,1,0:T(8,128)(2,1)}), bf16[8,64,1408]{2,1,0:T(8,128)(2,1)}, u32[]{:S(2)}, u32[]{:S(2)}) async-start(bf16[8,64,1408]{2,1,0:T(8,128)(2,1)} %bitcast.17), calls=%async_computation.7 | async-start | bytes 2883584 | tf_op jit(solution)/shard_map/all_to_all | solution.py:128
  564.0 37.5 %reduce-scatter.9.cloned.1.call-start = ((), (), s32[]{:S(2)}) async-start(), calls=%async_computation.15 | async-start | bytes 1310720 | tf_op jit(solution)/shard_map/reduce_scatter | solution.py:136
  601.5 21.6 %collective-permute-start.52 = (bf16[64,2048]{1,0:T(8,128)(2,1)}, bf16[64,2048]{1,0:T(8,128)(2,1)S(1)}, u32[]{:S(2)}, u32[]{:S(2)}) collective-permute-start(bf16[64,2048]{1,0:T(8,128)(2,1)} %reduce-scatter.9.cloned.1.call-done), channel_id=1, source_target_pairs={{0,0},{8,1},{16,2},{24,3},{1,4},{9,5},{17,6},{25,7},{2,8},{10,9},{... | collective-permute-start | bytes 786440 | tf_op jit(solution)/shard_map/ppermute | solution.py:967
  (90 other events, 1044.2 us)
Sparse Core Ops, SparseCore 0:
  28.4 39.1 all-gather.4
  79.6 33.6 all-gather.6
  124.5 112.8 all-gather.8
  238.8 57.2 all-gather.10
  335.5 53.2 reduce-scatter.10
  390.9 102.3 reduce-scatter.4
  534.1 32.2 reduce-scatter.6
  572.8 28.6 reduce-scatter.8

commit v2 on v0

--- a/solution.py
+++ b/solution.py
@@ -195,7 +195,9 @@
     def _():
         copies = [
             pltpu.make_async_copy(
-                source.at[pl.ds(i * rows, rows)], buffer.at[pl.ds(i * rows, rows)], semaphores.at[i]
+                source.at[pl.ds(i * rows, rows), pl.ds(0, buffer.shape[1])],
+                buffer.at[pl.ds(i * rows, rows)],
+                semaphores.at[i],
             )
             for i in range(count)
         ]
@@ -286,7 +288,7 @@
                 pltpu.VMEM((n, tok, D), BF),
                 pltpu.SemaphoreType.DMA((n,)),
                 pltpu.SemaphoreType.DMA((n,)),
-                pltpu.VMEM(weight.shape, BF),
+                pltpu.VMEM((D, width + 2 * HD), BF),
                 pltpu.SemaphoreType.DMA((chunks(D),)),
             ],
         ),
@@ -901,16 +903,6 @@
     slots = jnp.arange(n_ctx, dtype=jnp.int32)
     slot_of = jnp.sum(jnp.where(order[None, :] == slots[:, None], slots[None, :], 0), axis=1)
     index = jnp.arange(seq, dtype=jnp.int32)
-    lengths = doc_lengths[0]
-    ends = jnp.cumsum(lengths)
-    starts = jnp.sum((index[:, None] >= ends[None, :]).astype(jnp.int32) * lengths[None, :], axis=1)
-    lane = jnp.arange(128, dtype=F32) % HALF
-    frequency = 10000.0 ** (-lane * 2.0 / HD)
-    angles = (index - starts).astype(F32)[:, None] * frequency[None, :]
-    cosine = jnp.cos(angles)
-    sine = jnp.sin(angles)
-    starts_row = starts[None, :]
-
     gain_one = gain_attn.astype(F32)[:, None]
     gain_two = gain_ffn.astype(F32)[:, None]
     qkv = (qkv_weight.astype(F32) * gain_one).astype(BF)
@@ -920,19 +912,29 @@
     kv_cols = jnp.repeat(jnp.concatenate([k_cols, v_cols], axis=2), sharers, axis=0)
     owner_pairs = [(b, b % n_dp * n_ctx + b // n_dp) for b in range(n_dp * n_ctx)]
     out_own = lax.ppermute(out_weight, ("dp", "ctx"), owner_pairs)
-    out_part = gather_dp(out_own)
-    qkv_own = exchange(after(jnp.concatenate([q_cols, kv_cols], axis=2), out_own)).reshape(
-        n_ctx * rows, columns
-    )
-    qkv_part = gather_dp(qkv_own)
+    qkv_own = exchange(jnp.concatenate([q_cols, kv_cols], axis=2)).reshape(n_ctx * rows, columns)
+    attn_part = gather_dp(
+        jnp.concatenate([qkv_own, out_own.reshape(n_ctx * rows, width)], axis=1)
+    )
+    qkv_part = attn_part[:, :columns]
+    out_part = attn_part[:, columns:].reshape(width, D)
 
     hidden_in = block_in.astype(F32)
     rms_one = lax.rsqrt(jnp.mean(hidden_in * hidden_in, axis=-1, keepdims=True) + EPS)
-    one_pieces = gather_slots(after((hidden_in * rms_one).astype(BF), qkv_own), n_ctx)
-
+    one_direct = gather_direct(after((hidden_in * rms_one).astype(BF), qkv_own, out_own), n_ctx)
+    lengths = after(doc_lengths[0], one_direct[1])
+    ends = jnp.cumsum(lengths)
+    starts = jnp.sum((index[:, None] >= ends[None, :]).astype(jnp.int32) * lengths[None, :], axis=1)
+    lane = jnp.arange(128, dtype=F32) % HALF
+    frequency = 10000.0 ** (-lane * 2.0 / HD)
+    angles = (index - starts).astype(F32)[:, None] * frequency[None, :]
+    cosine = jnp.cos(angles)
+    sine = jnp.sin(angles)
+    starts_row = starts[None, :]
     gate_up_cols = split_columns(
         gate_up_weight, after(gain_two, cosine, sine), n_ctx, n_dp, ff_rows
     )
+    one_pieces = gather_rest(one_direct, n_ctx, (), (attn_part, gate_up_cols))
     gate_up_own = exchange(after(gate_up_cols, *one_pieces[: n_ctx // 2])).reshape(
         n_ctx * rows, 2 * ff
     )
@@ -940,13 +942,14 @@
     down_part = gather_dp(after(down_weight, gate_up_own))
 
     queries, keys, values, keys_t, values_t, all_one = project_qkv(
-        order, one_pieces, qkv_part, spread_matrix(width), widen_matrix(width), cosine, sine, width, tok
-    )
-    out_pieces = gather_slots(out_part, n_ctx)
+        order, one_pieces, attn_part, spread_matrix(width), widen_matrix(width), cosine, sine, width, tok
+    )
+    out_direct = gather_direct(out_part, n_ctx)
     attn, slot_attn, attended, lse = attend_forward(
-        slot_of, starts_row, after(queries, gate_up_own), keys, values_t, heads, tok, 0, n_ctx, ()
+        slot_of, starts_row, after(queries, gate_up_own, *out_direct), keys, values_t, heads, tok, 0, n_ctx, ()
     )
     attn_tokens = exchange(attn.reshape(n_ctx, tok, width))
+    out_pieces = gather_rest(out_direct, n_ctx, (queries,), (attn,))
     state, norm_two = project_out(order, attn_tokens, out_pieces, block_in)
 
     two_pieces = gather_slots(norm_two, n_ctx)

time: 628 us -> 630 us (level)
  starting transfers between devices: 116 us -> 81.1 us
  blocking collectives: 19.8 us -> 38 us
  waiting for transfers between devices: 135 us -> 146 us
    ppermute x26, starting transfers between devices: 43.7 us -> 18.6 us  [swap_core(): return lax.ppermute(x, 'ctx', [(c, c ^ 1) for c in range(n_ctx)])]
    all_to_all x1 -> x2, blocking collectives: 19.8 us -> 38 us  [exchange(): return lax.all_to_all(x, 'ctx', split_axis=0, concat_axis=0, tiled=False)]
    ppermute x18, waiting for transfers between devices: 78.4 us -> 92.6 us  [swap_stage(): return lax.ppermute(x, 'ctx', pairs)]
    all_to_all x5 -> x4, waiting for transfers between devices: 27.7 us -> 15.8 us  [exchange(): return lax.all_to_all(x, 'ctx', split_axis=0, concat_axis=0, tiled=False)]
    all_to_all x5 -> x4, starting transfers between devices: 35.7 us -> 27.3 us  [exchange(): return lax.all_to_all(x, 'ctx', split_axis=0, concat_axis=0, tiled=False)]
  transfers between devices with their start and end apart: 62 -> 60, of which waited for: 19 -> 18; matrix products, arithmetic and copies ran while one was open for 22% -> 22% of each run, Pallas kernels for 27% -> 27%
where the time goes in v2:
time: 630 us; the launch traced here: 622 us
  Pallas kernels  184 us (29%)
  waiting for transfers between devices  146 us (23%)
  matrix products  102 us (16%)
  starting transfers between devices  81.1 us (13%)
  other arithmetic  39.1 us (6%)
  blocking collectives  38 us (6%)
  local copies, waits for them, and re-layouts  16.5 us (3%)
  between operations  15.3 us (2%)
    ppermute x18, waiting for transfers between devices, swap_stage(): return lax.ppermute(x, 'ctx', pairs)  92.6 us
    pallas_call x1, Pallas kernels, attend_backward(): pl.pallas_call(kernel, grid_spec=pltpu.PrefetchScalarGridSpec(num_scalar_...  56.1 us
    dot_general x8, matrix products, nt(): lax.dot_general(a, b, (((1,), (1,)), ((), ())), preferred_element_type=F32)  45.5 us
    dot_general x4, matrix products, outer_rows(): lax.dot_general(activations, gradients, (((0,), (0,)), ((), ())), preferr...  39.9 us
    all_to_all x2, blocking collectives, exchange(): return lax.all_to_all(x, 'ctx', split_axis=0, concat_axis=0, tiled=False)  38 us
    all_to_all x4, starting transfers between devices, exchange(): return lax.all_to_all(x, 'ctx', split_axis=0, concat_axis=0, tiled=False)  27.3 us
    ppermute x18, starting transfers between devices, swap_stage(): return lax.ppermute(x, 'ctx', pairs)  25.2 us
    pallas_call x1, Pallas kernels, attend_forward(): pl.pallas_call(kernel, grid_spec=pltpu.PrefetchScalarGridSpec(num_scalar_...  24.7 us
  transfers between devices with their start and end apart: 60, of which 18 were waited for; matrix products, arithmetic and copies ran while one was open for 22% of the time, Pallas kernels for 27%

profile of v2, /device:TPU:1, one launch (start us, length us, event | category | flops | bytes accessed | tf_op | source)
XLA Modules:
  0.0 621.5 jit_solution(13605307561369866435)
XLA Ops:
  25.1 8.7 %collective-permute-start.1 = (bf16[256,2048]{1,0:T(8,128)(2,1)}, bf16[256,2048]{1,0:T(8,128)(2,1)}, u32[]{:S(2)}, u32[]{:S(2)}) collective-permute-start(bf16[256,2048]{1,0:T(8,128)(2,1)} %fusion.2.refs_0_), channel_id=1, source_target_pairs={{0,2},{1,5},{2,0},{3,7},{4,6},{5,1},{6,4},{7,3},{8,10},{9,13},{10,... | collective-permute-start | bytes 3145736 | tf_op jit(solution)/shard_map/ppermute | solution.py:54
  35.0 20.8 %collective-permute-done.1.refs_1_ = bf16[256,2048]{1,0:T(8,128)(2,1)} collective-permute-done((bf16[256,2048]{1,0:T(8,128)(2,1)}, bf16[256,2048]{1,0:T(8,128)(2,1)}, u32[]{:S(2)}, u32[]{:S(2)}) %collective-permute-start.1) | collective-permute-done | bytes 1048608 | tf_op jit(solution)/shard_map/ppermute | solution.py:54
  65.6 11.0 %collective-permute-done.3.refs_3_ = bf16[256,2048]{1,0:T(8,128)(2,1)} collective-permute-done((bf16[256,2048]{1,0:T(8,128)(2,1)}, bf16[256,2048]{1,0:T(8,128)(2,1)}, u32[]{:S(2)}, u32[]{:S(2)}) %collective-permute-start.3) | collective-permute-done | bytes 1048608 | tf_op jit(solution)/shard_map/ppermute | solution.py:54
  76.7 6.7 %all-to-all-start.1 = ((bf16[8,64,1408]{2,1,0:T(8,128)(2,1)}), bf16[8,64,1408]{2,1,0:T(8,128)(2,1)S(1)}, u32[]{:S(2)}, u32[]{:S(2)}) async-start(bf16[8,64,1408]{2,1,0:T(8,128)(2,1)} %split_columns.1), calls=%async_computation.1 | async-start | bytes 2883584 | tf_op jit(solution)/shard_map/all_to_all | solution.py:128
  83.4 7.0 %all-gather.4.cloned.1.call-done.refs_8_ = bf16[2048,640]{1,0:T(8,128)(2,1)} async-done(((bf16[512,640]{1,0:T(8,128)(2,1)}), bf16[2048,640]{1,0:T(8,128)(2,1)}) %all-gather.4.cloned.1.call-update) | async-done | bytes 2621456 | tf_op jit(solution)/shard_map/all_gather | solution.py:132
  92.3 7.2 %all-to-all-done.1 = bf16[8,64,1408]{2,1,0:T(8,128)(2,1)S(1)} async-done(((bf16[8,64,1408]{2,1,0:T(8,128)(2,1)}), bf16[8,64,1408]{2,1,0:T(8,128)(2,1)S(1)}, u32[]{:S(2)}, u32[]{:S(2)}) %all-to-all-start.1) | async-done | bytes 1441824 | tf_op jit(solution)/shard_map/all_to_all | solution.py:128
  104.7 16.8 %project_qkv.1 = (bf16[2048,256]{1,0:T(8,128)(2,1)}, bf16[2048,256]{1,0:T(8,128)(2,1)}, bf16[2048,256]{1,0:T(8,128)(2,1)}, bf16[64,2048]{1,0:T(8,128)(2,1)}, bf1...) custom-call(s32[8]{0:T(128)} %copy-done.29, bf16[256,2048]{1,0:T(8,128)(2,1)} %fusion.2.refs_0_, ...), custom_call_target="tpu_custom_call" | custom-call | flops 99999997952 | bytes 1048576 | tf_op jit(solution)/shard_map/project_qkv/pallas_call | solution.py:265
  129.2 24.7 %attend_forward.1 = (bf16[2048,256]{1,0:T(8,128)(2,1)}, bf16[2048,256]{1,0:T(8,128)(2,1)}, f32[2048,256]{1,0:T(8,128)}, f32[8,4,256]{2,1,0:T(4,128)}) custom-call(s32[8]{0:T(128)} %select_reduce_fusion.1.slot_ref, s32[1,2048]{1,0:T(1,128)} %bitcast.60, bf16[2048,256]{1,0:T(8,128)(2,1)} %get-tuple-element.66.q_ref, ...), custom_call_target="tpu_custom_call" | custom-call | flops 99999997952 | bytes 1048576 | tf_op jit(solution)/shard_map/attend_forward/pallas_call | solution.py:680
  155.9 18.7 %all_to_all.30.a_ref = bf16[8,256,256]{2,1,0:T(8,128)(2,1)} all-to-all(bf16[8,256,256]{2,1,0:T(8,128)(2,1)} %bitcast.54), channel_id=1, replica_groups=mesh['dp'=4,'ctx'=8] {'ctx'}, dimensions={0} | all-to-all | bytes 2097152 | tf_op jit(solution)/shard_map/all_to_all | solution.py:128
  177.5 11.1 %project_out.1 = (f32[256,2048]{1,0:T(8,128)}, bf16[256,2048]{1,0:T(8,128)(2,1)}) custom-call(s32[8]{0:T(128)} %copy-done.29, bf16[8,256,256]{2,1,0:T(8,128)(2,1)} %all_to_all.30.a_ref, bf16[256,2048]{1,0:T(8,128)(2,1)} %copy-done.6, bf16[256,2048]{1,0:T(8,128)(2,1)} %copy-done.12, bf16[256,2048]{1,0:T(8,128)(2,1)} %collective-permute-done.9.refs_2_, ...), custom_call_target="tpu_custom_call" | custom-call | flops 1048576 | bytes 1048576 | tf_op jit(solution)/shard_map/project_out/pallas_call | solution.py:335
  189.8 21.9 %collective-permute-done.15.refs_1_ = bf16[256,2048]{1,0:T(8,128)(2,1)S(1)} collective-permute-done((bf16[256,2048]{1,0:T(8,128)(2,1)}, bf16[256,2048]{1,0:T(8,128)(2,1)S(1)}, u32[]{:S(2)}, u32[]{:S(2)}) %collective-permute-start.15) | collective-permute-done | bytes 1048608 | tf_op jit(solution)/shard_map/ppermute | solution.py:54
  217.3 8.5 %collective-permute-done.17.refs_3_ = bf16[256,2048]{1,0:T(8,128)(2,1)} collective-permute-done((bf16[256,2048]{1,0:T(8,128)(2,1)S(1)}, bf16[256,2048]{1,0:T(8,128)(2,1)}, u32[]{:S(2)}, u32[]{:S(2)}) %collective-permute-start.17) | collective-permute-done | bytes 1048608 | tf_op jit(solution)/shard_map/ppermute | solution.py:54
  234.2 24.1 %feed_forward.1 = (bf16[2048,704]{1,0:T(8,128)(2,1)}, bf16[2048,1408]{1,0:T(8,128)(2,1)}, bf16[2048,2048]{1,0:T(8,128)(2,1)}) custom-call(bf16[256,2048]{1,0:T(8,128)(2,1)} %get-tuple-element.76.refs_0_, bf16[256,2048]{1,0:T(8,128)(2,1)} %copy-done.39, bf16[256,2048]{1,0:T(8,128)(2,1)} %collective-permute-done.16.refs_2_, ...), custom_call_target="tpu_custom_call" | custom-call | flops 99999997952 | bytes 1048576 | tf_op jit(solution)/shard_map/feed_forward/pallas_call | solution.py:384
  260.5 11.9 %collective-permute-done.24.refs_3_ = bf16[256,2048]{1,0:T(8,128)(2,1)S(1)} collective-permute-done((bf16[256,2048]{1,0:T(8,128)(2,1)S(1)}, bf16[256,2048]{1,0:T(8,128)(2,1)S(1)}, u32[]{:S(2)}, u32[]{:S(2)}) %collective-permute-start.24) | collective-permute-done | bytes 1048608 | tf_op jit(solution)/shard_map/ppermute | solution.py:54
  277.2 6.5 %lay_out.2.g_ref = bf16[2048,2048]{1,0:T(8,128)(2,1)} custom-call(bf16[256,2048]{1,0:T(8,128)(2,1)} %g_ref.1, bf16[256,2048]{1,0:T(8,128)(2,1)} %copy-done.19, bf16[256,2048]{1,0:T(8,128)(2,1)} %collective-permute-done.23.refs_2_, bf16[256,2048]{1,0:T(8,128)(2,1)} %copy-done.20, bf16[256,2048]{1,0:T(8,128)(2,1)} %copy-done.22, bf16[256,2048]{1,0:T(8,128)(2,1)} %copy-done.23, ...), custom_call_target="tpu_custom_call" | custom-call | flops 1048576 | bytes 1048576 | tf_op jit(solution)/shard_map/lay_out/pallas_call | solution.py:473
  283.7 10.7 %convolution_convert_fusion.1 = bf16[704,2048]{1,0:T(8,128)(2,1)} fusion(bf16[2048,704]{1,0:T(8,128)(2,1)} %get-tuple-element.83, bf16[2048,2048]{1,0:T(8,128)(2,1)} %lay_out.2.g_ref), kind=kOutput, calls=%fused_computation.9 | convolution fusion | flops 5907021824 | bytes 14155776 | tf_op jit(solution)/shard_map/dot_general | solution.py:841
  294.4 15.2 %feed_backward.1 = bf16[2048,1408]{1,0:T(8,128)(2,1)} custom-call(bf16[2048,1408]{1,0:T(8,128)(2,1)} %get-tuple-element.81.factor_ref, bf16[2048,2048]{1,0:T(8,128)(2,1)} %lay_out.2.g_ref, bf16[704,2048]{1,0:T(8,128)(2,1)} %all-gather.8.cloned.1.call-done.w_hbm), custom_call_target="tpu_custom_call" | custom-call | flops 99999997952 | bytes 1048576 | tf_op jit(solution)/shard_map/feed_backward/pallas_call | solution.py:429
  309.6 7.8 %convolution_convert_fusion.7 = bf16[512,2048]{1,0:T(8,128)(2,1)} fusion(bf16[2048,1408]{1,0:T(8,128)(2,1)} %all-gather.6.cloned.1.call-done.refs_8_, bf16[2048,1408]{1,0:T(8,128)(2,1)} %feed_backward.1), kind=kOutput, calls=%fused_computation.15 | convolution fusion | flops 2953838592 | bytes 9306112 | tf_op jit(solution)/shard_map/dot_general | solution.py:27
  317.4 7.8 %convolution_convert_fusion.6 = bf16[512,2048]{1,0:T(8,128)(2,1)} fusion(bf16[2048,1408]{1,0:T(8,128)(2,1)} %all-gather.6.cloned.1.call-done.refs_8_, bf16[2048,1408]{1,0:T(8,128)(2,1)} %feed_backward.1), kind=kOutput, calls=%fused_computation.14 | convolution fusion | flops 2953838592 | bytes 9306112 | tf_op jit(solution)/shard_map/dot_general | solution.py:27
  325.9 8.0 %convert_add_fusion.6 = bf16[512,2048]{1,0:T(8,128)(2,1)} fusion(bf16[512,2048]{1,0:T(8,128)(2,1)S(1)} %collective-permute-done.29, bf16[2048,1408]{1,0:T(8,128)(2,1)} %all-gather.6.cloned.1.call-done.refs_8_, bf16[2048,1408]{1,0:T(8,128)(2,1)} %feed_backward.1), kind=kOutput, calls=%fused_computation.8 | convolution fusion | flops 2955935744 | bytes 11403264 | tf_op jit(solution)/shard_map/dot_general | solution.py:27
  335.1 9.6 %convert_add_fusion.5 = f32[512,2048]{1,0:T(8,128)} fusion(bf16[512,2048]{1,0:T(8,128)(2,1)} %collective-permute-done.30, bf16[2048,1408]{1,0:T(8,128)(2,1)} %all-gather.6.cloned.1.call-done.refs_8_, bf16[2048,1408]{1,0:T(8,128)(2,1)} %feed_backward.1), kind=kOutput, calls=%fused_computation.7 | convolution fusion | flops 2954887168 | bytes 13500416 | tf_op jit(solution)/shard_map/dot_general | solution.py:27
  351.6 15.8 %convolution_convert_fusion = bf16[2048,1408]{1,0:T(8,128)(2,1)} fusion(bf16[2048,2048]{1,0:T(8,128)(2,1)S(1)} %bitcast.68, bf16[2048,1408]{1,0:T(8,128)(2,1)S(1)} %bitcast.66), kind=kOutput, calls=%fused_computation | convolution fusion | flops 11814043648 | bytes 19922944 | tf_op jit(solution)/shard_map/dot_general | solution.py:841
  386.3 10.6 %branch_back.1 = (f32[256,2048]{1,0:T(8,128)}, bf16[256,2048]{1,0:T(8,128)(2,1)}, bf16[8,256,256]{2,1,0:T(8,128)(2,1)}) custom-call(s32[8]{0:T(128)} %copy-done.29, f32[256,2048]{1,0:T(8,128)} %slice_add_fusion.2.d_ref, f32[256,2048]{1,0:T(8,128)} %get-tuple-element.75.state_ref, bf16[256,2048]{1,0:T(8,128)(2,1)} %g_ref.1, bf16[256,2048]{1,0:T(8,128)(2,1)} %copy-done.6, ...), custom_call_target="tpu_custom_call" | custom-call | flops 1048576 | bytes 1048576 | tf_op jit(solution)/shard_map/branch_back/pallas_call | solution.py:524
  396.9 19.3 %all_to_all.31 = bf16[8,256,256]{2,1,0:T(8,128)(2,1)} all-to-all(bf16[8,256,256]{2,1,0:T(8,128)(2,1)} %get-tuple-element.87), channel_id=1, replica_groups=mesh['dp'=4,'ctx'=8] {'ctx'}, dimensions={0} | all-to-all | bytes 2097152 | tf_op jit(solution)/shard_map/all_to_all | solution.py:128
  419.8 56.1 %attend_backward.1 = bf16[2048,384]{1,0:T(8,128)(2,1)} custom-call(s32[8]{0:T(128)} %select_reduce_fusion.1.slot_ref, s32[1,2048]{1,0:T(1,128)} %bitcast.61, bf16[2048,256]{1,0:T(8,128)(2,1)} %get-tuple-element.66.q_ref, bf16[2048,256]{1,0:T(8,128)(2,1)} %get-tuple-element.67.k_ref, bf16[64,2048]{1,0:T(8,128)(2,1)} %get-tuple-element.90.kt_ref, ...), custom_call_target="tpu_custom_call" | custom-call | flops 20000000000 | bytes 1048576 | tf_op jit(solution)/shard_map/attend_backward/pallas_call | solution.py:812
  475.9 9.8 %convolution_convert_fusion.8 = bf16[2048,384]{1,0:T(8,128)(2,1)} fusion(bf16[2048,2048]{1,0:T(8,128)(2,1)} %get-tuple-element.94, bf16[2048,384]{1,0:T(8,128)(2,1)} %attend_backward.1), kind=kOutput, calls=%fused_computation.16 | convolution fusion | flops 3222011904 | bytes 11534336 | tf_op jit(solution)/shard_map/dot_general | solution.py:841
  521.1 9.2 %collective-permute-done.42 = bf16[512,2048]{1,0:T(8,128)(2,1)} collective-permute-done((bf16[512,2048]{1,0:T(8,128)(2,1)}, bf16[512,2048]{1,0:T(8,128)(2,1)}, u32[]{:S(2)}, u32[]{:S(2)}) %collective-permute-start.42) | collective-permute-done | bytes 2097184 | tf_op jit(solution)/shard_map/ppermute | solution.py:54
  543.8 6.6 %all-to-all-start.5 = ((bf16[8,64,1408]{2,1,0:T(8,128)(2,1)}), bf16[8,64,1408]{2,1,0:T(8,128)(2,1)}, u32[]{:S(2)}, u32[]{:S(2)}) async-start(bf16[8,64,1408]{2,1,0:T(8,128)(2,1)} %bitcast.18), calls=%async_computation.8 | async-start | bytes 2883584 | tf_op jit(solution)/shard_map/all_to_all | solution.py:128
  559.1 8.6 %all-to-all-done.5.s_ref = bf16[8,64,1408]{2,1,0:T(8,128)(2,1)} async-done(((bf16[8,64,1408]{2,1,0:T(8,128)(2,1)}), bf16[8,64,1408]{2,1,0:T(8,128)(2,1)}, u32[]{:S(2)}, u32[]{:S(2)}) %all-to-all-start.5) | async-done | bytes 1441824 | tf_op jit(solution)/shard_map/all_to_all | solution.py:128
  567.7 8.7 %all-to-all-start.4 = ((bf16[8,64,384]{2,1,0:T(8,128)(2,1)}), bf16[8,64,384]{2,1,0:T(8,128)(2,1)S(1)}, u32[]{:S(2)}, u32[]{:S(2)}) async-start(bf16[8,64,384]{2,1,0:T(8,128)(2,1)} %bitcast.57), calls=%async_computation.6 | async-start | bytes 786432 | tf_op jit(solution)/shard_map/all_to_all | solution.py:128
  576.4 9.2 %join_columns.1 = (f32[64,11264]{1,0:T(8,128)}, f32[64,1]{1,0:T(8,128)}) custom-call(bf16[8,64,1408]{2,1,0:T(8,128)(2,1)} %all-to-all-done.5.s_ref, bf16[64,11264]{1,0:T(8,128)(2,1)} %w_ref.3, f32[64,1]{1,0:T(8,128)} %copy.50.gain_ref), custom_call_target="tpu_custom_call" | custom-call | flops 99999997952 | bytes 1048576 | tf_op jit(solution)/shard_map/join_columns/pallas_call | solution.py:601
  597.2 16.3 %collective-permute-done.48 = bf16[64,2048]{1,0:T(8,128)(2,1)S(1)} collective-permute-done((bf16[64,2048]{1,0:T(8,128)(2,1)}, bf16[64,2048]{1,0:T(8,128)(2,1)S(1)}, u32[]{:S(2)}, u32[]{:S(2)}) %collective-permute-start.48) | collective-permute-done | bytes 262176 | tf_op jit(solution)/shard_map/ppermute | solution.py:1021
  (278 shorter events, 171.1 us)
Async XLA Ops:
  15.5 74.9 %all-gather.4.cloned.1.call-start = ((), (), s32[]{:S(2)}) async-start(), calls=%async_computation.10 | async-start | bytes 3276800 | tf_op jit(solution)/shard_map/all_gather | solution.py:132
  25.1 30.7 %collective-permute-start.1 = (bf16[256,2048]{1,0:T(8,128)(2,1)}, bf16[256,2048]{1,0:T(8,128)(2,1)}, u32[]{:S(2)}, u32[]{:S(2)}) collective-permute-start(bf16[256,2048]{1,0:T(8,128)(2,1)} %fusion.2.refs_0_), channel_id=1, source_target_pairs={{0,2},{1,5},{2,0},{3,7},{4,6},{5,1},{6,4},{7,3},{8,10},{9,13},{10,... | collective-permute-start | bytes 3145736 | tf_op jit(solution)/shard_map/ppermute | solution.py:54
  34.0 31.7 %collective-permute-start.2 = (bf16[256,2048]{1,0:T(8,128)(2,1)}, bf16[256,2048]{1,0:T(8,128)(2,1)}, u32[]{:S(2)}, u32[]{:S(2)}) collective-permute-start(bf16[256,2048]{1,0:T(8,128)(2,1)} %fusion.2.refs_0_), channel_id=1, source_target_pairs={{0,4},{1,3},{2,6},{3,1},{4,0},{5,7},{6,2},{7,5},{8,12},{9,11},{10,... | collective-permute-start | bytes 3145736 | tf_op jit(solution)/shard_map/ppermute | solution.py:54
  76.7 22.9 %all-to-all-start.1 = ((bf16[8,64,1408]{2,1,0:T(8,128)(2,1)}), bf16[8,64,1408]{2,1,0:T(8,128)(2,1)S(1)}, u32[]{:S(2)}, u32[]{:S(2)}) async-start(bf16[8,64,1408]{2,1,0:T(8,128)(2,1)} %split_columns.1), calls=%async_computation.1 | async-start | bytes 2883584 | tf_op jit(solution)/shard_map/all_to_all | solution.py:128
  83.4 150.8 %all-gather.6.cloned.1.call-start = ((), (), s32[]{:S(2)}) async-start(), calls=%async_computation.11 | async-start | bytes 7208960 | tf_op jit(solution)/shard_map/all_gather | solution.py:132
  100.6 193.8 %all-gather.8.cloned.1.call-start = ((), (), s32[]{:S(2)}) async-start(), calls=%async_computation.12 | async-start | bytes 3604480 | tf_op jit(solution)/shard_map/all_gather | solution.py:132
  101.3 20.8 %collective-permute-start.8 = (bf16[256,2048]{1,0:T(8,128)(2,1)S(1)}, bf16[256,2048]{1,0:T(8,128)(2,1)S(1)}, u32[]{:S(2)}, u32[]{:S(2)}) collective-permute-start(bf16[256,2048]{1,0:T(8,128)(2,1)S(1)} %reshape.131.refs_0_), channel_id=1, source_target_pairs={{0,2},{1,5},{2,0},{3,7},{4,6},{5,1},{6,4},{7,3},{8,10},{9,13},{10,... | collective-permute-start | bytes 3145736 | tf_op jit(solution)/shard_map/ppermute | solution.py:54
  102.5 24.4 %collective-permute-start.9 = (bf16[256,2048]{1,0:T(8,128)(2,1)S(1)}, bf16[256,2048]{1,0:T(8,128)(2,1)}, u32[]{:S(2)}, u32[]{:S(2)}) collective-permute-start(bf16[256,2048]{1,0:T(8,128)(2,1)S(1)} %reshape.131.refs_0_), channel_id=1, source_target_pairs={{0,4},{1,3},{2,6},{3,1},{4,0},{5,7},{6,2},{7,5},{8,12},{9,11},{10,... | collective-permute-start | bytes 3145736 | tf_op jit(solution)/shard_map/ppermute | solution.py:54
  126.9 28.9 %collective-permute-start.10 = (bf16[256,2048]{1,0:T(8,128)(2,1)S(1)}, bf16[256,2048]{1,0:T(8,128)(2,1)}, u32[]{:S(2)}, u32[]{:S(2)}) collective-permute-start(bf16[256,2048]{1,0:T(8,128)(2,1)S(1)} %collective-permute-done.8.refs_1_), channel_id=1, source_target_pairs={{0,4},{1,3},{2,6},{3,1},{4,0},{5,7},{6,2},{7,5},{8,12},{9,11},{10,... | collective-permute-start | bytes 3145736 | tf_op jit(solution)/shard_map/ppermute | solution.py:54
  154.0 20.6 %collective-permute-start.11 = (bf16[256,2048]{1,0:T(8,128)(2,1)S(1)}, bf16[256,2048]{1,0:T(8,128)(2,1)S(1)}, u32[]{:S(2)}, u32[]{:S(2)}) collective-permute-start(bf16[256,2048]{1,0:T(8,128)(2,1)S(1)} %copy-done.7), channel_id=1, source_target_pairs={{0,1},{1,0},{2,3},{3,2},{4,5},{5,4},{6,7},{7,6},{8,9},{9,8},{10,11... | collective-permute-start | bytes 3145736 | tf_op jit(solution)/shard_map/ppermute | solution.py:58
  155.4 20.2 %collective-permute-start.13 = (bf16[256,2048]{1,0:T(8,128)(2,1)}, bf16[256,2048]{1,0:T(8,128)(2,1)S(1)}, u32[]{:S(2)}, u32[]{:S(2)}) collective-permute-start(bf16[256,2048]{1,0:T(8,128)(2,1)} %collective-permute-done.9.refs_2_), channel_id=1, source_target_pairs={{0,1},{1,0},{2,3},{3,2},{4,5},{5,4},{6,7},{7,6},{8,9},{9,8},{10,11... | collective-permute-start | bytes 3145736 | tf_op jit(solution)/shard_map/ppermute | solution.py:58
  155.8 21.7 %collective-permute-start.14 = (bf16[256,2048]{1,0:T(8,128)(2,1)}, bf16[256,2048]{1,0:T(8,128)(2,1)}, u32[]{:S(2)}, u32[]{:S(2)}) collective-permute-start(bf16[256,2048]{1,0:T(8,128)(2,1)} %collective-permute-done.10.refs_3_), channel_id=1, source_target_pairs={{0,1},{1,0},{2,3},{3,2},{4,5},{5,4},{6,7},{7,6},{8,9},{9,8},{10,11... | collective-permute-start | bytes 3145736 | tf_op jit(solution)/shard_map/ppermute | solution.py:58
  188.6 23.1 %collective-permute-start.15 = (bf16[256,2048]{1,0:T(8,128)(2,1)}, bf16[256,2048]{1,0:T(8,128)(2,1)S(1)}, u32[]{:S(2)}, u32[]{:S(2)}) collective-permute-start(bf16[256,2048]{1,0:T(8,128)(2,1)} %get-tuple-element.76.refs_0_), channel_id=1, source_target_pairs={{0,2},{1,5},{2,0},{3,7},{4,6},{5,1},{6,4},{7,3},{8,10},{9,13},{10,... | collective-permute-start | bytes 3145736 | tf_op jit(solution)/shard_map/ppermute | solution.py:54
  189.0 27.8 %collective-permute-start.16 = (bf16[256,2048]{1,0:T(8,128)(2,1)}, bf16[256,2048]{1,0:T(8,128)(2,1)}, u32[]{:S(2)}, u32[]{:S(2)}) collective-permute-start(bf16[256,2048]{1,0:T(8,128)(2,1)} %get-tuple-element.76.refs_0_), channel_id=1, source_target_pairs={{0,4},{1,3},{2,6},{3,1},{4,0},{5,7},{6,2},{7,5},{8,12},{9,11},{10,... | collective-permute-start | bytes 3145736 | tf_op jit(solution)/shard_map/ppermute | solution.py:54
  229.7 270.2 %reduce-scatter.11.cloned.1.call-start = ((), (), s32[]{:S(2)}) async-start(), calls=%async_computation.16 | async-start | bytes 3604480 | tf_op jit(solution)/shard_map/reduce_scatter | solution.py:136
  232.3 26.0 %collective-permute-start.22 = (bf16[256,2048]{1,0:T(8,128)(2,1)S(1)}, bf16[256,2048]{1,0:T(8,128)(2,1)S(1)}, u32[]{:S(2)}, u32[]{:S(2)}) collective-permute-start(bf16[256,2048]{1,0:T(8,128)(2,1)S(1)} %copy-done.11), channel_id=1, source_target_pairs={{0,2},{1,5},{2,0},{3,7},{4,6},{5,1},{6,4},{7,3},{8,10},{9,13},{10,... | collective-permute-start | bytes 3145736 | tf_op jit(solution)/shard_map/ppermute | solution.py:54
  234.0 26.1 %collective-permute-start.23 = (bf16[256,2048]{1,0:T(8,128)(2,1)S(1)}, bf16[256,2048]{1,0:T(8,128)(2,1)}, u32[]{:S(2)}, u32[]{:S(2)}) collective-permute-start(bf16[256,2048]{1,0:T(8,128)(2,1)S(1)} %copy-done.11), channel_id=1, source_target_pairs={{0,4},{1,3},{2,6},{3,1},{4,0},{5,7},{6,2},{7,5},{8,12},{9,11},{10,... | collective-permute-start | bytes 3145736 | tf_op jit(solution)/shard_map/ppermute | solution.py:54
  325.8 195.3 %reduce-scatter.5.cloned.1.call-start = ((), (), s32[]{:S(2)}) async-start(), calls=%async_computation.13 | async-start | bytes 7208960 | tf_op jit(solution)/shard_map/reduce_scatter | solution.py:136
  333.8 33.6 %collective-permute-start.33 = (bf16[512,2048]{1,0:T(8,128)(2,1)}, bf16[512,2048]{1,0:T(8,128)(2,1)S(1)}, u32[]{:S(2)}, u32[]{:S(2)}) collective-permute-start(bf16[512,2048]{1,0:T(8,128)(2,1)} %convert_add_fusion.6), channel_id=1, source_target_pairs={{0,4},{1,3},{2,6},{3,1},{4,0},{5,7},{6,2},{7,5},{8,12},{9,11},{10,... | collective-permute-start | bytes 6291464 | tf_op jit(solution)/shard_map/ppermute | solution.py:54
  347.8 22.9 %collective-permute-start.31 = (bf16[512,2048]{1,0:T(8,128)(2,1)}, bf16[512,2048]{1,0:T(8,128)(2,1)}, u32[]{:S(2)}, u32[]{:S(2)}) collective-permute-start(bf16[512,2048]{1,0:T(8,128)(2,1)} %convolution_convert_fusion.5), channel_id=1, source_target_pairs={{0,1},{1,0},{2,3},{3,2},{4,5},{5,4},{6,7},{7,6},{8,9},{9,8},{10,11... | collective-permute-start | bytes 6291464 | tf_op jit(solution)/shard_map/ppermute | solution.py:58
  351.0 25.9 %collective-permute-start.32 = (bf16[512,2048]{1,0:T(8,128)(2,1)}, bf16[512,2048]{1,0:T(8,128)(2,1)}, u32[]{:S(2)}, u32[]{:S(2)}) collective-permute-start(bf16[512,2048]{1,0:T(8,128)(2,1)} %convolution_convert_fusion.4), channel_id=1, source_target_pairs={{0,1},{1,0},{2,3},{3,2},{4,5},{5,4},{6,7},{7,6},{8,9},{9,8},{10,11... | collective-permute-start | bytes 6291464 | tf_op jit(solution)/shard_map/ppermute | solution.py:58
  367.4 191.7 %reduce-scatter.7.cloned.1.call-start = ((), (), s32[]{:S(2)}) async-start(), calls=%async_computation.14 | async-start | bytes 1966080 | tf_op jit(solution)/shard_map/reduce_scatter | solution.py:136
  416.2 69.6 %collective-permute-start.37 = (bf16[256,2048]{1,0:T(8,128)(2,1)}, bf16[256,2048]{1,0:T(8,128)(2,1)}, u32[]{:S(2)}, u32[]{:S(2)}) collective-permute-start(bf16[256,2048]{1,0:T(8,128)(2,1)} %get-tuple-element.96.refs_0_), channel_id=1, source_target_pairs={{0,2},{1,5},{2,0},{3,7},{4,6},{5,1},{6,4},{7,3},{8,10},{9,13},{10,... | collective-permute-start | bytes 3145736 | tf_op jit(solution)/shard_map/ppermute | solution.py:90
  416.4 69.3 %collective-permute-start.38 = (bf16[256,2048]{1,0:T(8,128)(2,1)}, bf16[256,2048]{1,0:T(8,128)(2,1)}, u32[]{:S(2)}, u32[]{:S(2)}) collective-permute-start(bf16[256,2048]{1,0:T(8,128)(2,1)} %get-tuple-element.96.refs_0_), channel_id=1, source_target_pairs={{0,4},{1,3},{2,6},{3,1},{4,0},{5,7},{6,2},{7,5},{8,12},{9,11},{10,... | collective-permute-start | bytes 3145736 | tf_op jit(solution)/shard_map/ppermute | solution.py:90
  417.3 68.4 %collective-permute-start.39 = (bf16[256,2048]{1,0:T(8,128)(2,1)}, bf16[256,2048]{1,0:T(8,128)(2,1)}, u32[]{:S(2)}, u32[]{:S(2)}) collective-permute-start(bf16[256,2048]{1,0:T(8,128)(2,1)} %get-tuple-element.96.refs_0_), channel_id=1, source_target_pairs={{0,6},{1,7},{2,4},{3,5},{4,2},{5,3},{6,0},{7,1},{8,14},{9,15},{10,... | collective-permute-start | bytes 3145736 | tf_op jit(solution)/shard_map/ppermute | solution.py:90
  418.8 67.8 %collective-permute-start.35 = (bf16[512,2048]{1,0:T(8,128)(2,1)}, bf16[512,2048]{1,0:T(8,128)(2,1)}, u32[]{:S(2)}, u32[]{:S(2)}) collective-permute-start(bf16[512,2048]{1,0:T(8,128)(2,1)} %convert_add_fusion.3), channel_id=1, source_target_pairs={{0,4},{1,3},{2,6},{3,1},{4,0},{5,7},{6,2},{7,5},{8,12},{9,11},{10,... | collective-permute-start | bytes 6291464 | tf_op jit(solution)/shard_map/ppermute | solution.py:54
  492.8 28.3 %collective-permute-start.40 = (bf16[512,2048]{1,0:T(8,128)(2,1)}, bf16[512,2048]{1,0:T(8,128)(2,1)}, u32[]{:S(2)}, u32[]{:S(2)}) collective-permute-start(bf16[512,2048]{1,0:T(8,128)(2,1)} %convolution_convert_fusion.3), channel_id=1, source_target_pairs={{0,1},{1,0},{2,3},{3,2},{4,5},{5,4},{6,7},{7,6},{8,9},{9,8},{10,11... | collective-permute-start | bytes 6291464 | tf_op jit(solution)/shard_map/ppermute | solution.py:58
  498.6 31.8 %collective-permute-start.42 = (bf16[512,2048]{1,0:T(8,128)(2,1)}, bf16[512,2048]{1,0:T(8,128)(2,1)}, u32[]{:S(2)}, u32[]{:S(2)}) collective-permute-start(bf16[512,2048]{1,0:T(8,128)(2,1)} %add_convert_fusion), channel_id=1, source_target_pairs={{0,4},{1,3},{2,6},{3,1},{4,0},{5,7},{6,2},{7,5},{8,12},{9,11},{10,... | collective-permute-start | bytes 6291464 | tf_op jit(solution)/shard_map/ppermute | solution.py:54
  514.3 36.3 %collective-permute-start.36 = (bf16[256,2048]{1,0:T(8,128)(2,1)}, bf16[256,2048]{1,0:T(8,128)(2,1)}, u32[]{:S(2)}, u32[]{:S(2)}) collective-permute-start(bf16[256,2048]{1,0:T(8,128)(2,1)} %slice.185), channel_id=1, source_target_pairs={{0,2},{1,5},{2,0},{3,7},{4,6},{5,1},{6,4},{7,3},{8,10},{9,13},{10,... | collective-permute-start | bytes 3145736 | tf_op jit(solution)/shard_map/ppermute | solution.py:54
  543.8 23.9 %all-to-all-start.5 = ((bf16[8,64,1408]{2,1,0:T(8,128)(2,1)}), bf16[8,64,1408]{2,1,0:T(8,128)(2,1)}, u32[]{:S(2)}, u32[]{:S(2)}) async-start(bf16[8,64,1408]{2,1,0:T(8,128)(2,1)} %bitcast.18), calls=%async_computation.8 | async-start | bytes 2883584 | tf_op jit(solution)/shard_map/all_to_all | solution.py:128
  550.5 41.3 %reduce-scatter.9.cloned.1.call-start = ((), (), s32[]{:S(2)}) async-start(), calls=%async_computation.15 | async-start | bytes 1310720 | tf_op jit(solution)/shard_map/reduce_scatter | solution.py:136
  591.7 21.7 %collective-permute-start.48 = (bf16[64,2048]{1,0:T(8,128)(2,1)}, bf16[64,2048]{1,0:T(8,128)(2,1)S(1)}, u32[]{:S(2)}, u32[]{:S(2)}) collective-permute-start(bf16[64,2048]{1,0:T(8,128)(2,1)} %reduce-scatter.9.cloned.1.call-done), channel_id=1, source_target_pairs={{0,0},{8,1},{16,2},{24,3},{1,4},{9,5},{17,6},{25,7},{2,8},{10,9},{... | collective-permute-start | bytes 786440 | tf_op jit(solution)/shard_map/ppermute | solution.py:1021
  (77 other events, 901.9 us)
Sparse Core Ops, SparseCore 0:
  35.1 55.2 all-gather.3
  100.8 109.4 all-gather.5
  229.8 59.6 all-gather.7
  325.9 56.1 reduce-scatter.10
  384.2 102.2 reduce-scatter.4
  521.3 35.3 reduce-scatter.6
  559.2 32.4 reduce-scatter.8

commit v3 on v0

--- a/solution.py
+++ b/solution.py
@@ -921,14 +921,12 @@
     owner_pairs = [(b, b % n_dp * n_ctx + b // n_dp) for b in range(n_dp * n_ctx)]
     out_own = lax.ppermute(out_weight, ("dp", "ctx"), owner_pairs)
     out_part = gather_dp(out_own)
-    qkv_own = exchange(after(jnp.concatenate([q_cols, kv_cols], axis=2), out_own)).reshape(
-        n_ctx * rows, columns
-    )
+    qkv_own = exchange(jnp.concatenate([q_cols, kv_cols], axis=2)).reshape(n_ctx * rows, columns)
     qkv_part = gather_dp(qkv_own)
 
     hidden_in = block_in.astype(F32)
     rms_one = lax.rsqrt(jnp.mean(hidden_in * hidden_in, axis=-1, keepdims=True) + EPS)
-    one_pieces = gather_slots(after((hidden_in * rms_one).astype(BF), qkv_own), n_ctx)
+    one_pieces = gather_slots(after((hidden_in * rms_one).astype(BF), qkv_own, out_own), n_ctx)
 
     gate_up_cols = split_columns(
         gate_up_weight, after(gain_two, cosine, sine), n_ctx, n_dp, ff_rows
@@ -942,11 +940,12 @@
     queries, keys, values, keys_t, values_t, all_one = project_qkv(
         order, one_pieces, qkv_part, spread_matrix(width), widen_matrix(width), cosine, sine, width, tok
     )
-    out_pieces = gather_slots(out_part, n_ctx)
+    out_direct = gather_direct(out_part, n_ctx)
     attn, slot_attn, attended, lse = attend_forward(
-        slot_of, starts_row, after(queries, gate_up_own), keys, values_t, heads, tok, 0, n_ctx, ()
+        slot_of, starts_row, after(queries, gate_up_own, *out_direct), keys, values_t, heads, tok, 0, n_ctx, ()
     )
     attn_tokens = exchange(attn.reshape(n_ctx, tok, width))
+    out_pieces = gather_rest(out_direct, n_ctx, (queries,), (attn,))
     state, norm_two = project_out(order, attn_tokens, out_pieces, block_in)
 
     two_pieces = gather_slots(norm_two, n_ctx)

time: 628 us -> 619 us (0.986)
  starting transfers between devices: 116 us -> 86.6 us
  blocking collectives: 19.8 us -> 38.5 us
    all_to_all x1 -> x2, blocking collectives: 19.8 us -> 38.5 us  [exchange(): return lax.all_to_all(x, 'ctx', split_axis=0, concat_axis=0, tiled=False)]
    all_to_all x5 -> x4, waiting for transfers between devices: 27.7 us -> 10 us  [exchange(): return lax.all_to_all(x, 'ctx', split_axis=0, concat_axis=0, tiled=False)]
    ppermute x26, starting transfers between devices: 43.7 us -> 30.3 us  [swap_core(): return lax.ppermute(x, 'ctx', [(c, c ^ 1) for c in range(n_ctx)])]
    all_to_all x5 -> x4, starting transfers between devices: 35.7 us -> 22.3 us  [exchange(): return lax.all_to_all(x, 'ctx', split_axis=0, concat_axis=0, tiled=False)]
    all_gather x4, waiting for transfers between devices: 6.11 us -> 18.7 us  [gather_dp(): return lax.all_gather(x, 'dp', axis=0, tiled=True)]
  transfers between devices with their start and end apart: 62 -> 61, of which waited for: 19 -> 18; matrix products, arithmetic and copies ran while one was open for 22% -> 21% of each run, Pallas kernels for 27% -> 28%
where the time goes in v3:
time: 619 us; the launch traced here: 612 us
  Pallas kernels  184 us (30%)
  waiting for transfers between devices  135 us (22%)
  matrix products  99.6 us (16%)
  starting transfers between devices  86.6 us (14%)
  blocking collectives  38.5 us (6%)
  other arithmetic  38.3 us (6%)
  between operations  15.4 us (2%)
  local copies, waits for them, and re-layouts  14.4 us (2%)
    ppermute x18, waiting for transfers between devices, swap_stage(): return lax.ppermute(x, 'ctx', pairs)  79 us
    pallas_call x1, Pallas kernels, attend_backward(): pl.pallas_call(kernel, grid_spec=pltpu.PrefetchScalarGridSpec(num_scalar_...  56 us
    dot_general x8, matrix products, nt(): lax.dot_general(a, b, (((1,), (1,)), ((), ())), preferred_element_type=F32)  43.4 us
    dot_general x4, matrix products, outer_rows(): lax.dot_general(activations, gradients, (((0,), (0,)), ((), ())), preferr...  39.8 us
    all_to_all x2, blocking collectives, exchange(): return lax.all_to_all(x, 'ctx', split_axis=0, concat_axis=0, tiled=False)  38.5 us
    ppermute x26, starting transfers between devices, swap_core(): return lax.ppermute(x, 'ctx', [(c, c ^ 1) for c in range(n_ctx)])  30.3 us
    pallas_call x1, Pallas kernels, attend_forward(): pl.pallas_call(kernel, grid_spec=pltpu.PrefetchScalarGridSpec(num_scalar_...  24.7 us
    pallas_call x1, Pallas kernels, feed_forward(): pl.pallas_call(kernel, grid=(n // 2,), in_specs=any_specs(pieces) + [pl.B...  23.9 us
  transfers between devices with their start and end apart: 61, of which 18 were waited for; matrix products, arithmetic and copies ran while one was open for 21% of the time, Pallas kernels for 28%

profile of v3, /device:TPU:1, one launch (start us, length us, event | category | flops | bytes accessed | tf_op | source)
XLA Modules:
  0.0 611.7 jit_solution(9771224024312774952)
XLA Ops:
  25.1 8.7 %collective-permute-start.1 = (bf16[256,2048]{1,0:T(8,128)(2,1)}, bf16[256,2048]{1,0:T(8,128)(2,1)}, u32[]{:S(2)}, u32[]{:S(2)}) collective-permute-start(bf16[256,2048]{1,0:T(8,128)(2,1)} %fusion.2.refs_0_), channel_id=1, source_target_pairs={{0,2},{1,5},{2,0},{3,7},{4,6},{5,1},{6,4},{7,3},{8,10},{9,13},{10,... | collective-permute-start | bytes 3145736 | tf_op jit(solution)/shard_map/ppermute | solution.py:54
  34.3 20.7 %collective-permute-done.1.refs_1_ = bf16[256,2048]{1,0:T(8,128)(2,1)} collective-permute-done((bf16[256,2048]{1,0:T(8,128)(2,1)}, bf16[256,2048]{1,0:T(8,128)(2,1)}, u32[]{:S(2)}, u32[]{:S(2)}) %collective-permute-start.1) | collective-permute-done | bytes 1048608 | tf_op jit(solution)/shard_map/ppermute | solution.py:54
  61.4 7.0 %collective-permute-start.4 = (bf16[256,2048]{1,0:T(8,128)(2,1)}, bf16[256,2048]{1,0:T(8,128)(2,1)}, u32[]{:S(2)}, u32[]{:S(2)}) collective-permute-start(bf16[256,2048]{1,0:T(8,128)(2,1)} %fusion.2.refs_0_), channel_id=1, source_target_pairs={{0,1},{1,0},{2,3},{3,2},{4,5},{5,4},{6,7},{7,6},{8,9},{9,8},{10,11... | collective-permute-start | bytes 3145736 | tf_op jit(solution)/shard_map/ppermute | solution.py:58
  69.3 5.8 collective-permute-start.7
  85.2 18.1 %all-gather.5.cloned.1.call-done.refs_8_ = bf16[2048,384]{1,0:T(8,128)(2,1)} async-done(((bf16[512,384]{1,0:T(8,128)(2,1)}), bf16[2048,384]{1,0:T(8,128)(2,1)}) %all-gather.5.cloned.1.call-update) | async-done | bytes 1572880 | tf_op jit(solution)/shard_map/all_gather | solution.py:132
  103.3 16.2 %project_qkv.1 = (bf16[2048,256]{1,0:T(8,128)(2,1)}, bf16[2048,256]{1,0:T(8,128)(2,1)}, bf16[2048,256]{1,0:T(8,128)(2,1)}, bf16[64,2048]{1,0:T(8,128)(2,1)}, bf1...) custom-call(s32[8]{0:T(128)} %copy-done.31, bf16[256,2048]{1,0:T(8,128)(2,1)} %fusion.2.refs_0_, ...), custom_call_target="tpu_custom_call" | custom-call | flops 99999997952 | bytes 1048576 | tf_op jit(solution)/shard_map/project_qkv/pallas_call | solution.py:263
  122.0 24.7 %attend_forward.1 = (bf16[2048,256]{1,0:T(8,128)(2,1)}, bf16[2048,256]{1,0:T(8,128)(2,1)}, f32[2048,256]{1,0:T(8,128)}, f32[8,4,256]{2,1,0:T(4,128)}) custom-call(s32[8]{0:T(128)} %select_reduce_fusion.1.slot_ref, s32[1,2048]{1,0:T(1,128)} %bitcast.64, bf16[2048,256]{1,0:T(8,128)(2,1)} %get-tuple-element.56.q_ref, ...), custom_call_target="tpu_custom_call" | custom-call | flops 99999997952 | bytes 1048576 | tf_op jit(solution)/shard_map/attend_forward/pallas_call | solution.py:678
  148.6 18.7 %all_to_all.30.a_ref = bf16[8,256,256]{2,1,0:T(8,128)(2,1)} all-to-all(bf16[8,256,256]{2,1,0:T(8,128)(2,1)} %bitcast.58), channel_id=1, replica_groups=mesh['dp'=4,'ctx'=8] {'ctx'}, dimensions={0} | all-to-all | bytes 2097152 | tf_op jit(solution)/shard_map/all_to_all | solution.py:128
  170.2 11.1 %project_out.1 = (f32[256,2048]{1,0:T(8,128)}, bf16[256,2048]{1,0:T(8,128)(2,1)}) custom-call(s32[8]{0:T(128)} %copy-done.31, bf16[8,256,256]{2,1,0:T(8,128)(2,1)} %all_to_all.30.a_ref, bf16[256,2048]{1,0:T(8,128)(2,1)} %all-gather.7.cloned.1.call-done.refs_0_, bf16[256,2048]{1,0:T(8,128)(2,1)} %copy-done.11, ...), custom_call_target="tpu_custom_call" | custom-call | flops 1048576 | bytes 1048576 | tf_op jit(solution)/shard_map/project_out/pallas_call | solution.py:333
  182.5 22.0 %collective-permute-done.15.refs_1_ = bf16[256,2048]{1,0:T(8,128)(2,1)S(1)} collective-permute-done((bf16[256,2048]{1,0:T(8,128)(2,1)}, bf16[256,2048]{1,0:T(8,128)(2,1)S(1)}, u32[]{:S(2)}, u32[]{:S(2)}) %collective-permute-start.15) | collective-permute-done | bytes 1048608 | tf_op jit(solution)/shard_map/ppermute | solution.py:54
  210.0 8.5 %collective-permute-done.17.refs_3_ = bf16[256,2048]{1,0:T(8,128)(2,1)} collective-permute-done((bf16[256,2048]{1,0:T(8,128)(2,1)S(1)}, bf16[256,2048]{1,0:T(8,128)(2,1)}, u32[]{:S(2)}, u32[]{:S(2)}) %collective-permute-start.17) | collective-permute-done | bytes 1048608 | tf_op jit(solution)/shard_map/ppermute | solution.py:54
  227.5 23.9 %feed_forward.1 = (bf16[2048,704]{1,0:T(8,128)(2,1)}, bf16[2048,1408]{1,0:T(8,128)(2,1)}, bf16[2048,2048]{1,0:T(8,128)(2,1)}) custom-call(bf16[256,2048]{1,0:T(8,128)(2,1)} %get-tuple-element.66.refs_0_, bf16[256,2048]{1,0:T(8,128)(2,1)} %copy-done.41, bf16[256,2048]{1,0:T(8,128)(2,1)} %copy-done.42, bf16[256,2048]{1,0:T(8,128)(2,1)} %collective-permute-done.17.refs_3_, ...), custom_call_target="tpu_custom_call" | custom-call | flops 99999997952 | bytes 1048576 | tf_op jit(solution)/shard_map/feed_forward/pallas_call | solution.py:382
  253.9 11.6 %collective-permute-done.24.refs_3_ = bf16[256,2048]{1,0:T(8,128)(2,1)S(1)} collective-permute-done((bf16[256,2048]{1,0:T(8,128)(2,1)S(1)}, bf16[256,2048]{1,0:T(8,128)(2,1)S(1)}, u32[]{:S(2)}, u32[]{:S(2)}) %collective-permute-start.24) | collective-permute-done | bytes 1048608 | tf_op jit(solution)/shard_map/ppermute | solution.py:54
  269.2 6.5 %lay_out.2.g_ref = bf16[2048,2048]{1,0:T(8,128)(2,1)} custom-call(bf16[256,2048]{1,0:T(8,128)(2,1)} %g_ref.1, bf16[256,2048]{1,0:T(8,128)(2,1)} %copy-done.20, bf16[256,2048]{1,0:T(8,128)(2,1)} %copy-done.21, bf16[256,2048]{1,0:T(8,128)(2,1)} %copy-done.22, bf16[256,2048]{1,0:T(8,128)(2,1)} %copy-done.24, bf16[256,2048]{1,0:T(8,128)(2,1)} %copy-done.25, ...), custom_call_target="tpu_custom_call" | custom-call | flops 1048576 | bytes 1048576 | tf_op jit(solution)/shard_map/lay_out/pallas_call | solution.py:471
  275.7 10.7 %convolution_convert_fusion.1 = bf16[704,2048]{1,0:T(8,128)(2,1)} fusion(bf16[2048,704]{1,0:T(8,128)(2,1)} %get-tuple-element.73, bf16[2048,2048]{1,0:T(8,128)(2,1)} %lay_out.2.g_ref), kind=kOutput, calls=%fused_computation.9 | convolution fusion | flops 5907021824 | bytes 14155776 | tf_op jit(solution)/shard_map/dot_general | solution.py:839
  286.4 15.2 %feed_backward.1 = bf16[2048,1408]{1,0:T(8,128)(2,1)} custom-call(bf16[2048,1408]{1,0:T(8,128)(2,1)} %get-tuple-element.71.factor_ref, bf16[2048,2048]{1,0:T(8,128)(2,1)} %lay_out.2.g_ref, bf16[704,2048]{1,0:T(8,128)(2,1)} %all-gather.11.cloned.1.call-done.w_hbm), custom_call_target="tpu_custom_call" | custom-call | flops 99999997952 | bytes 1048576 | tf_op jit(solution)/shard_map/feed_backward/pallas_call | solution.py:427
  301.6 7.8 %convolution_convert_fusion.7 = bf16[512,2048]{1,0:T(8,128)(2,1)} fusion(bf16[2048,1408]{1,0:T(8,128)(2,1)} %all-gather.9.cloned.1.call-done.refs_8_, bf16[2048,1408]{1,0:T(8,128)(2,1)} %feed_backward.1), kind=kOutput, calls=%fused_computation.15 | convolution fusion | flops 2953838592 | bytes 9306112 | tf_op jit(solution)/shard_map/dot_general | solution.py:27
  309.9 7.8 %convolution_convert_fusion.6 = bf16[512,2048]{1,0:T(8,128)(2,1)} fusion(bf16[2048,1408]{1,0:T(8,128)(2,1)} %all-gather.9.cloned.1.call-done.refs_8_, bf16[2048,1408]{1,0:T(8,128)(2,1)} %feed_backward.1), kind=kOutput, calls=%fused_computation.14 | convolution fusion | flops 2953838592 | bytes 9306112 | tf_op jit(solution)/shard_map/dot_general | solution.py:27
  317.8 8.0 %convert_add_fusion.6 = bf16[512,2048]{1,0:T(8,128)(2,1)} fusion(bf16[512,2048]{1,0:T(8,128)(2,1)S(1)} %collective-permute-done.29, bf16[2048,1408]{1,0:T(8,128)(2,1)} %all-gather.9.cloned.1.call-done.refs_8_, bf16[2048,1408]{1,0:T(8,128)(2,1)} %feed_backward.1), kind=kOutput, calls=%fused_computation.8 | convolution fusion | flops 2955935744 | bytes 11403264 | tf_op jit(solution)/shard_map/dot_general | solution.py:27
  327.1 9.7 %convert_add_fusion.5 = f32[512,2048]{1,0:T(8,128)} fusion(bf16[512,2048]{1,0:T(8,128)(2,1)} %collective-permute-done.30, bf16[2048,1408]{1,0:T(8,128)(2,1)} %all-gather.9.cloned.1.call-done.refs_8_, bf16[2048,1408]{1,0:T(8,128)(2,1)} %feed_backward.1), kind=kOutput, calls=%fused_computation.7 | convolution fusion | flops 2954887168 | bytes 13500416 | tf_op jit(solution)/shard_map/dot_general | solution.py:27
  343.7 15.8 %convolution_convert_fusion = bf16[2048,1408]{1,0:T(8,128)(2,1)} fusion(bf16[2048,2048]{1,0:T(8,128)(2,1)S(1)} %bitcast.72, bf16[2048,1408]{1,0:T(8,128)(2,1)S(1)} %bitcast.70), kind=kOutput, calls=%fused_computation | convolution fusion | flops 11814043648 | bytes 19922944 | tf_op jit(solution)/shard_map/dot_general | solution.py:839
  378.5 10.8 %branch_back.1 = (f32[256,2048]{1,0:T(8,128)}, bf16[256,2048]{1,0:T(8,128)(2,1)}, bf16[8,256,256]{2,1,0:T(8,128)(2,1)}) custom-call(s32[8]{0:T(128)} %copy-done.31, f32[256,2048]{1,0:T(8,128)} %slice_add_fusion.2.d_ref, f32[256,2048]{1,0:T(8,128)} %get-tuple-element.65.state_ref, bf16[256,2048]{1,0:T(8,128)(2,1)} %g_ref.1, ...), custom_call_target="tpu_custom_call" | custom-call | flops 1048576 | bytes 1048576 | tf_op jit(solution)/shard_map/branch_back/pallas_call | solution.py:522
  389.4 19.8 %all_to_all.31 = bf16[8,256,256]{2,1,0:T(8,128)(2,1)} all-to-all(bf16[8,256,256]{2,1,0:T(8,128)(2,1)} %get-tuple-element.77), channel_id=1, replica_groups=mesh['dp'=4,'ctx'=8] {'ctx'}, dimensions={0} | all-to-all | bytes 2097152 | tf_op jit(solution)/shard_map/all_to_all | solution.py:128
  412.8 56.0 %attend_backward.1 = bf16[2048,384]{1,0:T(8,128)(2,1)} custom-call(s32[8]{0:T(128)} %select_reduce_fusion.1.slot_ref, s32[1,2048]{1,0:T(1,128)} %bitcast.65, bf16[2048,256]{1,0:T(8,128)(2,1)} %get-tuple-element.56.q_ref, bf16[2048,256]{1,0:T(8,128)(2,1)} %get-tuple-element.57.k_ref, bf16[64,2048]{1,0:T(8,128)(2,1)} %get-tuple-element.80.kt_ref, ...), custom_call_target="tpu_custom_call" | custom-call | flops 20000000000 | bytes 1048576 | tf_op jit(solution)/shard_map/attend_backward/pallas_call | solution.py:810
  468.9 9.7 %convolution_convert_fusion.8 = bf16[2048,384]{1,0:T(8,128)(2,1)} fusion(bf16[2048,2048]{1,0:T(8,128)(2,1)} %get-tuple-element.84, bf16[2048,384]{1,0:T(8,128)(2,1)} %attend_backward.1), kind=kOutput, calls=%fused_computation.16 | convolution fusion | flops 3222011904 | bytes 11534336 | tf_op jit(solution)/shard_map/dot_general | solution.py:839
  504.9 6.5 %lay_out.3 = bf16[2048,2048]{1,0:T(8,128)(2,1)} custom-call(bf16[256,2048]{1,0:T(8,128)(2,1)} %get-tuple-element.86.refs_0_, bf16[256,2048]{1,0:T(8,128)(2,1)} %collective-permute-done.37.refs_1_, bf16[256,2048]{1,0:T(8,128)(2,1)} %collective-permute-done.38.refs_2_, bf16[256,2048]{1,0:T(8,128)(2,1)} %collective-permute-done.39.refs_3_, ...), custom_call_target="tpu_custom_call" | custom-call | flops 1048576 | bytes 1048576 | tf_op jit(solution)/shard_map/lay_out/pallas_call | solution.py:471
  511.5 11.8 %collective-permute-done.42 = bf16[512,2048]{1,0:T(8,128)(2,1)} collective-permute-done((bf16[512,2048]{1,0:T(8,128)(2,1)}, bf16[512,2048]{1,0:T(8,128)(2,1)}, u32[]{:S(2)}, u32[]{:S(2)}) %collective-permute-start.42) | collective-permute-done | bytes 2097184 | tf_op jit(solution)/shard_map/ppermute | solution.py:54
  536.6 5.8 all-to-all-start.5
  551.6 10.0 %all-to-all-done.5.s_ref = bf16[8,64,1408]{2,1,0:T(8,128)(2,1)} async-done(((bf16[8,64,1408]{2,1,0:T(8,128)(2,1)}), bf16[8,64,1408]{2,1,0:T(8,128)(2,1)}, u32[]{:S(2)}, u32[]{:S(2)}) %all-to-all-start.5) | async-done | bytes 1441824 | tf_op jit(solution)/shard_map/all_to_all | solution.py:128
  561.6 7.7 %all-to-all-start.4 = ((bf16[8,64,384]{2,1,0:T(8,128)(2,1)}), bf16[8,64,384]{2,1,0:T(8,128)(2,1)S(1)}, u32[]{:S(2)}, u32[]{:S(2)}) async-start(bf16[8,64,384]{2,1,0:T(8,128)(2,1)} %bitcast.61), calls=%async_computation.6 | async-start | bytes 786432 | tf_op jit(solution)/shard_map/all_to_all | solution.py:128
  569.3 9.2 %join_columns.1 = (f32[64,11264]{1,0:T(8,128)}, f32[64,1]{1,0:T(8,128)}) custom-call(bf16[8,64,1408]{2,1,0:T(8,128)(2,1)} %all-to-all-done.5.s_ref, bf16[64,11264]{1,0:T(8,128)(2,1)} %w_ref.3, f32[64,1]{1,0:T(8,128)} %copy.50.gain_ref), custom_call_target="tpu_custom_call" | custom-call | flops 99999997952 | bytes 1048576 | tf_op jit(solution)/shard_map/join_columns/pallas_call | solution.py:599
  587.4 16.2 %collective-permute-done.48 = bf16[64,2048]{1,0:T(8,128)(2,1)S(1)} collective-permute-done((bf16[64,2048]{1,0:T(8,128)(2,1)}, bf16[64,2048]{1,0:T(8,128)(2,1)S(1)}, u32[]{:S(2)}, u32[]{:S(2)}) %collective-permute-start.48) | collective-permute-done | bytes 262176 | tf_op jit(solution)/shard_map/ppermute | solution.py:1017
  (282 shorter events, 153.9 us)
Async XLA Ops:
  15.5 63.4 %all-gather.7.cloned.1.call-start = ((), (), s32[]{:S(2)}) async-start(), calls=%async_computation.11 | async-start | bytes 1310720 | tf_op jit(solution)/shard_map/all_gather | solution.py:132
  25.1 29.9 %collective-permute-start.1 = (bf16[256,2048]{1,0:T(8,128)(2,1)}, bf16[256,2048]{1,0:T(8,128)(2,1)}, u32[]{:S(2)}, u32[]{:S(2)}) collective-permute-start(bf16[256,2048]{1,0:T(8,128)(2,1)} %fusion.2.refs_0_), channel_id=1, source_target_pairs={{0,2},{1,5},{2,0},{3,7},{4,6},{5,1},{6,4},{7,3},{8,10},{9,13},{10,... | collective-permute-start | bytes 3145736 | tf_op jit(solution)/shard_map/ppermute | solution.py:54
  33.9 69.5 %all-gather.5.cloned.1.call-start = ((), (), s32[]{:S(2)}) async-start(), calls=%async_computation.10 | async-start | bytes 1966080 | tf_op jit(solution)/shard_map/all_gather | solution.py:132
  34.2 34.3 %collective-permute-start.2 = (bf16[256,2048]{1,0:T(8,128)(2,1)}, bf16[256,2048]{1,0:T(8,128)(2,1)}, u32[]{:S(2)}, u32[]{:S(2)}) collective-permute-start(bf16[256,2048]{1,0:T(8,128)(2,1)} %fusion.2.refs_0_), channel_id=1, source_target_pairs={{0,4},{1,3},{2,6},{3,1},{4,0},{5,7},{6,2},{7,5},{8,12},{9,11},{10,... | collective-permute-start | bytes 3145736 | tf_op jit(solution)/shard_map/ppermute | solution.py:54
  61.4 22.9 %collective-permute-start.4 = (bf16[256,2048]{1,0:T(8,128)(2,1)}, bf16[256,2048]{1,0:T(8,128)(2,1)}, u32[]{:S(2)}, u32[]{:S(2)}) collective-permute-start(bf16[256,2048]{1,0:T(8,128)(2,1)} %fusion.2.refs_0_), channel_id=1, source_target_pairs={{0,1},{1,0},{2,3},{3,2},{4,5},{5,4},{6,7},{7,6},{8,9},{9,8},{10,11... | collective-permute-start | bytes 3145736 | tf_op jit(solution)/shard_map/ppermute | solution.py:58
  69.3 34.1 %collective-permute-start.7 = (bf16[256,2048]{1,0:T(8,128)(2,1)}, bf16[256,2048]{1,0:T(8,128)(2,1)}, u32[]{:S(2)}, u32[]{:S(2)}) collective-permute-start(bf16[256,2048]{1,0:T(8,128)(2,1)} %collective-permute-done.3.refs_3_), channel_id=1, source_target_pairs={{0,1},{1,0},{2,3},{3,2},{4,5},{5,4},{6,7},{7,6},{8,9},{9,8},{10,11... | collective-permute-start | bytes 3145736 | tf_op jit(solution)/shard_map/ppermute | solution.py:58
  79.0 40.6 %collective-permute-start.8 = (bf16[256,2048]{1,0:T(8,128)(2,1)}, bf16[256,2048]{1,0:T(8,128)(2,1)S(1)}, u32[]{:S(2)}, u32[]{:S(2)}) collective-permute-start(bf16[256,2048]{1,0:T(8,128)(2,1)} %all-gather.7.cloned.1.call-done.refs_0_), channel_id=1, source_target_pairs={{0,2},{1,5},{2,0},{3,7},{4,6},{5,1},{6,4},{7,3},{8,10},{9,13},{10,... | collective-permute-start | bytes 3145736 | tf_op jit(solution)/shard_map/ppermute | solution.py:54
  80.7 40.1 %all-to-all-start.1 = ((bf16[8,64,1408]{2,1,0:T(8,128)(2,1)}), bf16[8,64,1408]{2,1,0:T(8,128)(2,1)S(1)}, u32[]{:S(2)}, u32[]{:S(2)}) async-start(bf16[8,64,1408]{2,1,0:T(8,128)(2,1)} %split_columns.1), calls=%async_computation.1 | async-start | bytes 2883584 | tf_op jit(solution)/shard_map/all_to_all | solution.py:128
  84.3 143.2 %all-gather.9.cloned.1.call-start = ((), (), s32[]{:S(2)}) async-start(), calls=%async_computation.12 | async-start | bytes 7208960 | tf_op jit(solution)/shard_map/all_gather | solution.py:132
  84.3 37.7 %collective-permute-start.9 = (bf16[256,2048]{1,0:T(8,128)(2,1)}, bf16[256,2048]{1,0:T(8,128)(2,1)}, u32[]{:S(2)}, u32[]{:S(2)}) collective-permute-start(bf16[256,2048]{1,0:T(8,128)(2,1)} %all-gather.7.cloned.1.call-done.refs_0_), channel_id=1, source_target_pairs={{0,4},{1,3},{2,6},{3,1},{4,0},{5,7},{6,2},{7,5},{8,12},{9,11},{10,... | collective-permute-start | bytes 3145736 | tf_op jit(solution)/shard_map/ppermute | solution.py:54
  119.6 28.9 %collective-permute-start.10 = (bf16[256,2048]{1,0:T(8,128)(2,1)S(1)}, bf16[256,2048]{1,0:T(8,128)(2,1)}, u32[]{:S(2)}, u32[]{:S(2)}) collective-permute-start(bf16[256,2048]{1,0:T(8,128)(2,1)S(1)} %collective-permute-done.8.refs_1_), channel_id=1, source_target_pairs={{0,4},{1,3},{2,6},{3,1},{4,0},{5,7},{6,2},{7,5},{8,12},{9,11},{10,... | collective-permute-start | bytes 3145736 | tf_op jit(solution)/shard_map/ppermute | solution.py:54
  122.0 164.4 %all-gather.11.cloned.1.call-start = ((), (), s32[]{:S(2)}) async-start(), calls=%async_computation.13 | async-start | bytes 3604480 | tf_op jit(solution)/shard_map/all_gather | solution.py:132
  148.5 21.7 %collective-permute-start.14 = (bf16[256,2048]{1,0:T(8,128)(2,1)}, bf16[256,2048]{1,0:T(8,128)(2,1)}, u32[]{:S(2)}, u32[]{:S(2)}) collective-permute-start(bf16[256,2048]{1,0:T(8,128)(2,1)} %collective-permute-done.10.refs_3_), channel_id=1, source_target_pairs={{0,1},{1,0},{2,3},{3,2},{4,5},{5,4},{6,7},{7,6},{8,9},{9,8},{10,11... | collective-permute-start | bytes 3145736 | tf_op jit(solution)/shard_map/ppermute | solution.py:58
  181.3 23.1 %collective-permute-start.15 = (bf16[256,2048]{1,0:T(8,128)(2,1)}, bf16[256,2048]{1,0:T(8,128)(2,1)S(1)}, u32[]{:S(2)}, u32[]{:S(2)}) collective-permute-start(bf16[256,2048]{1,0:T(8,128)(2,1)} %get-tuple-element.66.refs_0_), channel_id=1, source_target_pairs={{0,2},{1,5},{2,0},{3,7},{4,6},{5,1},{6,4},{7,3},{8,10},{9,13},{10,... | collective-permute-start | bytes 3145736 | tf_op jit(solution)/shard_map/ppermute | solution.py:54
  181.6 27.8 %collective-permute-start.16 = (bf16[256,2048]{1,0:T(8,128)(2,1)}, bf16[256,2048]{1,0:T(8,128)(2,1)S(1)}, u32[]{:S(2)}, u32[]{:S(2)}) collective-permute-start(bf16[256,2048]{1,0:T(8,128)(2,1)} %get-tuple-element.66.refs_0_), channel_id=1, source_target_pairs={{0,4},{1,3},{2,6},{3,1},{4,0},{5,7},{6,2},{7,5},{8,12},{9,11},{10,... | collective-permute-start | bytes 3145736 | tf_op jit(solution)/shard_map/ppermute | solution.py:54
  222.4 269.0 %reduce-scatter.11.cloned.1.call-start = ((), (), s32[]{:S(2)}) async-start(), calls=%async_computation.17 | async-start | bytes 3604480 | tf_op jit(solution)/shard_map/reduce_scatter | solution.py:136
  225.0 26.4 %collective-permute-start.22 = (bf16[256,2048]{1,0:T(8,128)(2,1)S(1)}, bf16[256,2048]{1,0:T(8,128)(2,1)S(1)}, u32[]{:S(2)}, u32[]{:S(2)}) collective-permute-start(bf16[256,2048]{1,0:T(8,128)(2,1)S(1)} %copy-done.9), channel_id=1, source_target_pairs={{0,2},{1,5},{2,0},{3,7},{4,6},{5,1},{6,4},{7,3},{8,10},{9,13},{10,... | collective-permute-start | bytes 3145736 | tf_op jit(solution)/shard_map/ppermute | solution.py:54
  226.7 26.7 %collective-permute-start.23 = (bf16[256,2048]{1,0:T(8,128)(2,1)S(1)}, bf16[256,2048]{1,0:T(8,128)(2,1)S(1)}, u32[]{:S(2)}, u32[]{:S(2)}) collective-permute-start(bf16[256,2048]{1,0:T(8,128)(2,1)S(1)} %copy-done.9), channel_id=1, source_target_pairs={{0,4},{1,3},{2,6},{3,1},{4,0},{5,7},{6,2},{7,5},{8,12},{9,11},{10,... | collective-permute-start | bytes 3145736 | tf_op jit(solution)/shard_map/ppermute | solution.py:54
  317.8 193.7 %reduce-scatter.5.cloned.1.call-start = ((), (), s32[]{:S(2)}) async-start(), calls=%async_computation.14 | async-start | bytes 7208960 | tf_op jit(solution)/shard_map/reduce_scatter | solution.py:136
  325.9 33.7 %collective-permute-start.33 = (bf16[512,2048]{1,0:T(8,128)(2,1)}, bf16[512,2048]{1,0:T(8,128)(2,1)S(1)}, u32[]{:S(2)}, u32[]{:S(2)}) collective-permute-start(bf16[512,2048]{1,0:T(8,128)(2,1)} %convert_add_fusion.6), channel_id=1, source_target_pairs={{0,4},{1,3},{2,6},{3,1},{4,0},{5,7},{6,2},{7,5},{8,12},{9,11},{10,... | collective-permute-start | bytes 6291464 | tf_op jit(solution)/shard_map/ppermute | solution.py:54
  339.9 24.1 %collective-permute-start.31 = (bf16[512,2048]{1,0:T(8,128)(2,1)}, bf16[512,2048]{1,0:T(8,128)(2,1)}, u32[]{:S(2)}, u32[]{:S(2)}) collective-permute-start(bf16[512,2048]{1,0:T(8,128)(2,1)} %convolution_convert_fusion.5), channel_id=1, source_target_pairs={{0,1},{1,0},{2,3},{3,2},{4,5},{5,4},{6,7},{7,6},{8,9},{9,8},{10,11... | collective-permute-start | bytes 6291464 | tf_op jit(solution)/shard_map/ppermute | solution.py:58
  343.6 25.8 %collective-permute-start.32 = (bf16[512,2048]{1,0:T(8,128)(2,1)}, bf16[512,2048]{1,0:T(8,128)(2,1)}, u32[]{:S(2)}, u32[]{:S(2)}) collective-permute-start(bf16[512,2048]{1,0:T(8,128)(2,1)} %convolution_convert_fusion.4), channel_id=1, source_target_pairs={{0,1},{1,0},{2,3},{3,2},{4,5},{5,4},{6,7},{7,6},{8,9},{9,8},{10,11... | collective-permute-start | bytes 6291464 | tf_op jit(solution)/shard_map/ppermute | solution.py:58
  359.5 192.0 %reduce-scatter.7.cloned.1.call-start = ((), (), s32[]{:S(2)}) async-start(), calls=%async_computation.15 | async-start | bytes 1966080 | tf_op jit(solution)/shard_map/reduce_scatter | solution.py:136
  409.2 69.4 %collective-permute-start.37 = (bf16[256,2048]{1,0:T(8,128)(2,1)}, bf16[256,2048]{1,0:T(8,128)(2,1)}, u32[]{:S(2)}, u32[]{:S(2)}) collective-permute-start(bf16[256,2048]{1,0:T(8,128)(2,1)} %get-tuple-element.86.refs_0_), channel_id=1, source_target_pairs={{0,2},{1,5},{2,0},{3,7},{4,6},{5,1},{6,4},{7,3},{8,10},{9,13},{10,... | collective-permute-start | bytes 3145736 | tf_op jit(solution)/shard_map/ppermute | solution.py:90
  409.4 69.1 %collective-permute-start.38 = (bf16[256,2048]{1,0:T(8,128)(2,1)}, bf16[256,2048]{1,0:T(8,128)(2,1)}, u32[]{:S(2)}, u32[]{:S(2)}) collective-permute-start(bf16[256,2048]{1,0:T(8,128)(2,1)} %get-tuple-element.86.refs_0_), channel_id=1, source_target_pairs={{0,4},{1,3},{2,6},{3,1},{4,0},{5,7},{6,2},{7,5},{8,12},{9,11},{10,... | collective-permute-start | bytes 3145736 | tf_op jit(solution)/shard_map/ppermute | solution.py:90
  410.3 68.2 %collective-permute-start.39 = (bf16[256,2048]{1,0:T(8,128)(2,1)}, bf16[256,2048]{1,0:T(8,128)(2,1)}, u32[]{:S(2)}, u32[]{:S(2)}) collective-permute-start(bf16[256,2048]{1,0:T(8,128)(2,1)} %get-tuple-element.86.refs_0_), channel_id=1, source_target_pairs={{0,6},{1,7},{2,4},{3,5},{4,2},{5,3},{6,0},{7,1},{8,14},{9,15},{10,... | collective-permute-start | bytes 3145736 | tf_op jit(solution)/shard_map/ppermute | solution.py:90
  411.8 67.8 %collective-permute-start.35 = (bf16[512,2048]{1,0:T(8,128)(2,1)}, bf16[512,2048]{1,0:T(8,128)(2,1)}, u32[]{:S(2)}, u32[]{:S(2)}) collective-permute-start(bf16[512,2048]{1,0:T(8,128)(2,1)} %convert_add_fusion.3), channel_id=1, source_target_pairs={{0,4},{1,3},{2,6},{3,1},{4,0},{5,7},{6,2},{7,5},{8,12},{9,11},{10,... | collective-permute-start | bytes 6291464 | tf_op jit(solution)/shard_map/ppermute | solution.py:54
  484.5 27.1 %collective-permute-start.40 = (bf16[512,2048]{1,0:T(8,128)(2,1)}, bf16[512,2048]{1,0:T(8,128)(2,1)}, u32[]{:S(2)}, u32[]{:S(2)}) collective-permute-start(bf16[512,2048]{1,0:T(8,128)(2,1)} %convolution_convert_fusion.3), channel_id=1, source_target_pairs={{0,1},{1,0},{2,3},{3,2},{4,5},{5,4},{6,7},{7,6},{8,9},{9,8},{10,11... | collective-permute-start | bytes 6291464 | tf_op jit(solution)/shard_map/ppermute | solution.py:58
  490.3 33.0 %collective-permute-start.42 = (bf16[512,2048]{1,0:T(8,128)(2,1)}, bf16[512,2048]{1,0:T(8,128)(2,1)}, u32[]{:S(2)}, u32[]{:S(2)}) collective-permute-start(bf16[512,2048]{1,0:T(8,128)(2,1)} %add_convert_fusion), channel_id=1, source_target_pairs={{0,4},{1,3},{2,6},{3,1},{4,0},{5,7},{6,2},{7,5},{8,12},{9,11},{10,... | collective-permute-start | bytes 6291464 | tf_op jit(solution)/shard_map/ppermute | solution.py:54
  504.7 37.9 %collective-permute-start.36 = (bf16[256,2048]{1,0:T(8,128)(2,1)}, bf16[256,2048]{1,0:T(8,128)(2,1)}, u32[]{:S(2)}, u32[]{:S(2)}) collective-permute-start(bf16[256,2048]{1,0:T(8,128)(2,1)} %slice.167), channel_id=1, source_target_pairs={{0,2},{1,5},{2,0},{3,7},{4,6},{5,1},{6,4},{7,3},{8,10},{9,13},{10,... | collective-permute-start | bytes 3145736 | tf_op jit(solution)/shard_map/ppermute | solution.py:54
  536.6 25.0 %all-to-all-start.5 = ((bf16[8,64,1408]{2,1,0:T(8,128)(2,1)}), bf16[8,64,1408]{2,1,0:T(8,128)(2,1)}, u32[]{:S(2)}, u32[]{:S(2)}) async-start(bf16[8,64,1408]{2,1,0:T(8,128)(2,1)} %bitcast.18), calls=%async_computation.8 | async-start | bytes 2883584 | tf_op jit(solution)/shard_map/all_to_all | solution.py:128
  542.5 39.5 %reduce-scatter.9.cloned.1.call-start = ((), (), s32[]{:S(2)}) async-start(), calls=%async_computation.16 | async-start | bytes 1310720 | tf_op jit(solution)/shard_map/reduce_scatter | solution.py:136
  (80 other events, 1040.5 us)
Sparse Core Ops, SparseCore 0:
  34.0 27.5 all-gather.6
  68.5 34.7 all-gather.4
  122.1 105.3 all-gather.8
  228.9 57.2 all-gather.10
  317.9 54.4 reduce-scatter.10
  374.6 102.3 reduce-scatter.4
  511.7 32.1 reduce-scatter.6
  551.7 30.2 reduce-scatter.8

commit v4 on v3

--- a/solution.py
+++ b/solution.py
@@ -152,7 +152,7 @@
     return buffer[pl.ds(step * count, count)].reshape(count * buffer.shape[1], buffer.shape[2])
 
 
-def keep_pieces(buffer, target, semaphores, count=1):
+def keep_pieces(buffer, target, semaphores):
     step = pl.program_id(0)
     total, tok = buffer.shape[0], buffer.shape[1]
 
@@ -160,10 +160,9 @@
         rows = pl.ds(pl.multiple_of(at * tok, tok), tok)
         return pltpu.make_async_copy(buffer.at[at], target.at[rows], semaphores.at[at])
 
-    for i in range(count):
-        copy(step * count + i).start()
-
-    @pl.when(step == total // count - 1)
+    copy(step).start()
+
+    @pl.when(step == total - 1)
     def _():
         for i in range(total):
             copy(i).wait()
@@ -365,10 +364,10 @@
 
     def kernel(*refs):
         parts = refs[:n]
-        w_hbm, hidden_ref, factor_ref, all_hbm, buffer, semaphores, keep_semaphores, w_ref, w_semaphores = refs[n:]
+        w_hbm, hidden_ref, factor_ref, all_ref, buffer, semaphores, w_ref, w_semaphores = refs[n:]
         fetch_rows(w_hbm, w_ref, w_semaphores)
         x = fetch_piece(parts, buffer, semaphores, 2)
-        keep_pieces(buffer, all_hbm, keep_semaphores, 2)
+        all_ref[...] = x
         both = nn(x, w_ref[...])
         gate = both[:, :ff]
         up = both[:, ff:]
@@ -386,11 +385,10 @@
         out_specs=[
             pl.BlockSpec((tok, ff), rows),
             pl.BlockSpec((tok, 2 * ff), rows),
-            pl.BlockSpec(memory_space=pltpu.HBM),
+            pl.BlockSpec((tok, D), rows),
         ],
         scratch_shapes=[
             pltpu.VMEM((n, tok // 2, D), BF),
-            pltpu.SemaphoreType.DMA((n,)),
             pltpu.SemaphoreType.DMA((n,)),
             pltpu.VMEM(weight.shape, BF),
             pltpu.SemaphoreType.DMA((chunks(D),)),
@@ -985,7 +983,7 @@
         keys,
         keys_t,
         values,
-        grad_attn,
+        after(grad_attn, down_sums),
         attended,
         lse,
         cosine,
@@ -994,8 +992,8 @@
         heads,
         tok,
     )
-    qkv_terms = outer_rows(all_one, grad_mixed)
-    qkv_sums = scatter_dp(after(qkv_terms, gate_up_sums))
+    qkv_terms = outer_rows(all_one, after(grad_mixed, gate_up_sums))
+    qkv_sums = scatter_dp(qkv_terms)
     one_pairs, _ = scatter_pairs(
         lambda lo, hi: nt(
             rows_of(after(grad_mixed, qkv_terms, hidden_arrived, *branch_here), lo, hi), qkv_part

time: 619 us -> 637 us (1.029)
  waiting for transfers between devices: 135 us -> 149 us
  starting transfers between devices: 86.6 us -> 98.3 us
    ppermute x18, waiting for transfers between devices: 79 us -> 97.7 us  [swap_stage(): return lax.ppermute(x, 'ctx', pairs)]
    ppermute x26, starting transfers between devices: 30.3 us -> 42.6 us  [swap_core(): return lax.ppermute(x, 'ctx', [(c, c ^ 1) for c in range(n_ctx)])]
  transfers between devices with their start and end apart: 61 -> 61, of which waited for: 18 -> 17; matrix products, arithmetic and copies ran while one was open for 21% -> 20% of each run, Pallas kernels for 28% -> 26%
where the time goes in v4:
time: 637 us; the launch traced here: 629 us
  Pallas kernels  180 us (28%)
  waiting for transfers between devices  149 us (23%)
  starting transfers between devices  98.3 us (15%)
  matrix products  94.2 us (15%)
  blocking collectives  39.4 us (6%)
  other arithmetic  36.5 us (6%)
  local copies, waits for them, and re-layouts  15.4 us (2%)
  between operations  15.4 us (2%)
    ppermute x18, waiting for transfers between devices, swap_stage(): return lax.ppermute(x, 'ctx', pairs)  97.7 us
    pallas_call x1, Pallas kernels, attend_backward(): pl.pallas_call(kernel, grid_spec=pltpu.PrefetchScalarGridSpec(num_scalar_...  55.8 us
    ppermute x26, starting transfers between devices, swap_core(): return lax.ppermute(x, 'ctx', [(c, c ^ 1) for c in range(n_ctx)])  42.6 us
    dot_general x4, matrix products, outer_rows(): lax.dot_general(activations, gradients, (((0,), (0,)), ((), ())), preferr...  42.2 us
    dot_general x8, matrix products, nt(): lax.dot_general(a, b, (((1,), (1,)), ((), ())), preferred_element_type=F32)  40.3 us
    all_to_all x2, blocking collectives, exchange(): return lax.all_to_all(x, 'ctx', split_axis=0, concat_axis=0, tiled=False)  39.4 us
    pallas_call x1, Pallas kernels, attend_forward(): pl.pallas_call(kernel, grid_spec=pltpu.PrefetchScalarGridSpec(num_scalar_...  24.8 us
    ppermute x18, starting transfers between devices, swap_stage(): return lax.ppermute(x, 'ctx', pairs)  23.3 us
  transfers between devices with their start and end apart: 61, of which 17 were waited for; matrix products, arithmetic and copies ran while one was open for 20% of the time, Pallas kernels for 26%

profile of v4, /device:TPU:1, one launch (start us, length us, event | category | flops | bytes accessed | tf_op | source)
XLA Modules:
  0.0 629.1 jit_solution(17722907196109182505)
XLA Ops:
  25.1 8.7 %collective-permute-start.1 = (bf16[256,2048]{1,0:T(8,128)(2,1)}, bf16[256,2048]{1,0:T(8,128)(2,1)}, u32[]{:S(2)}, u32[]{:S(2)}) collective-permute-start(bf16[256,2048]{1,0:T(8,128)(2,1)} %fusion.2.refs_0_), channel_id=1, source_target_pairs={{0,2},{1,5},{2,0},{3,7},{4,6},{5,1},{6,4},{7,3},{8,10},{9,13},{10,... | collective-permute-start | bytes 3145736 | tf_op jit(solution)/shard_map/ppermute | solution.py:54
  34.3 20.7 %collective-permute-done.1.refs_1_ = bf16[256,2048]{1,0:T(8,128)(2,1)} collective-permute-done((bf16[256,2048]{1,0:T(8,128)(2,1)}, bf16[256,2048]{1,0:T(8,128)(2,1)}, u32[]{:S(2)}, u32[]{:S(2)}) %collective-permute-start.1) | collective-permute-done | bytes 1048608 | tf_op jit(solution)/shard_map/ppermute | solution.py:54
  61.4 7.0 %collective-permute-start.4 = (bf16[256,2048]{1,0:T(8,128)(2,1)}, bf16[256,2048]{1,0:T(8,128)(2,1)}, u32[]{:S(2)}, u32[]{:S(2)}) collective-permute-start(bf16[256,2048]{1,0:T(8,128)(2,1)} %fusion.2.refs_0_), channel_id=1, source_target_pairs={{0,1},{1,0},{2,3},{3,2},{4,5},{5,4},{6,7},{7,6},{8,9},{9,8},{10,11... | collective-permute-start | bytes 3145736 | tf_op jit(solution)/shard_map/ppermute | solution.py:58
  85.2 18.1 %all-gather.5.cloned.1.call-done.refs_8_ = bf16[2048,384]{1,0:T(8,128)(2,1)} async-done(((bf16[512,384]{1,0:T(8,128)(2,1)}), bf16[2048,384]{1,0:T(8,128)(2,1)}) %all-gather.5.cloned.1.call-update) | async-done | bytes 1572880 | tf_op jit(solution)/shard_map/all_gather | solution.py:132
  103.4 16.2 %project_qkv.1 = (bf16[2048,256]{1,0:T(8,128)(2,1)}, bf16[2048,256]{1,0:T(8,128)(2,1)}, bf16[2048,256]{1,0:T(8,128)(2,1)}, bf16[64,2048]{1,0:T(8,128)(2,1)}, bf1...) custom-call(s32[8]{0:T(128)} %copy-done.27, bf16[256,2048]{1,0:T(8,128)(2,1)} %fusion.2.refs_0_, ...), custom_call_target="tpu_custom_call" | custom-call | flops 99999997952 | bytes 1048576 | tf_op jit(solution)/shard_map/project_qkv/pallas_call | solution.py:262
  122.1 24.8 %attend_forward.1 = (bf16[2048,256]{1,0:T(8,128)(2,1)}, bf16[2048,256]{1,0:T(8,128)(2,1)}, f32[2048,256]{1,0:T(8,128)}, f32[8,4,256]{2,1,0:T(4,128)}) custom-call(s32[8]{0:T(128)} %select_reduce_fusion.1.slot_ref, s32[1,2048]{1,0:T(1,128)} %bitcast.65, bf16[2048,256]{1,0:T(8,128)(2,1)} %get-tuple-element.57.q_ref, ...), custom_call_target="tpu_custom_call" | custom-call | flops 99999997952 | bytes 1048576 | tf_op jit(solution)/shard_map/attend_forward/pallas_call | solution.py:676
  148.6 18.7 %all_to_all.30.a_ref = bf16[8,256,256]{2,1,0:T(8,128)(2,1)} all-to-all(bf16[8,256,256]{2,1,0:T(8,128)(2,1)} %bitcast.59), channel_id=1, replica_groups=mesh['dp'=4,'ctx'=8] {'ctx'}, dimensions={0} | all-to-all | bytes 2097152 | tf_op jit(solution)/shard_map/all_to_all | solution.py:128
  170.2 11.1 %project_out.1 = (f32[256,2048]{1,0:T(8,128)}, bf16[256,2048]{1,0:T(8,128)(2,1)}) custom-call(s32[8]{0:T(128)} %copy-done.27, bf16[8,256,256]{2,1,0:T(8,128)(2,1)} %all_to_all.30.a_ref, bf16[256,2048]{1,0:T(8,128)(2,1)} %all-gather.7.cloned.1.call-done.refs_0_, bf16[256,2048]{1,0:T(8,128)(2,1)} %copy-done.9, ...), custom_call_target="tpu_custom_call" | custom-call | flops 1048576 | bytes 1048576 | tf_op jit(solution)/shard_map/project_out/pallas_call | solution.py:332
  182.5 22.0 %collective-permute-done.15.refs_1_ = bf16[256,2048]{1,0:T(8,128)(2,1)S(1)} collective-permute-done((bf16[256,2048]{1,0:T(8,128)(2,1)}, bf16[256,2048]{1,0:T(8,128)(2,1)S(1)}, u32[]{:S(2)}, u32[]{:S(2)}) %collective-permute-start.15) | collective-permute-done | bytes 1048608 | tf_op jit(solution)/shard_map/ppermute | solution.py:54
  209.9 8.5 %collective-permute-done.17.refs_3_ = bf16[256,2048]{1,0:T(8,128)(2,1)} collective-permute-done((bf16[256,2048]{1,0:T(8,128)(2,1)S(1)}, bf16[256,2048]{1,0:T(8,128)(2,1)}, u32[]{:S(2)}, u32[]{:S(2)}) %collective-permute-start.17) | collective-permute-done | bytes 1048608 | tf_op jit(solution)/shard_map/ppermute | solution.py:54
  227.4 22.1 %feed_forward.1 = (bf16[2048,704]{1,0:T(8,128)(2,1)}, bf16[2048,1408]{1,0:T(8,128)(2,1)}, bf16[2048,2048]{1,0:T(8,128)(2,1)}) custom-call(bf16[256,2048]{1,0:T(8,128)(2,1)} %get-tuple-element.67.refs_0_, bf16[256,2048]{1,0:T(8,128)(2,1)} %copy-done.36, bf16[256,2048]{1,0:T(8,128)(2,1)} %copy-done.37, bf16[256,2048]{1,0:T(8,128)(2,1)} %collective-permute-done.17.refs_3_, ...), custom_call_target="tpu_custom_call" | custom-call | flops 99999997952 | bytes 1048576 | tf_op jit(solution)/shard_map/feed_forward/pallas_call | solution.py:381
  253.1 10.6 %collective-permute-done.24.refs_3_ = bf16[256,2048]{1,0:T(8,128)(2,1)S(1)} collective-permute-done((bf16[256,2048]{1,0:T(8,128)(2,1)S(1)}, bf16[256,2048]{1,0:T(8,128)(2,1)S(1)}, u32[]{:S(2)}, u32[]{:S(2)}) %collective-permute-start.24) | collective-permute-done | bytes 1048608 | tf_op jit(solution)/shard_map/ppermute | solution.py:54
  267.8 6.5 %lay_out.2.g_ref = bf16[2048,2048]{1,0:T(8,128)(2,1)} custom-call(bf16[256,2048]{1,0:T(8,128)(2,1)} %g_ref.1, bf16[256,2048]{1,0:T(8,128)(2,1)} %copy-done.17, bf16[256,2048]{1,0:T(8,128)(2,1)} %copy-done.18, bf16[256,2048]{1,0:T(8,128)(2,1)} %copy-done.19, bf16[256,2048]{1,0:T(8,128)(2,1)} %copy-done.20, bf16[256,2048]{1,0:T(8,128)(2,1)} %copy-done.21, ...), custom_call_target="tpu_custom_call" | custom-call | flops 1048576 | bytes 1048576 | tf_op jit(solution)/shard_map/lay_out/pallas_call | solution.py:469
  274.3 10.7 %convolution_convert_fusion.1 = bf16[704,2048]{1,0:T(8,128)(2,1)} fusion(bf16[2048,704]{1,0:T(8,128)(2,1)} %get-tuple-element.74, bf16[2048,2048]{1,0:T(8,128)(2,1)} %lay_out.2.g_ref), kind=kOutput, calls=%fused_computation.9 | convolution fusion | flops 5907021824 | bytes 14155776 | tf_op jit(solution)/shard_map/dot_general | solution.py:837
  286.1 14.8 %feed_backward.1 = bf16[2048,1408]{1,0:T(8,128)(2,1)} custom-call(bf16[2048,1408]{1,0:T(8,128)(2,1)} %get-tuple-element.72.factor_ref, bf16[2048,2048]{1,0:T(8,128)(2,1)} %lay_out.2.g_ref, bf16[704,2048]{1,0:T(8,128)(2,1)} %all-gather.11.cloned.1.call-done.w_hbm), custom_call_target="tpu_custom_call" | custom-call | flops 99999997952 | bytes 1048576 | tf_op jit(solution)/shard_map/feed_backward/pallas_call | solution.py:425
  300.9 7.8 %convolution_convert_fusion.7 = bf16[512,2048]{1,0:T(8,128)(2,1)} fusion(bf16[2048,1408]{1,0:T(8,128)(2,1)} %all-gather.9.cloned.1.call-done.refs_8_, bf16[2048,1408]{1,0:T(8,128)(2,1)} %feed_backward.1), kind=kOutput, calls=%fused_computation.15 | convolution fusion | flops 2953838592 | bytes 9306112 | tf_op jit(solution)/shard_map/dot_general | solution.py:27
  310.0 6.7 %convolution_convert_fusion.6 = bf16[512,2048]{1,0:T(8,128)(2,1)S(1)} fusion(bf16[2048,1408]{1,0:T(8,128)(2,1)} %all-gather.9.cloned.1.call-done.refs_8_, bf16[2048,1408]{1,0:T(8,128)(2,1)} %feed_backward.1), kind=kOutput, calls=%fused_computation.14 | convolution fusion | flops 2953838592 | bytes 9306112 | tf_op jit(solution)/shard_map/dot_general | solution.py:27
  316.8 8.0 %convert_add_fusion.6 = bf16[512,2048]{1,0:T(8,128)(2,1)} fusion(bf16[512,2048]{1,0:T(8,128)(2,1)S(1)} %collective-permute-done.29, bf16[2048,1408]{1,0:T(8,128)(2,1)} %all-gather.9.cloned.1.call-done.refs_8_, bf16[2048,1408]{1,0:T(8,128)(2,1)} %feed_backward.1), kind=kOutput, calls=%fused_computation.8 | convolution fusion | flops 2955935744 | bytes 11403264 | tf_op jit(solution)/shard_map/dot_general | solution.py:27
  329.9 15.0 %convolution_convert_fusion = bf16[2048,1408]{1,0:T(8,128)(2,1)} fusion(bf16[2048,2048]{1,0:T(8,128)(2,1)S(1)} %bitcast.75, bf16[2048,1408]{1,0:T(8,128)(2,1)S(1)} %bitcast.73), kind=kOutput, calls=%fused_computation | convolution fusion | flops 11814043648 | bytes 19922944 | tf_op jit(solution)/shard_map/dot_general | solution.py:837
  352.3 18.3 %collective-permute-done.33 = bf16[512,2048]{1,0:T(8,128)(2,1)S(1)} collective-permute-done((bf16[512,2048]{1,0:T(8,128)(2,1)}, bf16[512,2048]{1,0:T(8,128)(2,1)S(1)}, u32[]{:S(2)}, u32[]{:S(2)}) %collective-permute-start.33) | collective-permute-done | bytes 2097184 | tf_op jit(solution)/shard_map/ppermute | solution.py:54
  387.5 10.2 %branch_back.1 = (f32[256,2048]{1,0:T(8,128)}, bf16[256,2048]{1,0:T(8,128)(2,1)}, bf16[8,256,256]{2,1,0:T(8,128)(2,1)}) custom-call(s32[8]{0:T(128)} %copy-done.27, f32[256,2048]{1,0:T(8,128)} %slice_add_fusion.2.d_ref, f32[256,2048]{1,0:T(8,128)} %get-tuple-element.66.state_ref, bf16[256,2048]{1,0:T(8,128)(2,1)} %g_ref.1, ...), custom_call_target="tpu_custom_call" | custom-call | flops 1048576 | bytes 1048576 | tf_op jit(solution)/shard_map/branch_back/pallas_call | solution.py:520
  397.7 20.7 %all_to_all.31 = bf16[8,256,256]{2,1,0:T(8,128)(2,1)} all-to-all(bf16[8,256,256]{2,1,0:T(8,128)(2,1)} %get-tuple-element.78), channel_id=1, replica_groups=mesh['dp'=4,'ctx'=8] {'ctx'}, dimensions={0} | all-to-all | bytes 2097152 | tf_op jit(solution)/shard_map/all_to_all | solution.py:128
  423.8 55.8 %attend_backward.1 = bf16[2048,384]{1,0:T(8,128)(2,1)} custom-call(s32[8]{0:T(128)} %select_reduce_fusion.1.slot_ref, s32[1,2048]{1,0:T(1,128)} %bitcast.66, bf16[2048,256]{1,0:T(8,128)(2,1)} %get-tuple-element.57.q_ref, bf16[2048,256]{1,0:T(8,128)(2,1)} %get-tuple-element.58.k_ref, bf16[64,2048]{1,0:T(8,128)(2,1)} %get-tuple-element.81.kt_ref, ...), custom_call_target="tpu_custom_call" | custom-call | flops 20000000000 | bytes 1048576 | tf_op jit(solution)/shard_map/attend_backward/pallas_call | solution.py:808
  479.7 10.5 %collective-permute-start.46 = (bf16[256,2048]{1,0:T(8,128)(2,1)}, bf16[256,2048]{1,0:T(8,128)(2,1)}, u32[]{:S(2)}, u32[]{:S(2)}) collective-permute-start(bf16[256,2048]{1,0:T(8,128)(2,1)} %collective-permute-done.38.refs_2_), channel_id=1, source_target_pairs={{0,1},{1,0},{2,3},{3,2},{4,5},{5,4},{6,7},{7,6},{8,9},{9,8},{10,11... | collective-permute-start | bytes 3145736 | tf_op jit(solution)/shard_map/ppermute | solution.py:58
  496.1 9.8 %convolution_convert_fusion.8 = bf16[2048,384]{1,0:T(8,128)(2,1)} fusion(bf16[2048,2048]{1,0:T(8,128)(2,1)} %get-tuple-element.86, bf16[2048,384]{1,0:T(8,128)(2,1)} %attend_backward.1), kind=kOutput, calls=%fused_computation.16 | convolution fusion | flops 3222011904 | bytes 11534336 | tf_op jit(solution)/shard_map/dot_general | solution.py:837
  512.9 6.5 %lay_out.3 = bf16[2048,2048]{1,0:T(8,128)(2,1)} custom-call(bf16[256,2048]{1,0:T(8,128)(2,1)} %get-tuple-element.89.refs_0_, bf16[256,2048]{1,0:T(8,128)(2,1)} %collective-permute-done.37.refs_1_, bf16[256,2048]{1,0:T(8,128)(2,1)} %collective-permute-done.38.refs_2_, bf16[256,2048]{1,0:T(8,128)(2,1)} %collective-permute-done.39.refs_3_, ...), custom_call_target="tpu_custom_call" | custom-call | flops 1048576 | bytes 1048576 | tf_op jit(solution)/shard_map/lay_out/pallas_call | solution.py:469
  534.4 6.8 %convolution_convert_fusion.9 = bf16[256,2048]{1,0:T(8,128)(2,1)} fusion(bf16[2048,256]{1,0:T(8,128)(2,1)S(1)} %copy-done.13, bf16[2048,2048]{1,0:T(8,128)(2,1)} %lay_out.3), kind=kOutput, calls=%fused_computation.22 | convolution fusion | flops 2148007936 | bytes 10485760 | tf_op jit(solution)/shard_map/dot_general | solution.py:837
  547.1 7.4 %all-to-all-start.4 = ((bf16[8,64,384]{2,1,0:T(8,128)(2,1)}), bf16[8,64,384]{2,1,0:T(8,128)(2,1)S(1)}, u32[]{:S(2)}, u32[]{:S(2)}) async-start(bf16[8,64,384]{2,1,0:T(8,128)(2,1)} %bitcast.62), calls=%async_computation.7 | async-start | bytes 786432 | tf_op jit(solution)/shard_map/all_to_all | solution.py:128
  554.5 9.2 %join_columns.1 = (f32[64,11264]{1,0:T(8,128)}, f32[64,1]{1,0:T(8,128)}) custom-call(bf16[8,64,1408]{2,1,0:T(8,128)(2,1)} %all-to-all-done.5.s_ref, bf16[64,11264]{1,0:T(8,128)(2,1)} %w_ref.3, f32[64,1]{1,0:T(8,128)} %copy.50.gain_ref), custom_call_target="tpu_custom_call" | custom-call | flops 99999997952 | bytes 1048576 | tf_op jit(solution)/shard_map/join_columns/pallas_call | solution.py:597
  565.1 10.8 %all-to-all-done.4 = bf16[8,64,384]{2,1,0:T(8,128)(2,1)S(1)} async-done(((bf16[8,64,384]{2,1,0:T(8,128)(2,1)}), bf16[8,64,384]{2,1,0:T(8,128)(2,1)S(1)}, u32[]{:S(2)}, u32[]{:S(2)}) %all-to-all-start.4) | async-done | bytes 393248 | tf_op jit(solution)/shard_map/all_to_all | solution.py:128
  585.8 11.4 %collective-permute-done.43 = bf16[256,2048]{1,0:T(8,128)(2,1)S(1)} collective-permute-done((bf16[256,2048]{1,0:T(8,128)(2,1)}, bf16[256,2048]{1,0:T(8,128)(2,1)S(1)}, u32[]{:S(2)}, u32[]{:S(2)}) %collective-permute-start.43) | collective-permute-done | bytes 1048608 | tf_op jit(solution)/shard_map/ppermute | solution.py:54
  608.0 13.0 %collective-permute-done.48 = bf16[64,2048]{1,0:T(8,128)(2,1)S(1)} collective-permute-done((bf16[64,2048]{1,0:T(8,128)(2,1)}, bf16[64,2048]{1,0:T(8,128)(2,1)S(1)}, u32[]{:S(2)}, u32[]{:S(2)}) %collective-permute-start.48) | collective-permute-done | bytes 262176 | tf_op jit(solution)/shard_map/ppermute | solution.py:1015
  (275 shorter events, 165.1 us)
Async XLA Ops:
  15.5 63.4 %all-gather.7.cloned.1.call-start = ((), (), s32[]{:S(2)}) async-start(), calls=%async_computation.11 | async-start | bytes 1310720 | tf_op jit(solution)/shard_map/all_gather | solution.py:132
  25.1 29.9 %collective-permute-start.1 = (bf16[256,2048]{1,0:T(8,128)(2,1)}, bf16[256,2048]{1,0:T(8,128)(2,1)}, u32[]{:S(2)}, u32[]{:S(2)}) collective-permute-start(bf16[256,2048]{1,0:T(8,128)(2,1)} %fusion.2.refs_0_), channel_id=1, source_target_pairs={{0,2},{1,5},{2,0},{3,7},{4,6},{5,1},{6,4},{7,3},{8,10},{9,13},{10,... | collective-permute-start | bytes 3145736 | tf_op jit(solution)/shard_map/ppermute | solution.py:54
  33.9 69.5 %all-gather.5.cloned.1.call-start = ((), (), s32[]{:S(2)}) async-start(), calls=%async_computation.10 | async-start | bytes 1966080 | tf_op jit(solution)/shard_map/all_gather | solution.py:132
  34.2 34.3 %collective-permute-start.2 = (bf16[256,2048]{1,0:T(8,128)(2,1)}, bf16[256,2048]{1,0:T(8,128)(2,1)}, u32[]{:S(2)}, u32[]{:S(2)}) collective-permute-start(bf16[256,2048]{1,0:T(8,128)(2,1)} %fusion.2.refs_0_), channel_id=1, source_target_pairs={{0,4},{1,3},{2,6},{3,1},{4,0},{5,7},{6,2},{7,5},{8,12},{9,11},{10,... | collective-permute-start | bytes 3145736 | tf_op jit(solution)/shard_map/ppermute | solution.py:54
  69.3 34.1 %collective-permute-start.7 = (bf16[256,2048]{1,0:T(8,128)(2,1)}, bf16[256,2048]{1,0:T(8,128)(2,1)}, u32[]{:S(2)}, u32[]{:S(2)}) collective-permute-start(bf16[256,2048]{1,0:T(8,128)(2,1)} %collective-permute-done.3.refs_3_), channel_id=1, source_target_pairs={{0,1},{1,0},{2,3},{3,2},{4,5},{5,4},{6,7},{7,6},{8,9},{9,8},{10,11... | collective-permute-start | bytes 3145736 | tf_op jit(solution)/shard_map/ppermute | solution.py:58
  79.0 40.6 %collective-permute-start.8 = (bf16[256,2048]{1,0:T(8,128)(2,1)}, bf16[256,2048]{1,0:T(8,128)(2,1)S(1)}, u32[]{:S(2)}, u32[]{:S(2)}) collective-permute-start(bf16[256,2048]{1,0:T(8,128)(2,1)} %all-gather.7.cloned.1.call-done.refs_0_), channel_id=1, source_target_pairs={{0,2},{1,5},{2,0},{3,7},{4,6},{5,1},{6,4},{7,3},{8,10},{9,13},{10,... | collective-permute-start | bytes 3145736 | tf_op jit(solution)/shard_map/ppermute | solution.py:54
  80.7 40.2 %all-to-all-start.1 = ((bf16[8,64,1408]{2,1,0:T(8,128)(2,1)}), bf16[8,64,1408]{2,1,0:T(8,128)(2,1)S(1)}, u32[]{:S(2)}, u32[]{:S(2)}) async-start(bf16[8,64,1408]{2,1,0:T(8,128)(2,1)} %split_columns.1), calls=%async_computation.1 | async-start | bytes 2883584 | tf_op jit(solution)/shard_map/all_to_all | solution.py:128
  84.3 143.2 %all-gather.9.cloned.1.call-start = ((), (), s32[]{:S(2)}) async-start(), calls=%async_computation.12 | async-start | bytes 7208960 | tf_op jit(solution)/shard_map/all_gather | solution.py:132
  84.3 37.7 %collective-permute-start.9 = (bf16[256,2048]{1,0:T(8,128)(2,1)}, bf16[256,2048]{1,0:T(8,128)(2,1)}, u32[]{:S(2)}, u32[]{:S(2)}) collective-permute-start(bf16[256,2048]{1,0:T(8,128)(2,1)} %all-gather.7.cloned.1.call-done.refs_0_), channel_id=1, source_target_pairs={{0,4},{1,3},{2,6},{3,1},{4,0},{5,7},{6,2},{7,5},{8,12},{9,11},{10,... | collective-permute-start | bytes 3145736 | tf_op jit(solution)/shard_map/ppermute | solution.py:54
  119.6 28.9 %collective-permute-start.10 = (bf16[256,2048]{1,0:T(8,128)(2,1)S(1)}, bf16[256,2048]{1,0:T(8,128)(2,1)}, u32[]{:S(2)}, u32[]{:S(2)}) collective-permute-start(bf16[256,2048]{1,0:T(8,128)(2,1)S(1)} %collective-permute-done.8.refs_1_), channel_id=1, source_target_pairs={{0,4},{1,3},{2,6},{3,1},{4,0},{5,7},{6,2},{7,5},{8,12},{9,11},{10,... | collective-permute-start | bytes 3145736 | tf_op jit(solution)/shard_map/ppermute | solution.py:54
  122.0 164.1 %all-gather.11.cloned.1.call-start = ((), (), s32[]{:S(2)}) async-start(), calls=%async_computation.13 | async-start | bytes 3604480 | tf_op jit(solution)/shard_map/all_gather | solution.py:132
  181.6 27.8 %collective-permute-start.16 = (bf16[256,2048]{1,0:T(8,128)(2,1)}, bf16[256,2048]{1,0:T(8,128)(2,1)S(1)}, u32[]{:S(2)}, u32[]{:S(2)}) collective-permute-start(bf16[256,2048]{1,0:T(8,128)(2,1)} %get-tuple-element.67.refs_0_), channel_id=1, source_target_pairs={{0,4},{1,3},{2,6},{3,1},{4,0},{5,7},{6,2},{7,5},{8,12},{9,11},{10,... | collective-permute-start | bytes 3145736 | tf_op jit(solution)/shard_map/ppermute | solution.py:54
  222.3 201.5 %reduce-scatter.5.cloned.1.call-start = ((), (), s32[]{:S(2)}) async-start(), calls=%async_computation.14 | async-start | bytes 3604480 | tf_op jit(solution)/shard_map/reduce_scatter | solution.py:136
  224.9 24.6 %collective-permute-start.22 = (bf16[256,2048]{1,0:T(8,128)(2,1)S(1)}, bf16[256,2048]{1,0:T(8,128)(2,1)S(1)}, u32[]{:S(2)}, u32[]{:S(2)}) collective-permute-start(bf16[256,2048]{1,0:T(8,128)(2,1)S(1)} %copy-done.7), channel_id=1, source_target_pairs={{0,2},{1,5},{2,0},{3,7},{4,6},{5,1},{6,4},{7,3},{8,10},{9,13},{10,... | collective-permute-start | bytes 3145736 | tf_op jit(solution)/shard_map/ppermute | solution.py:54
  226.7 25.9 %collective-permute-start.23 = (bf16[256,2048]{1,0:T(8,128)(2,1)S(1)}, bf16[256,2048]{1,0:T(8,128)(2,1)S(1)}, u32[]{:S(2)}, u32[]{:S(2)}) collective-permute-start(bf16[256,2048]{1,0:T(8,128)(2,1)S(1)} %copy-done.7), channel_id=1, source_target_pairs={{0,4},{1,3},{2,6},{3,1},{4,0},{5,7},{6,2},{7,5},{8,12},{9,11},{10,... | collective-permute-start | bytes 3145736 | tf_op jit(solution)/shard_map/ppermute | solution.py:54
  309.5 186.6 %reduce-scatter.7.cloned.1.call-start = ((), (), s32[]{:S(2)}) async-start(), calls=%async_computation.15 | async-start | bytes 7208960 | tf_op jit(solution)/shard_map/reduce_scatter | solution.py:136
  344.9 202.2 %reduce-scatter.9.cloned.1.call-start = ((), (), s32[]{:S(2)}) async-start(), calls=%async_computation.16 | async-start | bytes 1966080 | tf_op jit(solution)/shard_map/reduce_scatter | solution.py:136
  345.1 25.5 %collective-permute-start.33 = (bf16[512,2048]{1,0:T(8,128)(2,1)}, bf16[512,2048]{1,0:T(8,128)(2,1)S(1)}, u32[]{:S(2)}, u32[]{:S(2)}) collective-permute-start(bf16[512,2048]{1,0:T(8,128)(2,1)} %convert_add_fusion.6), channel_id=1, source_target_pairs={{0,4},{1,3},{2,6},{3,1},{4,0},{5,7},{6,2},{7,5},{8,12},{9,11},{10,... | collective-permute-start | bytes 6291464 | tf_op jit(solution)/shard_map/ppermute | solution.py:54
  352.2 24.5 %collective-permute-start.32 = (bf16[512,2048]{1,0:T(8,128)(2,1)S(1)}, bf16[512,2048]{1,0:T(8,128)(2,1)S(1)}, u32[]{:S(2)}, u32[]{:S(2)}) collective-permute-start(bf16[512,2048]{1,0:T(8,128)(2,1)S(1)} %convolution_convert_fusion.4), channel_id=1, source_target_pairs={{0,1},{1,0},{2,3},{3,2},{4,5},{5,4},{6,7},{7,6},{8,9},{9,8},{10,11... | collective-permute-start | bytes 6291464 | tf_op jit(solution)/shard_map/ppermute | solution.py:58
  418.4 71.9 %collective-permute-start.35 = (bf16[512,2048]{1,0:T(8,128)(2,1)}, bf16[512,2048]{1,0:T(8,128)(2,1)S(1)}, u32[]{:S(2)}, u32[]{:S(2)}) collective-permute-start(bf16[512,2048]{1,0:T(8,128)(2,1)} %convert_add_fusion.3), channel_id=1, source_target_pairs={{0,4},{1,3},{2,6},{3,1},{4,0},{5,7},{6,2},{7,5},{8,12},{9,11},{10,... | collective-permute-start | bytes 6291464 | tf_op jit(solution)/shard_map/ppermute | solution.py:54
  419.4 60.2 %collective-permute-start.37 = (bf16[256,2048]{1,0:T(8,128)(2,1)}, bf16[256,2048]{1,0:T(8,128)(2,1)}, u32[]{:S(2)}, u32[]{:S(2)}) collective-permute-start(bf16[256,2048]{1,0:T(8,128)(2,1)} %get-tuple-element.89.refs_0_), channel_id=1, source_target_pairs={{0,2},{1,5},{2,0},{3,7},{4,6},{5,1},{6,4},{7,3},{8,10},{9,13},{10,... | collective-permute-start | bytes 3145736 | tf_op jit(solution)/shard_map/ppermute | solution.py:90
  419.6 60.2 %collective-permute-start.38 = (bf16[256,2048]{1,0:T(8,128)(2,1)}, bf16[256,2048]{1,0:T(8,128)(2,1)}, u32[]{:S(2)}, u32[]{:S(2)}) collective-permute-start(bf16[256,2048]{1,0:T(8,128)(2,1)} %get-tuple-element.89.refs_0_), channel_id=1, source_target_pairs={{0,4},{1,3},{2,6},{3,1},{4,0},{5,7},{6,2},{7,5},{8,12},{9,11},{10,... | collective-permute-start | bytes 3145736 | tf_op jit(solution)/shard_map/ppermute | solution.py:90
  420.1 70.1 %collective-permute-start.39 = (bf16[256,2048]{1,0:T(8,128)(2,1)}, bf16[256,2048]{1,0:T(8,128)(2,1)}, u32[]{:S(2)}, u32[]{:S(2)}) collective-permute-start(bf16[256,2048]{1,0:T(8,128)(2,1)} %get-tuple-element.89.refs_0_), channel_id=1, source_target_pairs={{0,6},{1,7},{2,4},{3,5},{4,2},{5,3},{6,0},{7,1},{8,14},{9,15},{10,... | collective-permute-start | bytes 3145736 | tf_op jit(solution)/shard_map/ppermute | solution.py:90
  422.1 86.5 %collective-permute-start.44 = (bf16[256,2048]{1,0:T(8,128)(2,1)}, bf16[256,2048]{1,0:T(8,128)(2,1)}, u32[]{:S(2)}, u32[]{:S(2)}) collective-permute-start(bf16[256,2048]{1,0:T(8,128)(2,1)} %get-tuple-element.89.refs_0_), channel_id=1, source_target_pairs={{0,1},{1,0},{2,3},{3,2},{4,5},{5,4},{6,7},{7,6},{8,9},{9,8},{10,11... | collective-permute-start | bytes 3145736 | tf_op jit(solution)/shard_map/ppermute | solution.py:58
  479.6 33.2 %collective-permute-start.45 = (bf16[256,2048]{1,0:T(8,128)(2,1)}, bf16[256,2048]{1,0:T(8,128)(2,1)}, u32[]{:S(2)}, u32[]{:S(2)}) collective-permute-start(bf16[256,2048]{1,0:T(8,128)(2,1)} %collective-permute-done.37.refs_1_), channel_id=1, source_target_pairs={{0,1},{1,0},{2,3},{3,2},{4,5},{5,4},{6,7},{7,6},{8,9},{9,8},{10,11... | collective-permute-start | bytes 3145736 | tf_op jit(solution)/shard_map/ppermute | solution.py:58
  479.7 33.1 %collective-permute-start.46 = (bf16[256,2048]{1,0:T(8,128)(2,1)}, bf16[256,2048]{1,0:T(8,128)(2,1)}, u32[]{:S(2)}, u32[]{:S(2)}) collective-permute-start(bf16[256,2048]{1,0:T(8,128)(2,1)} %collective-permute-done.38.refs_2_), channel_id=1, source_target_pairs={{0,1},{1,0},{2,3},{3,2},{4,5},{5,4},{6,7},{7,6},{8,9},{9,8},{10,11... | collective-permute-start | bytes 3145736 | tf_op jit(solution)/shard_map/ppermute | solution.py:58
  496.1 23.3 %collective-permute-start.36 = (bf16[256,2048]{1,0:T(8,128)(2,1)}, bf16[256,2048]{1,0:T(8,128)(2,1)}, u32[]{:S(2)}, u32[]{:S(2)}) collective-permute-start(bf16[256,2048]{1,0:T(8,128)(2,1)} %slice.167), channel_id=1, source_target_pairs={{0,2},{1,5},{2,0},{3,7},{4,6},{5,1},{6,4},{7,3},{8,10},{9,13},{10,... | collective-permute-start | bytes 3145736 | tf_op jit(solution)/shard_map/ppermute | solution.py:54
  508.6 32.6 %collective-permute-start.41 = (bf16[512,2048]{1,0:T(8,128)(2,1)}, bf16[512,2048]{1,0:T(8,128)(2,1)}, u32[]{:S(2)}, u32[]{:S(2)}) collective-permute-start(bf16[512,2048]{1,0:T(8,128)(2,1)} %convolution_convert_fusion.2), channel_id=1, source_target_pairs={{0,1},{1,0},{2,3},{3,2},{4,5},{5,4},{6,7},{7,6},{8,9},{9,8},{10,11... | collective-permute-start | bytes 6291464 | tf_op jit(solution)/shard_map/ppermute | solution.py:58
  526.0 50.1 %collective-permute-start.40 = (bf16[512,2048]{1,0:T(8,128)(2,1)}, bf16[512,2048]{1,0:T(8,128)(2,1)}, u32[]{:S(2)}, u32[]{:S(2)}) collective-permute-start(bf16[512,2048]{1,0:T(8,128)(2,1)} %convolution_convert_fusion.3), channel_id=1, source_target_pairs={{0,1},{1,0},{2,3},{3,2},{4,5},{5,4},{6,7},{7,6},{8,9},{9,8},{10,11... | collective-permute-start | bytes 6291464 | tf_op jit(solution)/shard_map/ppermute | solution.py:58
  545.3 30.8 %collective-permute-start.42 = (bf16[512,2048]{1,0:T(8,128)(2,1)}, bf16[512,2048]{1,0:T(8,128)(2,1)S(1)}, u32[]{:S(2)}, u32[]{:S(2)}) collective-permute-start(bf16[512,2048]{1,0:T(8,128)(2,1)} %add_convert_fusion), channel_id=1, source_target_pairs={{0,4},{1,3},{2,6},{3,1},{4,0},{5,7},{6,2},{7,5},{8,12},{9,11},{10,... | collective-permute-start | bytes 6291464 | tf_op jit(solution)/shard_map/ppermute | solution.py:54
  547.1 28.9 %all-to-all-start.4 = ((bf16[8,64,384]{2,1,0:T(8,128)(2,1)}), bf16[8,64,384]{2,1,0:T(8,128)(2,1)S(1)}, u32[]{:S(2)}, u32[]{:S(2)}) async-start(bf16[8,64,384]{2,1,0:T(8,128)(2,1)} %bitcast.62), calls=%async_computation.7 | async-start | bytes 786432 | tf_op jit(solution)/shard_map/all_to_all | solution.py:128
  554.5 44.9 %reduce-scatter.11.cloned.1.call-start = ((), (), s32[]{:S(2)}) async-start(), calls=%async_computation.17 | async-start | bytes 1310720 | tf_op jit(solution)/shard_map/reduce_scatter | solution.py:136
  (76 other events, 1094.4 us)
Sparse Core Ops, SparseCore 0:
  34.0 27.5 all-gather.6
  68.5 34.7 all-gather.4
  122.1 105.2 all-gather.8
  228.9 57.2 all-gather.10
  309.6 54.1 reduce-scatter.4
  366.0 102.3 reduce-scatter.6
  506.0 33.3 reduce-scatter.8
  565.2 25.6 reduce-scatter.10

commit v5 on v4

--- a/solution.py
+++ b/solution.py
@@ -983,7 +983,7 @@
         keys,
         keys_t,
         values,
-        after(grad_attn, down_sums),
+        grad_attn,
         attended,
         lse,
         cosine,
@@ -992,8 +992,8 @@
         heads,
         tok,
     )
-    qkv_terms = outer_rows(all_one, after(grad_mixed, gate_up_sums))
-    qkv_sums = scatter_dp(qkv_terms)
+    qkv_terms = outer_rows(all_one, grad_mixed)
+    qkv_sums = scatter_dp(after(qkv_terms, gate_up_sums))
     one_pairs, _ = scatter_pairs(
         lambda lo, hi: nt(
             rows_of(after(grad_mixed, qkv_terms, hidden_arrived, *branch_here), lo, hi), qkv_part

time: 637 us -> 619 us (0.972)
  waiting for transfers between devices: 149 us -> 136 us
  starting transfers between devices: 98.3 us -> 88.3 us
    ppermute x18, waiting for transfers between devices: 97.7 us -> 78 us  [swap_stage(): return lax.ppermute(x, 'ctx', pairs)]
    ppermute x26, starting transfers between devices: 42.6 us -> 32.1 us  [swap_core(): return lax.ppermute(x, 'ctx', [(c, c ^ 1) for c in range(n_ctx)])]
  transfers between devices with their start and end apart: 61 -> 61, of which waited for: 17 -> 19; matrix products, arithmetic and copies ran while one was open for 20% -> 21% of each run, Pallas kernels for 26% -> 27%
where the time goes in v5:
time: 619 us; the launch traced here: 612 us
  Pallas kernels  182 us (29%)
  waiting for transfers between devices  136 us (22%)
  matrix products  99.7 us (16%)
  starting transfers between devices  88.3 us (14%)
  blocking collectives  38.5 us (6%)
  other arithmetic  38.3 us (6%)
  between operations  15.4 us (2%)
  local copies, waits for them, and re-layouts  14.4 us (2%)
    ppermute x18, waiting for transfers between devices, swap_stage(): return lax.ppermute(x, 'ctx', pairs)  78 us
    pallas_call x1, Pallas kernels, attend_backward(): pl.pallas_call(kernel, grid_spec=pltpu.PrefetchScalarGridSpec(num_scalar_...  56 us
    dot_general x8, matrix products, nt(): lax.dot_general(a, b, (((1,), (1,)), ((), ())), preferred_element_type=F32)  43.3 us
    dot_general x4, matrix products, outer_rows(): lax.dot_general(activations, gradients, (((0,), (0,)), ((), ())), preferr...  39.8 us
    all_to_all x2, blocking collectives, exchange(): return lax.all_to_all(x, 'ctx', split_axis=0, concat_axis=0, tiled=False)  38.5 us
    ppermute x26, starting transfers between devices, swap_core(): return lax.ppermute(x, 'ctx', [(c, c ^ 1) for c in range(n_ctx)])  32.1 us
    pallas_call x1, Pallas kernels, attend_forward(): pl.pallas_call(kernel, grid_spec=pltpu.PrefetchScalarGridSpec(num_scalar_...  24.7 us
    ppermute x18, starting transfers between devices, swap_stage(): return lax.ppermute(x, 'ctx', pairs)  23.9 us
  transfers between devices with their start and end apart: 61, of which 19 were waited for; matrix products, arithmetic and copies ran while one was open for 21% of the time, Pallas kernels for 27%

profile of v5, /device:TPU:1, one launch (start us, length us, event | category | flops | bytes accessed | tf_op | source)
XLA Modules:
  0.0 611.7 jit_solution(13787762109590214585)
XLA Ops:
  25.1 8.7 %collective-permute-start.1 = (bf16[256,2048]{1,0:T(8,128)(2,1)}, bf16[256,2048]{1,0:T(8,128)(2,1)}, u32[]{:S(2)}, u32[]{:S(2)}) collective-permute-start(bf16[256,2048]{1,0:T(8,128)(2,1)} %fusion.2.refs_0_), channel_id=1, source_target_pairs={{0,2},{1,5},{2,0},{3,7},{4,6},{5,1},{6,4},{7,3},{8,10},{9,13},{10,... | collective-permute-start | bytes 3145736 | tf_op jit(solution)/shard_map/ppermute | solution.py:54
  34.3 20.7 %collective-permute-done.1.refs_1_ = bf16[256,2048]{1,0:T(8,128)(2,1)} collective-permute-done((bf16[256,2048]{1,0:T(8,128)(2,1)}, bf16[256,2048]{1,0:T(8,128)(2,1)}, u32[]{:S(2)}, u32[]{:S(2)}) %collective-permute-start.1) | collective-permute-done | bytes 1048608 | tf_op jit(solution)/shard_map/ppermute | solution.py:54
  61.4 7.0 %collective-permute-start.4 = (bf16[256,2048]{1,0:T(8,128)(2,1)}, bf16[256,2048]{1,0:T(8,128)(2,1)}, u32[]{:S(2)}, u32[]{:S(2)}) collective-permute-start(bf16[256,2048]{1,0:T(8,128)(2,1)} %fusion.2.refs_0_), channel_id=1, source_target_pairs={{0,1},{1,0},{2,3},{3,2},{4,5},{5,4},{6,7},{7,6},{8,9},{9,8},{10,11... | collective-permute-start | bytes 3145736 | tf_op jit(solution)/shard_map/ppermute | solution.py:58
  69.3 5.8 collective-permute-start.7
  85.2 18.1 %all-gather.5.cloned.1.call-done.refs_8_ = bf16[2048,384]{1,0:T(8,128)(2,1)} async-done(((bf16[512,384]{1,0:T(8,128)(2,1)}), bf16[2048,384]{1,0:T(8,128)(2,1)}) %all-gather.5.cloned.1.call-update) | async-done | bytes 1572880 | tf_op jit(solution)/shard_map/all_gather | solution.py:132
  103.3 16.2 %project_qkv.1 = (bf16[2048,256]{1,0:T(8,128)(2,1)}, bf16[2048,256]{1,0:T(8,128)(2,1)}, bf16[2048,256]{1,0:T(8,128)(2,1)}, bf16[64,2048]{1,0:T(8,128)(2,1)}, bf1...) custom-call(s32[8]{0:T(128)} %copy-done.31, bf16[256,2048]{1,0:T(8,128)(2,1)} %fusion.2.refs_0_, ...), custom_call_target="tpu_custom_call" | custom-call | flops 99999997952 | bytes 1048576 | tf_op jit(solution)/shard_map/project_qkv/pallas_call | solution.py:262
  122.0 24.7 %attend_forward.1 = (bf16[2048,256]{1,0:T(8,128)(2,1)}, bf16[2048,256]{1,0:T(8,128)(2,1)}, f32[2048,256]{1,0:T(8,128)}, f32[8,4,256]{2,1,0:T(4,128)}) custom-call(s32[8]{0:T(128)} %select_reduce_fusion.1.slot_ref, s32[1,2048]{1,0:T(1,128)} %bitcast.64, bf16[2048,256]{1,0:T(8,128)(2,1)} %get-tuple-element.56.q_ref, ...), custom_call_target="tpu_custom_call" | custom-call | flops 99999997952 | bytes 1048576 | tf_op jit(solution)/shard_map/attend_forward/pallas_call | solution.py:676
  148.6 18.7 %all_to_all.30.a_ref = bf16[8,256,256]{2,1,0:T(8,128)(2,1)} all-to-all(bf16[8,256,256]{2,1,0:T(8,128)(2,1)} %bitcast.58), channel_id=1, replica_groups=mesh['dp'=4,'ctx'=8] {'ctx'}, dimensions={0} | all-to-all | bytes 2097152 | tf_op jit(solution)/shard_map/all_to_all | solution.py:128
  170.2 11.1 %project_out.1 = (f32[256,2048]{1,0:T(8,128)}, bf16[256,2048]{1,0:T(8,128)(2,1)}) custom-call(s32[8]{0:T(128)} %copy-done.31, bf16[8,256,256]{2,1,0:T(8,128)(2,1)} %all_to_all.30.a_ref, bf16[256,2048]{1,0:T(8,128)(2,1)} %all-gather.7.cloned.1.call-done.refs_0_, bf16[256,2048]{1,0:T(8,128)(2,1)} %copy-done.11, ...), custom_call_target="tpu_custom_call" | custom-call | flops 1048576 | bytes 1048576 | tf_op jit(solution)/shard_map/project_out/pallas_call | solution.py:332
  182.5 22.0 %collective-permute-done.15.refs_1_ = bf16[256,2048]{1,0:T(8,128)(2,1)S(1)} collective-permute-done((bf16[256,2048]{1,0:T(8,128)(2,1)}, bf16[256,2048]{1,0:T(8,128)(2,1)S(1)}, u32[]{:S(2)}, u32[]{:S(2)}) %collective-permute-start.15) | collective-permute-done | bytes 1048608 | tf_op jit(solution)/shard_map/ppermute | solution.py:54
  210.0 8.5 %collective-permute-done.17.refs_3_ = bf16[256,2048]{1,0:T(8,128)(2,1)} collective-permute-done((bf16[256,2048]{1,0:T(8,128)(2,1)S(1)}, bf16[256,2048]{1,0:T(8,128)(2,1)}, u32[]{:S(2)}, u32[]{:S(2)}) %collective-permute-start.17) | collective-permute-done | bytes 1048608 | tf_op jit(solution)/shard_map/ppermute | solution.py:54
  227.5 22.1 %feed_forward.1 = (bf16[2048,704]{1,0:T(8,128)(2,1)}, bf16[2048,1408]{1,0:T(8,128)(2,1)}, bf16[2048,2048]{1,0:T(8,128)(2,1)}) custom-call(bf16[256,2048]{1,0:T(8,128)(2,1)} %get-tuple-element.66.refs_0_, bf16[256,2048]{1,0:T(8,128)(2,1)} %copy-done.41, bf16[256,2048]{1,0:T(8,128)(2,1)} %copy-done.42, bf16[256,2048]{1,0:T(8,128)(2,1)} %collective-permute-done.17.refs_3_, ...), custom_call_target="tpu_custom_call" | custom-call | flops 99999997952 | bytes 1048576 | tf_op jit(solution)/shard_map/feed_forward/pallas_call | solution.py:381
  253.1 10.6 %collective-permute-done.24.refs_3_ = bf16[256,2048]{1,0:T(8,128)(2,1)S(1)} collective-permute-done((bf16[256,2048]{1,0:T(8,128)(2,1)S(1)}, bf16[256,2048]{1,0:T(8,128)(2,1)S(1)}, u32[]{:S(2)}, u32[]{:S(2)}) %collective-permute-start.24) | collective-permute-done | bytes 1048608 | tf_op jit(solution)/shard_map/ppermute | solution.py:54
  267.8 6.5 %lay_out.2.g_ref = bf16[2048,2048]{1,0:T(8,128)(2,1)} custom-call(bf16[256,2048]{1,0:T(8,128)(2,1)} %g_ref.1, bf16[256,2048]{1,0:T(8,128)(2,1)} %copy-done.20, bf16[256,2048]{1,0:T(8,128)(2,1)} %copy-done.21, bf16[256,2048]{1,0:T(8,128)(2,1)} %copy-done.22, bf16[256,2048]{1,0:T(8,128)(2,1)} %copy-done.24, bf16[256,2048]{1,0:T(8,128)(2,1)} %copy-done.25, ...), custom_call_target="tpu_custom_call" | custom-call | flops 1048576 | bytes 1048576 | tf_op jit(solution)/shard_map/lay_out/pallas_call | solution.py:469
  274.4 10.7 %convolution_convert_fusion.1 = bf16[704,2048]{1,0:T(8,128)(2,1)} fusion(bf16[2048,704]{1,0:T(8,128)(2,1)} %get-tuple-element.73, bf16[2048,2048]{1,0:T(8,128)(2,1)} %lay_out.2.g_ref), kind=kOutput, calls=%fused_computation.9 | convolution fusion | flops 5907021824 | bytes 14155776 | tf_op jit(solution)/shard_map/dot_general | solution.py:837
  286.1 15.2 %feed_backward.1 = bf16[2048,1408]{1,0:T(8,128)(2,1)} custom-call(bf16[2048,1408]{1,0:T(8,128)(2,1)} %get-tuple-element.71.factor_ref, bf16[2048,2048]{1,0:T(8,128)(2,1)} %lay_out.2.g_ref, bf16[704,2048]{1,0:T(8,128)(2,1)} %all-gather.11.cloned.1.call-done.w_hbm), custom_call_target="tpu_custom_call" | custom-call | flops 99999997952 | bytes 1048576 | tf_op jit(solution)/shard_map/feed_backward/pallas_call | solution.py:425
  301.3 7.8 %convolution_convert_fusion.7 = bf16[512,2048]{1,0:T(8,128)(2,1)} fusion(bf16[2048,1408]{1,0:T(8,128)(2,1)} %all-gather.9.cloned.1.call-done.refs_8_, bf16[2048,1408]{1,0:T(8,128)(2,1)} %feed_backward.1), kind=kOutput, calls=%fused_computation.15 | convolution fusion | flops 2953838592 | bytes 9306112 | tf_op jit(solution)/shard_map/dot_general | solution.py:27
  309.9 7.8 %convolution_convert_fusion.6 = bf16[512,2048]{1,0:T(8,128)(2,1)} fusion(bf16[2048,1408]{1,0:T(8,128)(2,1)} %all-gather.9.cloned.1.call-done.refs_8_, bf16[2048,1408]{1,0:T(8,128)(2,1)} %feed_backward.1), kind=kOutput, calls=%fused_computation.14 | convolution fusion | flops 2953838592 | bytes 9306112 | tf_op jit(solution)/shard_map/dot_general | solution.py:27
  317.8 8.0 %convert_add_fusion.6 = bf16[512,2048]{1,0:T(8,128)(2,1)} fusion(bf16[512,2048]{1,0:T(8,128)(2,1)S(1)} %collective-permute-done.29, bf16[2048,1408]{1,0:T(8,128)(2,1)} %all-gather.9.cloned.1.call-done.refs_8_, bf16[2048,1408]{1,0:T(8,128)(2,1)} %feed_backward.1), kind=kOutput, calls=%fused_computation.8 | convolution fusion | flops 2955935744 | bytes 11403264 | tf_op jit(solution)/shard_map/dot_general | solution.py:27
  327.0 9.7 %convert_add_fusion.5 = f32[512,2048]{1,0:T(8,128)} fusion(bf16[512,2048]{1,0:T(8,128)(2,1)} %collective-permute-done.30, bf16[2048,1408]{1,0:T(8,128)(2,1)} %all-gather.9.cloned.1.call-done.refs_8_, bf16[2048,1408]{1,0:T(8,128)(2,1)} %feed_backward.1), kind=kOutput, calls=%fused_computation.7 | convolution fusion | flops 2954887168 | bytes 13500416 | tf_op jit(solution)/shard_map/dot_general | solution.py:27
  343.7 15.8 %convolution_convert_fusion = bf16[2048,1408]{1,0:T(8,128)(2,1)} fusion(bf16[2048,2048]{1,0:T(8,128)(2,1)S(1)} %bitcast.72, bf16[2048,1408]{1,0:T(8,128)(2,1)S(1)} %bitcast.70), kind=kOutput, calls=%fused_computation | convolution fusion | flops 11814043648 | bytes 19922944 | tf_op jit(solution)/shard_map/dot_general | solution.py:837
  378.5 10.8 %branch_back.1 = (f32[256,2048]{1,0:T(8,128)}, bf16[256,2048]{1,0:T(8,128)(2,1)}, bf16[8,256,256]{2,1,0:T(8,128)(2,1)}) custom-call(s32[8]{0:T(128)} %copy-done.31, f32[256,2048]{1,0:T(8,128)} %slice_add_fusion.2.d_ref, f32[256,2048]{1,0:T(8,128)} %get-tuple-element.65.state_ref, bf16[256,2048]{1,0:T(8,128)(2,1)} %g_ref.1, ...), custom_call_target="tpu_custom_call" | custom-call | flops 1048576 | bytes 1048576 | tf_op jit(solution)/shard_map/branch_back/pallas_call | solution.py:520
  389.4 19.8 %all_to_all.31 = bf16[8,256,256]{2,1,0:T(8,128)(2,1)} all-to-all(bf16[8,256,256]{2,1,0:T(8,128)(2,1)} %get-tuple-element.77), channel_id=1, replica_groups=mesh['dp'=4,'ctx'=8] {'ctx'}, dimensions={0} | all-to-all | bytes 2097152 | tf_op jit(solution)/shard_map/all_to_all | solution.py:128
  412.8 56.0 %attend_backward.1 = bf16[2048,384]{1,0:T(8,128)(2,1)} custom-call(s32[8]{0:T(128)} %select_reduce_fusion.1.slot_ref, s32[1,2048]{1,0:T(1,128)} %bitcast.65, bf16[2048,256]{1,0:T(8,128)(2,1)} %get-tuple-element.56.q_ref, bf16[2048,256]{1,0:T(8,128)(2,1)} %get-tuple-element.57.k_ref, bf16[64,2048]{1,0:T(8,128)(2,1)} %get-tuple-element.80.kt_ref, ...), custom_call_target="tpu_custom_call" | custom-call | flops 20000000000 | bytes 1048576 | tf_op jit(solution)/shard_map/attend_backward/pallas_call | solution.py:808
  468.9 9.7 %convolution_convert_fusion.8 = bf16[2048,384]{1,0:T(8,128)(2,1)} fusion(bf16[2048,2048]{1,0:T(8,128)(2,1)} %get-tuple-element.84, bf16[2048,384]{1,0:T(8,128)(2,1)} %attend_backward.1), kind=kOutput, calls=%fused_computation.16 | convolution fusion | flops 3222011904 | bytes 11534336 | tf_op jit(solution)/shard_map/dot_general | solution.py:837
  504.9 6.5 %lay_out.3 = bf16[2048,2048]{1,0:T(8,128)(2,1)} custom-call(bf16[256,2048]{1,0:T(8,128)(2,1)} %get-tuple-element.86.refs_0_, bf16[256,2048]{1,0:T(8,128)(2,1)} %collective-permute-done.37.refs_1_, bf16[256,2048]{1,0:T(8,128)(2,1)} %collective-permute-done.38.refs_2_, bf16[256,2048]{1,0:T(8,128)(2,1)} %collective-permute-done.39.refs_3_, ...), custom_call_target="tpu_custom_call" | custom-call | flops 1048576 | bytes 1048576 | tf_op jit(solution)/shard_map/lay_out/pallas_call | solution.py:469
  511.5 11.7 %collective-permute-done.42 = bf16[512,2048]{1,0:T(8,128)(2,1)} collective-permute-done((bf16[512,2048]{1,0:T(8,128)(2,1)}, bf16[512,2048]{1,0:T(8,128)(2,1)}, u32[]{:S(2)}, u32[]{:S(2)}) %collective-permute-start.42) | collective-permute-done | bytes 2097184 | tf_op jit(solution)/shard_map/ppermute | solution.py:54
  536.7 5.8 all-to-all-start.5
  551.6 10.0 %all-to-all-done.5.s_ref = bf16[8,64,1408]{2,1,0:T(8,128)(2,1)} async-done(((bf16[8,64,1408]{2,1,0:T(8,128)(2,1)}), bf16[8,64,1408]{2,1,0:T(8,128)(2,1)}, u32[]{:S(2)}, u32[]{:S(2)}) %all-to-all-start.5) | async-done | bytes 1441824 | tf_op jit(solution)/shard_map/all_to_all | solution.py:128
  561.6 7.7 %all-to-all-start.4 = ((bf16[8,64,384]{2,1,0:T(8,128)(2,1)}), bf16[8,64,384]{2,1,0:T(8,128)(2,1)S(1)}, u32[]{:S(2)}, u32[]{:S(2)}) async-start(bf16[8,64,384]{2,1,0:T(8,128)(2,1)} %bitcast.61), calls=%async_computation.6 | async-start | bytes 786432 | tf_op jit(solution)/shard_map/all_to_all | solution.py:128
  569.3 9.2 %join_columns.1 = (f32[64,11264]{1,0:T(8,128)}, f32[64,1]{1,0:T(8,128)}) custom-call(bf16[8,64,1408]{2,1,0:T(8,128)(2,1)} %all-to-all-done.5.s_ref, bf16[64,11264]{1,0:T(8,128)(2,1)} %w_ref.3, f32[64,1]{1,0:T(8,128)} %copy.50.gain_ref), custom_call_target="tpu_custom_call" | custom-call | flops 99999997952 | bytes 1048576 | tf_op jit(solution)/shard_map/join_columns/pallas_call | solution.py:597
  587.4 16.2 %collective-permute-done.48 = bf16[64,2048]{1,0:T(8,128)(2,1)S(1)} collective-permute-done((bf16[64,2048]{1,0:T(8,128)(2,1)}, bf16[64,2048]{1,0:T(8,128)(2,1)S(1)}, u32[]{:S(2)}, u32[]{:S(2)}) %collective-permute-start.48) | collective-permute-done | bytes 262176 | tf_op jit(solution)/shard_map/ppermute | solution.py:1015
  (282 shorter events, 156.8 us)
Async XLA Ops:
  15.5 63.4 %all-gather.7.cloned.1.call-start = ((), (), s32[]{:S(2)}) async-start(), calls=%async_computation.11 | async-start | bytes 1310720 | tf_op jit(solution)/shard_map/all_gather | solution.py:132
  25.1 29.9 %collective-permute-start.1 = (bf16[256,2048]{1,0:T(8,128)(2,1)}, bf16[256,2048]{1,0:T(8,128)(2,1)}, u32[]{:S(2)}, u32[]{:S(2)}) collective-permute-start(bf16[256,2048]{1,0:T(8,128)(2,1)} %fusion.2.refs_0_), channel_id=1, source_target_pairs={{0,2},{1,5},{2,0},{3,7},{4,6},{5,1},{6,4},{7,3},{8,10},{9,13},{10,... | collective-permute-start | bytes 3145736 | tf_op jit(solution)/shard_map/ppermute | solution.py:54
  33.9 69.5 %all-gather.5.cloned.1.call-start = ((), (), s32[]{:S(2)}) async-start(), calls=%async_computation.10 | async-start | bytes 1966080 | tf_op jit(solution)/shard_map/all_gather | solution.py:132
  34.2 34.3 %collective-permute-start.2 = (bf16[256,2048]{1,0:T(8,128)(2,1)}, bf16[256,2048]{1,0:T(8,128)(2,1)}, u32[]{:S(2)}, u32[]{:S(2)}) collective-permute-start(bf16[256,2048]{1,0:T(8,128)(2,1)} %fusion.2.refs_0_), channel_id=1, source_target_pairs={{0,4},{1,3},{2,6},{3,1},{4,0},{5,7},{6,2},{7,5},{8,12},{9,11},{10,... | collective-permute-start | bytes 3145736 | tf_op jit(solution)/shard_map/ppermute | solution.py:54
  61.4 22.9 %collective-permute-start.4 = (bf16[256,2048]{1,0:T(8,128)(2,1)}, bf16[256,2048]{1,0:T(8,128)(2,1)}, u32[]{:S(2)}, u32[]{:S(2)}) collective-permute-start(bf16[256,2048]{1,0:T(8,128)(2,1)} %fusion.2.refs_0_), channel_id=1, source_target_pairs={{0,1},{1,0},{2,3},{3,2},{4,5},{5,4},{6,7},{7,6},{8,9},{9,8},{10,11... | collective-permute-start | bytes 3145736 | tf_op jit(solution)/shard_map/ppermute | solution.py:58
  69.3 34.1 %collective-permute-start.7 = (bf16[256,2048]{1,0:T(8,128)(2,1)}, bf16[256,2048]{1,0:T(8,128)(2,1)}, u32[]{:S(2)}, u32[]{:S(2)}) collective-permute-start(bf16[256,2048]{1,0:T(8,128)(2,1)} %collective-permute-done.3.refs_3_), channel_id=1, source_target_pairs={{0,1},{1,0},{2,3},{3,2},{4,5},{5,4},{6,7},{7,6},{8,9},{9,8},{10,11... | collective-permute-start | bytes 3145736 | tf_op jit(solution)/shard_map/ppermute | solution.py:58
  79.0 40.6 %collective-permute-start.8 = (bf16[256,2048]{1,0:T(8,128)(2,1)}, bf16[256,2048]{1,0:T(8,128)(2,1)S(1)}, u32[]{:S(2)}, u32[]{:S(2)}) collective-permute-start(bf16[256,2048]{1,0:T(8,128)(2,1)} %all-gather.7.cloned.1.call-done.refs_0_), channel_id=1, source_target_pairs={{0,2},{1,5},{2,0},{3,7},{4,6},{5,1},{6,4},{7,3},{8,10},{9,13},{10,... | collective-permute-start | bytes 3145736 | tf_op jit(solution)/shard_map/ppermute | solution.py:54
  80.7 40.1 %all-to-all-start.1 = ((bf16[8,64,1408]{2,1,0:T(8,128)(2,1)}), bf16[8,64,1408]{2,1,0:T(8,128)(2,1)S(1)}, u32[]{:S(2)}, u32[]{:S(2)}) async-start(bf16[8,64,1408]{2,1,0:T(8,128)(2,1)} %split_columns.1), calls=%async_computation.1 | async-start | bytes 2883584 | tf_op jit(solution)/shard_map/all_to_all | solution.py:128
  84.3 143.2 %all-gather.9.cloned.1.call-start = ((), (), s32[]{:S(2)}) async-start(), calls=%async_computation.12 | async-start | bytes 7208960 | tf_op jit(solution)/shard_map/all_gather | solution.py:132
  84.3 37.7 %collective-permute-start.9 = (bf16[256,2048]{1,0:T(8,128)(2,1)}, bf16[256,2048]{1,0:T(8,128)(2,1)}, u32[]{:S(2)}, u32[]{:S(2)}) collective-permute-start(bf16[256,2048]{1,0:T(8,128)(2,1)} %all-gather.7.cloned.1.call-done.refs_0_), channel_id=1, source_target_pairs={{0,4},{1,3},{2,6},{3,1},{4,0},{5,7},{6,2},{7,5},{8,12},{9,11},{10,... | collective-permute-start | bytes 3145736 | tf_op jit(solution)/shard_map/ppermute | solution.py:54
  119.6 28.9 %collective-permute-start.10 = (bf16[256,2048]{1,0:T(8,128)(2,1)S(1)}, bf16[256,2048]{1,0:T(8,128)(2,1)}, u32[]{:S(2)}, u32[]{:S(2)}) collective-permute-start(bf16[256,2048]{1,0:T(8,128)(2,1)S(1)} %collective-permute-done.8.refs_1_), channel_id=1, source_target_pairs={{0,4},{1,3},{2,6},{3,1},{4,0},{5,7},{6,2},{7,5},{8,12},{9,11},{10,... | collective-permute-start | bytes 3145736 | tf_op jit(solution)/shard_map/ppermute | solution.py:54
  122.0 164.2 %all-gather.11.cloned.1.call-start = ((), (), s32[]{:S(2)}) async-start(), calls=%async_computation.13 | async-start | bytes 3604480 | tf_op jit(solution)/shard_map/all_gather | solution.py:132
  148.5 21.7 %collective-permute-start.14 = (bf16[256,2048]{1,0:T(8,128)(2,1)}, bf16[256,2048]{1,0:T(8,128)(2,1)}, u32[]{:S(2)}, u32[]{:S(2)}) collective-permute-start(bf16[256,2048]{1,0:T(8,128)(2,1)} %collective-permute-done.10.refs_3_), channel_id=1, source_target_pairs={{0,1},{1,0},{2,3},{3,2},{4,5},{5,4},{6,7},{7,6},{8,9},{9,8},{10,11... | collective-permute-start | bytes 3145736 | tf_op jit(solution)/shard_map/ppermute | solution.py:58
  181.3 23.1 %collective-permute-start.15 = (bf16[256,2048]{1,0:T(8,128)(2,1)}, bf16[256,2048]{1,0:T(8,128)(2,1)S(1)}, u32[]{:S(2)}, u32[]{:S(2)}) collective-permute-start(bf16[256,2048]{1,0:T(8,128)(2,1)} %get-tuple-element.66.refs_0_), channel_id=1, source_target_pairs={{0,2},{1,5},{2,0},{3,7},{4,6},{5,1},{6,4},{7,3},{8,10},{9,13},{10,... | collective-permute-start | bytes 3145736 | tf_op jit(solution)/shard_map/ppermute | solution.py:54
  181.6 27.8 %collective-permute-start.16 = (bf16[256,2048]{1,0:T(8,128)(2,1)}, bf16[256,2048]{1,0:T(8,128)(2,1)S(1)}, u32[]{:S(2)}, u32[]{:S(2)}) collective-permute-start(bf16[256,2048]{1,0:T(8,128)(2,1)} %get-tuple-element.66.refs_0_), channel_id=1, source_target_pairs={{0,4},{1,3},{2,6},{3,1},{4,0},{5,7},{6,2},{7,5},{8,12},{9,11},{10,... | collective-permute-start | bytes 3145736 | tf_op jit(solution)/shard_map/ppermute | solution.py:54
  222.4 269.0 %reduce-scatter.11.cloned.1.call-start = ((), (), s32[]{:S(2)}) async-start(), calls=%async_computation.17 | async-start | bytes 3604480 | tf_op jit(solution)/shard_map/reduce_scatter | solution.py:136
  225.0 24.6 %collective-permute-start.22 = (bf16[256,2048]{1,0:T(8,128)(2,1)S(1)}, bf16[256,2048]{1,0:T(8,128)(2,1)S(1)}, u32[]{:S(2)}, u32[]{:S(2)}) collective-permute-start(bf16[256,2048]{1,0:T(8,128)(2,1)S(1)} %copy-done.9), channel_id=1, source_target_pairs={{0,2},{1,5},{2,0},{3,7},{4,6},{5,1},{6,4},{7,3},{8,10},{9,13},{10,... | collective-permute-start | bytes 3145736 | tf_op jit(solution)/shard_map/ppermute | solution.py:54
  226.7 25.9 %collective-permute-start.23 = (bf16[256,2048]{1,0:T(8,128)(2,1)S(1)}, bf16[256,2048]{1,0:T(8,128)(2,1)S(1)}, u32[]{:S(2)}, u32[]{:S(2)}) collective-permute-start(bf16[256,2048]{1,0:T(8,128)(2,1)S(1)} %copy-done.9), channel_id=1, source_target_pairs={{0,4},{1,3},{2,6},{3,1},{4,0},{5,7},{6,2},{7,5},{8,12},{9,11},{10,... | collective-permute-start | bytes 3145736 | tf_op jit(solution)/shard_map/ppermute | solution.py:54
  317.8 193.7 %reduce-scatter.5.cloned.1.call-start = ((), (), s32[]{:S(2)}) async-start(), calls=%async_computation.14 | async-start | bytes 7208960 | tf_op jit(solution)/shard_map/reduce_scatter | solution.py:136
  325.9 33.7 %collective-permute-start.33 = (bf16[512,2048]{1,0:T(8,128)(2,1)}, bf16[512,2048]{1,0:T(8,128)(2,1)S(1)}, u32[]{:S(2)}, u32[]{:S(2)}) collective-permute-start(bf16[512,2048]{1,0:T(8,128)(2,1)} %convert_add_fusion.6), channel_id=1, source_target_pairs={{0,4},{1,3},{2,6},{3,1},{4,0},{5,7},{6,2},{7,5},{8,12},{9,11},{10,... | collective-permute-start | bytes 6291464 | tf_op jit(solution)/shard_map/ppermute | solution.py:54
  339.9 24.1 %collective-permute-start.31 = (bf16[512,2048]{1,0:T(8,128)(2,1)}, bf16[512,2048]{1,0:T(8,128)(2,1)}, u32[]{:S(2)}, u32[]{:S(2)}) collective-permute-start(bf16[512,2048]{1,0:T(8,128)(2,1)} %convolution_convert_fusion.5), channel_id=1, source_target_pairs={{0,1},{1,0},{2,3},{3,2},{4,5},{5,4},{6,7},{7,6},{8,9},{9,8},{10,11... | collective-permute-start | bytes 6291464 | tf_op jit(solution)/shard_map/ppermute | solution.py:58
  343.6 25.8 %collective-permute-start.32 = (bf16[512,2048]{1,0:T(8,128)(2,1)}, bf16[512,2048]{1,0:T(8,128)(2,1)}, u32[]{:S(2)}, u32[]{:S(2)}) collective-permute-start(bf16[512,2048]{1,0:T(8,128)(2,1)} %convolution_convert_fusion.4), channel_id=1, source_target_pairs={{0,1},{1,0},{2,3},{3,2},{4,5},{5,4},{6,7},{7,6},{8,9},{9,8},{10,11... | collective-permute-start | bytes 6291464 | tf_op jit(solution)/shard_map/ppermute | solution.py:58
  359.5 192.0 %reduce-scatter.7.cloned.1.call-start = ((), (), s32[]{:S(2)}) async-start(), calls=%async_computation.15 | async-start | bytes 1966080 | tf_op jit(solution)/shard_map/reduce_scatter | solution.py:136
  409.1 69.4 %collective-permute-start.37 = (bf16[256,2048]{1,0:T(8,128)(2,1)}, bf16[256,2048]{1,0:T(8,128)(2,1)}, u32[]{:S(2)}, u32[]{:S(2)}) collective-permute-start(bf16[256,2048]{1,0:T(8,128)(2,1)} %get-tuple-element.86.refs_0_), channel_id=1, source_target_pairs={{0,2},{1,5},{2,0},{3,7},{4,6},{5,1},{6,4},{7,3},{8,10},{9,13},{10,... | collective-permute-start | bytes 3145736 | tf_op jit(solution)/shard_map/ppermute | solution.py:90
  409.4 69.1 %collective-permute-start.38 = (bf16[256,2048]{1,0:T(8,128)(2,1)}, bf16[256,2048]{1,0:T(8,128)(2,1)}, u32[]{:S(2)}, u32[]{:S(2)}) collective-permute-start(bf16[256,2048]{1,0:T(8,128)(2,1)} %get-tuple-element.86.refs_0_), channel_id=1, source_target_pairs={{0,4},{1,3},{2,6},{3,1},{4,0},{5,7},{6,2},{7,5},{8,12},{9,11},{10,... | collective-permute-start | bytes 3145736 | tf_op jit(solution)/shard_map/ppermute | solution.py:90
  410.3 68.2 %collective-permute-start.39 = (bf16[256,2048]{1,0:T(8,128)(2,1)}, bf16[256,2048]{1,0:T(8,128)(2,1)}, u32[]{:S(2)}, u32[]{:S(2)}) collective-permute-start(bf16[256,2048]{1,0:T(8,128)(2,1)} %get-tuple-element.86.refs_0_), channel_id=1, source_target_pairs={{0,6},{1,7},{2,4},{3,5},{4,2},{5,3},{6,0},{7,1},{8,14},{9,15},{10,... | collective-permute-start | bytes 3145736 | tf_op jit(solution)/shard_map/ppermute | solution.py:90
  411.8 67.8 %collective-permute-start.35 = (bf16[512,2048]{1,0:T(8,128)(2,1)}, bf16[512,2048]{1,0:T(8,128)(2,1)}, u32[]{:S(2)}, u32[]{:S(2)}) collective-permute-start(bf16[512,2048]{1,0:T(8,128)(2,1)} %convert_add_fusion.3), channel_id=1, source_target_pairs={{0,4},{1,3},{2,6},{3,1},{4,0},{5,7},{6,2},{7,5},{8,12},{9,11},{10,... | collective-permute-start | bytes 6291464 | tf_op jit(solution)/shard_map/ppermute | solution.py:54
  484.5 27.1 %collective-permute-start.40 = (bf16[512,2048]{1,0:T(8,128)(2,1)}, bf16[512,2048]{1,0:T(8,128)(2,1)}, u32[]{:S(2)}, u32[]{:S(2)}) collective-permute-start(bf16[512,2048]{1,0:T(8,128)(2,1)} %convolution_convert_fusion.3), channel_id=1, source_target_pairs={{0,1},{1,0},{2,3},{3,2},{4,5},{5,4},{6,7},{7,6},{8,9},{9,8},{10,11... | collective-permute-start | bytes 6291464 | tf_op jit(solution)/shard_map/ppermute | solution.py:58
  490.3 33.0 %collective-permute-start.42 = (bf16[512,2048]{1,0:T(8,128)(2,1)}, bf16[512,2048]{1,0:T(8,128)(2,1)}, u32[]{:S(2)}, u32[]{:S(2)}) collective-permute-start(bf16[512,2048]{1,0:T(8,128)(2,1)} %add_convert_fusion), channel_id=1, source_target_pairs={{0,4},{1,3},{2,6},{3,1},{4,0},{5,7},{6,2},{7,5},{8,12},{9,11},{10,... | collective-permute-start | bytes 6291464 | tf_op jit(solution)/shard_map/ppermute | solution.py:54
  504.7 37.9 %collective-permute-start.36 = (bf16[256,2048]{1,0:T(8,128)(2,1)}, bf16[256,2048]{1,0:T(8,128)(2,1)}, u32[]{:S(2)}, u32[]{:S(2)}) collective-permute-start(bf16[256,2048]{1,0:T(8,128)(2,1)} %slice.167), channel_id=1, source_target_pairs={{0,2},{1,5},{2,0},{3,7},{4,6},{5,1},{6,4},{7,3},{8,10},{9,13},{10,... | collective-permute-start | bytes 3145736 | tf_op jit(solution)/shard_map/ppermute | solution.py:54
  536.7 25.0 %all-to-all-start.5 = ((bf16[8,64,1408]{2,1,0:T(8,128)(2,1)}), bf16[8,64,1408]{2,1,0:T(8,128)(2,1)}, u32[]{:S(2)}, u32[]{:S(2)}) async-start(bf16[8,64,1408]{2,1,0:T(8,128)(2,1)} %bitcast.18), calls=%async_computation.8 | async-start | bytes 2883584 | tf_op jit(solution)/shard_map/all_to_all | solution.py:128
  542.5 39.5 %reduce-scatter.9.cloned.1.call-start = ((), (), s32[]{:S(2)}) async-start(), calls=%async_computation.16 | async-start | bytes 1310720 | tf_op jit(solution)/shard_map/reduce_scatter | solution.py:136
  (80 other events, 1041.0 us)
Sparse Core Ops, SparseCore 0:
  34.0 27.5 all-gather.6
  68.5 34.7 all-gather.4
  122.1 105.3 all-gather.8
  228.9 57.2 all-gather.10
  317.9 54.5 reduce-scatter.10
  374.6 102.3 reduce-scatter.4
  511.7 32.1 reduce-scatter.6
  551.7 30.2 reduce-scatter.8

commit v6 on v5

--- a/solution.py
+++ b/solution.py
@@ -953,7 +953,7 @@
     all_grad = lay_out(grad_pieces)
     down_terms = outer_rows(hidden, all_grad)
     down_sums = scatter_dp(down_terms)
-    grad_gate_up = feed_backward(after(factors, down_terms), all_grad, down_part)
+    grad_gate_up = feed_backward(factors, all_grad, down_part)
 
     def rows_of(x, lo, hi):
         return lax.slice_in_dim(x, lo * tok, hi * tok, axis=0)

time: 619 us -> 626 us (1.011)
  waiting for transfers between devices: 136 us -> 148 us
    all_gather x4, waiting for transfers between devices: 19.8 us -> 31.4 us  [gather_dp(): return lax.all_gather(x, 'dp', axis=0, tiled=True)]
  transfers between devices with their start and end apart: 61 -> 61, of which waited for: 19 -> 19; matrix products, arithmetic and copies ran while one was open for 21% -> 20% of each run, Pallas kernels for 27% -> 27%
where the time goes in v6:
time: 626 us; the launch traced here: 618 us
  Pallas kernels  182 us (29%)
  waiting for transfers between devices  148 us (24%)
  matrix products  95 us (15%)
  starting transfers between devices  87.4 us (14%)
  other arithmetic  38.2 us (6%)
  blocking collectives  38 us (6%)
  between operations  15.5 us (2%)
  local copies, waits for them, and re-layouts  13.8 us (2%)
    ppermute x18, waiting for transfers between devices, swap_stage(): return lax.ppermute(x, 'ctx', pairs)  78.8 us
    pallas_call x1, Pallas kernels, attend_backward(): pl.pallas_call(kernel, grid_spec=pltpu.PrefetchScalarGridSpec(num_scalar_...  56 us
    dot_general x8, matrix products, nt(): lax.dot_general(a, b, (((1,), (1,)), ((), ())), preferred_element_type=F32)  41.9 us
    all_to_all x2, blocking collectives, exchange(): return lax.all_to_all(x, 'ctx', split_axis=0, concat_axis=0, tiled=False)  38 us
    dot_general x4, matrix products, outer_rows(): lax.dot_general(activations, gradients, (((0,), (0,)), ((), ())), preferr...  36.5 us
    all_gather x4, waiting for transfers between devices, gather_dp(): return lax.all_gather(x, 'dp', axis=0, tiled=True)  31.4 us
    ppermute x26, starting transfers between devices, swap_core(): return lax.ppermute(x, 'ctx', [(c, c ^ 1) for c in range(n_ctx)])  30.8 us
    pallas_call x1, Pallas kernels, attend_forward(): pl.pallas_call(kernel, grid_spec=pltpu.PrefetchScalarGridSpec(num_scalar_...  24.7 us
  transfers between devices with their start and end apart: 61, of which 19 were waited for; matrix products, arithmetic and copies ran while one was open for 20% of the time, Pallas kernels for 27%

profile of v6, /device:TPU:1, one launch (start us, length us, event | category | flops | bytes accessed | tf_op | source)
XLA Modules:
  0.0 618.1 jit_solution(10676831127464884601)
XLA Ops:
  25.1 8.7 %collective-permute-start.1 = (bf16[256,2048]{1,0:T(8,128)(2,1)}, bf16[256,2048]{1,0:T(8,128)(2,1)}, u32[]{:S(2)}, u32[]{:S(2)}) collective-permute-start(bf16[256,2048]{1,0:T(8,128)(2,1)} %fusion.2.refs_0_), channel_id=1, source_target_pairs={{0,2},{1,5},{2,0},{3,7},{4,6},{5,1},{6,4},{7,3},{8,10},{9,13},{10,... | collective-permute-start | bytes 3145736 | tf_op jit(solution)/shard_map/ppermute | solution.py:54
  34.3 20.7 %collective-permute-done.1.refs_1_ = bf16[256,2048]{1,0:T(8,128)(2,1)} collective-permute-done((bf16[256,2048]{1,0:T(8,128)(2,1)}, bf16[256,2048]{1,0:T(8,128)(2,1)}, u32[]{:S(2)}, u32[]{:S(2)}) %collective-permute-start.1) | collective-permute-done | bytes 1048608 | tf_op jit(solution)/shard_map/ppermute | solution.py:54
  61.4 7.0 %collective-permute-start.4 = (bf16[256,2048]{1,0:T(8,128)(2,1)}, bf16[256,2048]{1,0:T(8,128)(2,1)}, u32[]{:S(2)}, u32[]{:S(2)}) collective-permute-start(bf16[256,2048]{1,0:T(8,128)(2,1)} %fusion.2.refs_0_), channel_id=1, source_target_pairs={{0,1},{1,0},{2,3},{3,2},{4,5},{5,4},{6,7},{7,6},{8,9},{9,8},{10,11... | collective-permute-start | bytes 3145736 | tf_op jit(solution)/shard_map/ppermute | solution.py:58
  85.2 18.1 %all-gather.5.cloned.1.call-done.refs_8_ = bf16[2048,384]{1,0:T(8,128)(2,1)} async-done(((bf16[512,384]{1,0:T(8,128)(2,1)}), bf16[2048,384]{1,0:T(8,128)(2,1)}) %all-gather.5.cloned.1.call-update) | async-done | bytes 1572880 | tf_op jit(solution)/shard_map/all_gather | solution.py:132
  103.4 16.2 %project_qkv.1 = (bf16[2048,256]{1,0:T(8,128)(2,1)}, bf16[2048,256]{1,0:T(8,128)(2,1)}, bf16[2048,256]{1,0:T(8,128)(2,1)}, bf16[64,2048]{1,0:T(8,128)(2,1)}, bf1...) custom-call(s32[8]{0:T(128)} %copy-done.31, bf16[256,2048]{1,0:T(8,128)(2,1)} %fusion.2.refs_0_, ...), custom_call_target="tpu_custom_call" | custom-call | flops 99999997952 | bytes 1048576 | tf_op jit(solution)/shard_map/project_qkv/pallas_call | solution.py:262
  122.0 24.7 %attend_forward.1 = (bf16[2048,256]{1,0:T(8,128)(2,1)}, bf16[2048,256]{1,0:T(8,128)(2,1)}, f32[2048,256]{1,0:T(8,128)}, f32[8,4,256]{2,1,0:T(4,128)}) custom-call(s32[8]{0:T(128)} %select_reduce_fusion.1.slot_ref, s32[1,2048]{1,0:T(1,128)} %bitcast.66, bf16[2048,256]{1,0:T(8,128)(2,1)} %get-tuple-element.55.q_ref, ...), custom_call_target="tpu_custom_call" | custom-call | flops 99999997952 | bytes 1048576 | tf_op jit(solution)/shard_map/attend_forward/pallas_call | solution.py:676
  148.5 18.7 %all_to_all.30.a_ref = bf16[8,256,256]{2,1,0:T(8,128)(2,1)} all-to-all(bf16[8,256,256]{2,1,0:T(8,128)(2,1)} %bitcast.60), channel_id=1, replica_groups=mesh['dp'=4,'ctx'=8] {'ctx'}, dimensions={0} | all-to-all | bytes 2097152 | tf_op jit(solution)/shard_map/all_to_all | solution.py:128
  169.6 11.1 %project_out.1 = (f32[256,2048]{1,0:T(8,128)}, bf16[256,2048]{1,0:T(8,128)(2,1)}) custom-call(s32[8]{0:T(128)} %copy-done.31, bf16[8,256,256]{2,1,0:T(8,128)(2,1)} %all_to_all.30.a_ref, bf16[256,2048]{1,0:T(8,128)(2,1)} %all-gather.7.cloned.1.call-done.refs_0_, bf16[256,2048]{1,0:T(8,128)(2,1)} %copy-done.11, ...), custom_call_target="tpu_custom_call" | custom-call | flops 1048576 | bytes 1048576 | tf_op jit(solution)/shard_map/project_out/pallas_call | solution.py:332
  181.9 21.9 %collective-permute-done.15.refs_1_ = bf16[256,2048]{1,0:T(8,128)(2,1)S(1)} collective-permute-done((bf16[256,2048]{1,0:T(8,128)(2,1)}, bf16[256,2048]{1,0:T(8,128)(2,1)S(1)}, u32[]{:S(2)}, u32[]{:S(2)}) %collective-permute-start.15) | collective-permute-done | bytes 1048608 | tf_op jit(solution)/shard_map/ppermute | solution.py:54
  209.4 8.5 %collective-permute-done.17.refs_3_ = bf16[256,2048]{1,0:T(8,128)(2,1)} collective-permute-done((bf16[256,2048]{1,0:T(8,128)(2,1)S(1)}, bf16[256,2048]{1,0:T(8,128)(2,1)}, u32[]{:S(2)}, u32[]{:S(2)}) %collective-permute-start.17) | collective-permute-done | bytes 1048608 | tf_op jit(solution)/shard_map/ppermute | solution.py:54
  227.4 22.3 %feed_forward.1 = (bf16[2048,704]{1,0:T(8,128)(2,1)}, bf16[2048,1408]{1,0:T(8,128)(2,1)}, bf16[2048,2048]{1,0:T(8,128)(2,1)}) custom-call(bf16[256,2048]{1,0:T(8,128)(2,1)} %get-tuple-element.65.refs_0_, bf16[256,2048]{1,0:T(8,128)(2,1)} %copy-done.42, bf16[256,2048]{1,0:T(8,128)(2,1)} %copy-done.43, bf16[256,2048]{1,0:T(8,128)(2,1)} %collective-permute-done.17.refs_3_, ...), custom_call_target="tpu_custom_call" | custom-call | flops 99999997952 | bytes 1048576 | tf_op jit(solution)/shard_map/feed_forward/pallas_call | solution.py:381
  252.5 11.3 %collective-permute-done.24.refs_3_ = bf16[256,2048]{1,0:T(8,128)(2,1)S(1)} collective-permute-done((bf16[256,2048]{1,0:T(8,128)(2,1)S(1)}, bf16[256,2048]{1,0:T(8,128)(2,1)S(1)}, u32[]{:S(2)}, u32[]{:S(2)}) %collective-permute-start.24) | collective-permute-done | bytes 1048608 | tf_op jit(solution)/shard_map/ppermute | solution.py:54
  267.5 6.5 %lay_out.2.g_ref = bf16[2048,2048]{1,0:T(8,128)(2,1)} custom-call(bf16[256,2048]{1,0:T(8,128)(2,1)} %g_ref.1, bf16[256,2048]{1,0:T(8,128)(2,1)} %copy-done.20, bf16[256,2048]{1,0:T(8,128)(2,1)} %copy-done.21, bf16[256,2048]{1,0:T(8,128)(2,1)} %copy-done.22, bf16[256,2048]{1,0:T(8,128)(2,1)} %copy-done.24, bf16[256,2048]{1,0:T(8,128)(2,1)} %copy-done.25, ...), custom_call_target="tpu_custom_call" | custom-call | flops 1048576 | bytes 1048576 | tf_op jit(solution)/shard_map/lay_out/pallas_call | solution.py:469
  274.1 12.0 %all-gather.11.cloned.1.call-done.w_hbm = bf16[704,2048]{1,0:T(8,128)(2,1)} async-done(((bf16[176,2048]{1,0:T(8,128)(2,1)}), bf16[704,2048]{1,0:T(8,128)(2,1)}) %all-gather.11.cloned.1.call-update) | async-done | bytes 2883600 | tf_op jit(solution)/shard_map/all_gather | solution.py:132
  286.1 14.8 %feed_backward.1 = bf16[2048,1408]{1,0:T(8,128)(2,1)} custom-call(bf16[2048,1408]{1,0:T(8,128)(2,1)} %get-tuple-element.67.factor_ref, bf16[2048,2048]{1,0:T(8,128)(2,1)} %lay_out.2.g_ref, bf16[704,2048]{1,0:T(8,128)(2,1)} %all-gather.11.cloned.1.call-done.w_hbm), custom_call_target="tpu_custom_call" | custom-call | flops 99999997952 | bytes 1048576 | tf_op jit(solution)/shard_map/feed_backward/pallas_call | solution.py:425
  300.9 8.0 %convolution_convert_fusion.7 = bf16[512,2048]{1,0:T(8,128)(2,1)} fusion(bf16[2048,1408]{1,0:T(8,128)(2,1)} %all-gather.9.cloned.1.call-done.refs_8_, bf16[2048,1408]{1,0:T(8,128)(2,1)} %feed_backward.1), kind=kOutput, calls=%fused_computation.15 | convolution fusion | flops 2953838592 | bytes 9306112 | tf_op jit(solution)/shard_map/dot_general | solution.py:27
  309.6 6.3 %convolution_convert_fusion.6 = bf16[512,2048]{1,0:T(8,128)(2,1)} fusion(bf16[2048,1408]{1,0:T(8,128)(2,1)S(1)} %copy-done.39, bf16[2048,1408]{1,0:T(8,128)(2,1)} %feed_backward.1), kind=kOutput, calls=%fused_computation.14 | convolution fusion | flops 2953838592 | bytes 9306112 | tf_op jit(solution)/shard_map/dot_general | solution.py:27
  316.0 7.6 %convolution_convert_fusion.1 = bf16[704,2048]{1,0:T(8,128)(2,1)} fusion(bf16[2048,704]{1,0:T(8,128)(2,1)S(1)} %copy-done.46, bf16[2048,2048]{1,0:T(8,128)(2,1)S(1)} %bitcast.54), kind=kOutput, calls=%fused_computation.9 | convolution fusion | flops 5907021824 | bytes 14155776 | tf_op jit(solution)/shard_map/dot_general | solution.py:837
  324.1 8.0 %convert_add_fusion.6 = bf16[512,2048]{1,0:T(8,128)(2,1)} fusion(bf16[512,2048]{1,0:T(8,128)(2,1)S(1)} %collective-permute-done.29, bf16[2048,1408]{1,0:T(8,128)(2,1)} %all-gather.9.cloned.1.call-done.refs_8_, bf16[2048,1408]{1,0:T(8,128)(2,1)} %feed_backward.1), kind=kOutput, calls=%fused_computation.8 | convolution fusion | flops 2955935744 | bytes 11403264 | tf_op jit(solution)/shard_map/dot_general | solution.py:27
  333.3 9.7 %convert_add_fusion.5 = f32[512,2048]{1,0:T(8,128)} fusion(bf16[512,2048]{1,0:T(8,128)(2,1)} %collective-permute-done.30, bf16[2048,1408]{1,0:T(8,128)(2,1)} %all-gather.9.cloned.1.call-done.refs_8_, bf16[2048,1408]{1,0:T(8,128)(2,1)} %feed_backward.1), kind=kOutput, calls=%fused_computation.7 | convolution fusion | flops 2954887168 | bytes 13500416 | tf_op jit(solution)/shard_map/dot_general | solution.py:27
  350.0 15.6 %convolution_convert_fusion = bf16[2048,1408]{1,0:T(8,128)(2,1)} fusion(bf16[2048,2048]{1,0:T(8,128)(2,1)S(1)} %bitcast.74, bf16[2048,1408]{1,0:T(8,128)(2,1)S(1)} %bitcast.72), kind=kOutput, calls=%fused_computation | convolution fusion | flops 11814043648 | bytes 19922944 | tf_op jit(solution)/shard_map/dot_general | solution.py:837
  384.8 11.1 %branch_back.1 = (f32[256,2048]{1,0:T(8,128)}, bf16[256,2048]{1,0:T(8,128)(2,1)}, bf16[8,256,256]{2,1,0:T(8,128)(2,1)}) custom-call(s32[8]{0:T(128)} %copy-done.31, f32[256,2048]{1,0:T(8,128)} %slice_add_fusion.2.d_ref, f32[256,2048]{1,0:T(8,128)} %get-tuple-element.64.state_ref, bf16[256,2048]{1,0:T(8,128)(2,1)} %g_ref.1, ...), custom_call_target="tpu_custom_call" | custom-call | flops 1048576 | bytes 1048576 | tf_op jit(solution)/shard_map/branch_back/pallas_call | solution.py:520
  395.9 19.3 %all_to_all.31 = bf16[8,256,256]{2,1,0:T(8,128)(2,1)} all-to-all(bf16[8,256,256]{2,1,0:T(8,128)(2,1)} %get-tuple-element.75), channel_id=1, replica_groups=mesh['dp'=4,'ctx'=8] {'ctx'}, dimensions={0} | all-to-all | bytes 2097152 | tf_op jit(solution)/shard_map/all_to_all | solution.py:128
  418.9 56.0 %attend_backward.1 = bf16[2048,384]{1,0:T(8,128)(2,1)} custom-call(s32[8]{0:T(128)} %select_reduce_fusion.1.slot_ref, s32[1,2048]{1,0:T(1,128)} %bitcast.67, bf16[2048,256]{1,0:T(8,128)(2,1)} %get-tuple-element.55.q_ref, bf16[2048,256]{1,0:T(8,128)(2,1)} %get-tuple-element.56.k_ref, bf16[64,2048]{1,0:T(8,128)(2,1)} %get-tuple-element.78.kt_ref, ...), custom_call_target="tpu_custom_call" | custom-call | flops 20000000000 | bytes 1048576 | tf_op jit(solution)/shard_map/attend_backward/pallas_call | solution.py:808
  474.9 9.7 %convolution_convert_fusion.8 = bf16[2048,384]{1,0:T(8,128)(2,1)} fusion(bf16[2048,2048]{1,0:T(8,128)(2,1)} %get-tuple-element.82, bf16[2048,384]{1,0:T(8,128)(2,1)} %attend_backward.1), kind=kOutput, calls=%fused_computation.16 | convolution fusion | flops 3222011904 | bytes 11534336 | tf_op jit(solution)/shard_map/dot_general | solution.py:837
  511.0 6.5 %lay_out.3 = bf16[2048,2048]{1,0:T(8,128)(2,1)} custom-call(bf16[256,2048]{1,0:T(8,128)(2,1)} %get-tuple-element.84.refs_0_, bf16[256,2048]{1,0:T(8,128)(2,1)} %collective-permute-done.37.refs_1_, bf16[256,2048]{1,0:T(8,128)(2,1)} %collective-permute-done.38.refs_2_, bf16[256,2048]{1,0:T(8,128)(2,1)} %collective-permute-done.39.refs_3_, ...), custom_call_target="tpu_custom_call" | custom-call | flops 1048576 | bytes 1048576 | tf_op jit(solution)/shard_map/lay_out/pallas_call | solution.py:469
  517.6 11.7 %collective-permute-done.42 = bf16[512,2048]{1,0:T(8,128)(2,1)} collective-permute-done((bf16[512,2048]{1,0:T(8,128)(2,1)}, bf16[512,2048]{1,0:T(8,128)(2,1)}, u32[]{:S(2)}, u32[]{:S(2)}) %collective-permute-start.42) | collective-permute-done | bytes 2097184 | tf_op jit(solution)/shard_map/ppermute | solution.py:54
  542.7 5.9 all-to-all-start.5
  557.7 10.0 %all-to-all-done.5.s_ref = bf16[8,64,1408]{2,1,0:T(8,128)(2,1)} async-done(((bf16[8,64,1408]{2,1,0:T(8,128)(2,1)}), bf16[8,64,1408]{2,1,0:T(8,128)(2,1)}, u32[]{:S(2)}, u32[]{:S(2)}) %all-to-all-start.5) | async-done | bytes 1441824 | tf_op jit(solution)/shard_map/all_to_all | solution.py:128
  567.7 7.7 %all-to-all-start.4 = ((bf16[8,64,384]{2,1,0:T(8,128)(2,1)}), bf16[8,64,384]{2,1,0:T(8,128)(2,1)S(1)}, u32[]{:S(2)}, u32[]{:S(2)}) async-start(bf16[8,64,384]{2,1,0:T(8,128)(2,1)} %bitcast.63), calls=%async_computation.6 | async-start | bytes 786432 | tf_op jit(solution)/shard_map/all_to_all | solution.py:128
  575.4 9.2 %join_columns.1 = (f32[64,11264]{1,0:T(8,128)}, f32[64,1]{1,0:T(8,128)}) custom-call(bf16[8,64,1408]{2,1,0:T(8,128)(2,1)} %all-to-all-done.5.s_ref, bf16[64,11264]{1,0:T(8,128)(2,1)} %w_ref.3, f32[64,1]{1,0:T(8,128)} %copy.50.gain_ref), custom_call_target="tpu_custom_call" | custom-call | flops 99999997952 | bytes 1048576 | tf_op jit(solution)/shard_map/join_columns/pallas_call | solution.py:597
  593.7 16.3 %collective-permute-done.48 = bf16[64,2048]{1,0:T(8,128)(2,1)S(1)} collective-permute-done((bf16[64,2048]{1,0:T(8,128)(2,1)}, bf16[64,2048]{1,0:T(8,128)(2,1)S(1)}, u32[]{:S(2)}, u32[]{:S(2)}) %collective-permute-start.48) | collective-permute-done | bytes 262176 | tf_op jit(solution)/shard_map/ppermute | solution.py:1015
  (291 shorter events, 161.1 us)
Async XLA Ops:
  15.5 63.4 %all-gather.7.cloned.1.call-start = ((), (), s32[]{:S(2)}) async-start(), calls=%async_computation.11 | async-start | bytes 1310720 | tf_op jit(solution)/shard_map/all_gather | solution.py:132
  25.1 29.9 %collective-permute-start.1 = (bf16[256,2048]{1,0:T(8,128)(2,1)}, bf16[256,2048]{1,0:T(8,128)(2,1)}, u32[]{:S(2)}, u32[]{:S(2)}) collective-permute-start(bf16[256,2048]{1,0:T(8,128)(2,1)} %fusion.2.refs_0_), channel_id=1, source_target_pairs={{0,2},{1,5},{2,0},{3,7},{4,6},{5,1},{6,4},{7,3},{8,10},{9,13},{10,... | collective-permute-start | bytes 3145736 | tf_op jit(solution)/shard_map/ppermute | solution.py:54
  33.9 69.5 %all-gather.5.cloned.1.call-start = ((), (), s32[]{:S(2)}) async-start(), calls=%async_computation.10 | async-start | bytes 1966080 | tf_op jit(solution)/shard_map/all_gather | solution.py:132
  34.2 34.3 %collective-permute-start.2 = (bf16[256,2048]{1,0:T(8,128)(2,1)}, bf16[256,2048]{1,0:T(8,128)(2,1)}, u32[]{:S(2)}, u32[]{:S(2)}) collective-permute-start(bf16[256,2048]{1,0:T(8,128)(2,1)} %fusion.2.refs_0_), channel_id=1, source_target_pairs={{0,4},{1,3},{2,6},{3,1},{4,0},{5,7},{6,2},{7,5},{8,12},{9,11},{10,... | collective-permute-start | bytes 3145736 | tf_op jit(solution)/shard_map/ppermute | solution.py:54
  61.4 22.9 %collective-permute-start.4 = (bf16[256,2048]{1,0:T(8,128)(2,1)}, bf16[256,2048]{1,0:T(8,128)(2,1)}, u32[]{:S(2)}, u32[]{:S(2)}) collective-permute-start(bf16[256,2048]{1,0:T(8,128)(2,1)} %fusion.2.refs_0_), channel_id=1, source_target_pairs={{0,1},{1,0},{2,3},{3,2},{4,5},{5,4},{6,7},{7,6},{8,9},{9,8},{10,11... | collective-permute-start | bytes 3145736 | tf_op jit(solution)/shard_map/ppermute | solution.py:58
  69.3 34.1 %collective-permute-start.7 = (bf16[256,2048]{1,0:T(8,128)(2,1)}, bf16[256,2048]{1,0:T(8,128)(2,1)}, u32[]{:S(2)}, u32[]{:S(2)}) collective-permute-start(bf16[256,2048]{1,0:T(8,128)(2,1)} %collective-permute-done.3.refs_3_), channel_id=1, source_target_pairs={{0,1},{1,0},{2,3},{3,2},{4,5},{5,4},{6,7},{7,6},{8,9},{9,8},{10,11... | collective-permute-start | bytes 3145736 | tf_op jit(solution)/shard_map/ppermute | solution.py:58
  79.0 40.6 %collective-permute-start.8 = (bf16[256,2048]{1,0:T(8,128)(2,1)}, bf16[256,2048]{1,0:T(8,128)(2,1)S(1)}, u32[]{:S(2)}, u32[]{:S(2)}) collective-permute-start(bf16[256,2048]{1,0:T(8,128)(2,1)} %all-gather.7.cloned.1.call-done.refs_0_), channel_id=1, source_target_pairs={{0,2},{1,5},{2,0},{3,7},{4,6},{5,1},{6,4},{7,3},{8,10},{9,13},{10,... | collective-permute-start | bytes 3145736 | tf_op jit(solution)/shard_map/ppermute | solution.py:54
  80.7 40.1 %all-to-all-start.1 = ((bf16[8,64,1408]{2,1,0:T(8,128)(2,1)}), bf16[8,64,1408]{2,1,0:T(8,128)(2,1)S(1)}, u32[]{:S(2)}, u32[]{:S(2)}) async-start(bf16[8,64,1408]{2,1,0:T(8,128)(2,1)} %split_columns.1), calls=%async_computation.1 | async-start | bytes 2883584 | tf_op jit(solution)/shard_map/all_to_all | solution.py:128
  84.3 143.2 %all-gather.9.cloned.1.call-start = ((), (), s32[]{:S(2)}) async-start(), calls=%async_computation.12 | async-start | bytes 7208960 | tf_op jit(solution)/shard_map/all_gather | solution.py:132
  84.3 37.7 %collective-permute-start.9 = (bf16[256,2048]{1,0:T(8,128)(2,1)}, bf16[256,2048]{1,0:T(8,128)(2,1)}, u32[]{:S(2)}, u32[]{:S(2)}) collective-permute-start(bf16[256,2048]{1,0:T(8,128)(2,1)} %all-gather.7.cloned.1.call-done.refs_0_), channel_id=1, source_target_pairs={{0,4},{1,3},{2,6},{3,1},{4,0},{5,7},{6,2},{7,5},{8,12},{9,11},{10,... | collective-permute-start | bytes 3145736 | tf_op jit(solution)/shard_map/ppermute | solution.py:54
  119.6 28.9 %collective-permute-start.10 = (bf16[256,2048]{1,0:T(8,128)(2,1)S(1)}, bf16[256,2048]{1,0:T(8,128)(2,1)}, u32[]{:S(2)}, u32[]{:S(2)}) collective-permute-start(bf16[256,2048]{1,0:T(8,128)(2,1)S(1)} %collective-permute-done.8.refs_1_), channel_id=1, source_target_pairs={{0,4},{1,3},{2,6},{3,1},{4,0},{5,7},{6,2},{7,5},{8,12},{9,11},{10,... | collective-permute-start | bytes 3145736 | tf_op jit(solution)/shard_map/ppermute | solution.py:54
  122.0 164.1 %all-gather.11.cloned.1.call-start = ((), (), s32[]{:S(2)}) async-start(), calls=%async_computation.13 | async-start | bytes 3604480 | tf_op jit(solution)/shard_map/all_gather | solution.py:132
  180.7 23.1 %collective-permute-start.15 = (bf16[256,2048]{1,0:T(8,128)(2,1)}, bf16[256,2048]{1,0:T(8,128)(2,1)S(1)}, u32[]{:S(2)}, u32[]{:S(2)}) collective-permute-start(bf16[256,2048]{1,0:T(8,128)(2,1)} %get-tuple-element.65.refs_0_), channel_id=1, source_target_pairs={{0,2},{1,5},{2,0},{3,7},{4,6},{5,1},{6,4},{7,3},{8,10},{9,13},{10,... | collective-permute-start | bytes 3145736 | tf_op jit(solution)/shard_map/ppermute | solution.py:54
  181.0 27.8 %collective-permute-start.16 = (bf16[256,2048]{1,0:T(8,128)(2,1)}, bf16[256,2048]{1,0:T(8,128)(2,1)S(1)}, u32[]{:S(2)}, u32[]{:S(2)}) collective-permute-start(bf16[256,2048]{1,0:T(8,128)(2,1)} %get-tuple-element.65.refs_0_), channel_id=1, source_target_pairs={{0,4},{1,3},{2,6},{3,1},{4,0},{5,7},{6,2},{7,5},{8,12},{9,11},{10,... | collective-permute-start | bytes 3145736 | tf_op jit(solution)/shard_map/ppermute | solution.py:54
  221.7 275.7 %reduce-scatter.11.cloned.1.call-start = ((), (), s32[]{:S(2)}) async-start(), calls=%async_computation.17 | async-start | bytes 3604480 | tf_op jit(solution)/shard_map/reduce_scatter | solution.py:136
  224.4 25.4 %collective-permute-start.22 = (bf16[256,2048]{1,0:T(8,128)(2,1)S(1)}, bf16[256,2048]{1,0:T(8,128)(2,1)S(1)}, u32[]{:S(2)}, u32[]{:S(2)}) collective-permute-start(bf16[256,2048]{1,0:T(8,128)(2,1)S(1)} %copy-done.9), channel_id=1, source_target_pairs={{0,2},{1,5},{2,0},{3,7},{4,6},{5,1},{6,4},{7,3},{8,10},{9,13},{10,... | collective-permute-start | bytes 3145736 | tf_op jit(solution)/shard_map/ppermute | solution.py:54
  226.1 25.9 %collective-permute-start.23 = (bf16[256,2048]{1,0:T(8,128)(2,1)S(1)}, bf16[256,2048]{1,0:T(8,128)(2,1)S(1)}, u32[]{:S(2)}, u32[]{:S(2)}) collective-permute-start(bf16[256,2048]{1,0:T(8,128)(2,1)S(1)} %copy-done.9), channel_id=1, source_target_pairs={{0,4},{1,3},{2,6},{3,1},{4,0},{5,7},{6,2},{7,5},{8,12},{9,11},{10,... | collective-permute-start | bytes 3145736 | tf_op jit(solution)/shard_map/ppermute | solution.py:54
  323.6 193.9 %reduce-scatter.5.cloned.1.call-start = ((), (), s32[]{:S(2)}) async-start(), calls=%async_computation.14 | async-start | bytes 7208960 | tf_op jit(solution)/shard_map/reduce_scatter | solution.py:136
  332.1 33.8 %collective-permute-start.33 = (bf16[512,2048]{1,0:T(8,128)(2,1)}, bf16[512,2048]{1,0:T(8,128)(2,1)S(1)}, u32[]{:S(2)}, u32[]{:S(2)}) collective-permute-start(bf16[512,2048]{1,0:T(8,128)(2,1)} %convert_add_fusion.6), channel_id=1, source_target_pairs={{0,4},{1,3},{2,6},{3,1},{4,0},{5,7},{6,2},{7,5},{8,12},{9,11},{10,... | collective-permute-start | bytes 6291464 | tf_op jit(solution)/shard_map/ppermute | solution.py:54
  346.3 24.1 %collective-permute-start.32 = (bf16[512,2048]{1,0:T(8,128)(2,1)}, bf16[512,2048]{1,0:T(8,128)(2,1)}, u32[]{:S(2)}, u32[]{:S(2)}) collective-permute-start(bf16[512,2048]{1,0:T(8,128)(2,1)} %convolution_convert_fusion.4), channel_id=1, source_target_pairs={{0,1},{1,0},{2,3},{3,2},{4,5},{5,4},{6,7},{7,6},{8,9},{9,8},{10,11... | collective-permute-start | bytes 6291464 | tf_op jit(solution)/shard_map/ppermute | solution.py:58
  350.0 25.1 %collective-permute-start.31 = (bf16[512,2048]{1,0:T(8,128)(2,1)}, bf16[512,2048]{1,0:T(8,128)(2,1)}, u32[]{:S(2)}, u32[]{:S(2)}) collective-permute-start(bf16[512,2048]{1,0:T(8,128)(2,1)} %convolution_convert_fusion.5), channel_id=1, source_target_pairs={{0,1},{1,0},{2,3},{3,2},{4,5},{5,4},{6,7},{7,6},{8,9},{9,8},{10,11... | collective-permute-start | bytes 6291464 | tf_op jit(solution)/shard_map/ppermute | solution.py:58
  365.7 192.0 %reduce-scatter.7.cloned.1.call-start = ((), (), s32[]{:S(2)}) async-start(), calls=%async_computation.15 | async-start | bytes 1966080 | tf_op jit(solution)/shard_map/reduce_scatter | solution.py:136
  415.2 69.4 %collective-permute-start.37 = (bf16[256,2048]{1,0:T(8,128)(2,1)}, bf16[256,2048]{1,0:T(8,128)(2,1)}, u32[]{:S(2)}, u32[]{:S(2)}) collective-permute-start(bf16[256,2048]{1,0:T(8,128)(2,1)} %get-tuple-element.84.refs_0_), channel_id=1, source_target_pairs={{0,2},{1,5},{2,0},{3,7},{4,6},{5,1},{6,4},{7,3},{8,10},{9,13},{10,... | collective-permute-start | bytes 3145736 | tf_op jit(solution)/shard_map/ppermute | solution.py:90
  415.5 69.1 %collective-permute-start.38 = (bf16[256,2048]{1,0:T(8,128)(2,1)}, bf16[256,2048]{1,0:T(8,128)(2,1)}, u32[]{:S(2)}, u32[]{:S(2)}) collective-permute-start(bf16[256,2048]{1,0:T(8,128)(2,1)} %get-tuple-element.84.refs_0_), channel_id=1, source_target_pairs={{0,4},{1,3},{2,6},{3,1},{4,0},{5,7},{6,2},{7,5},{8,12},{9,11},{10,... | collective-permute-start | bytes 3145736 | tf_op jit(solution)/shard_map/ppermute | solution.py:90
  416.4 68.2 %collective-permute-start.39 = (bf16[256,2048]{1,0:T(8,128)(2,1)}, bf16[256,2048]{1,0:T(8,128)(2,1)}, u32[]{:S(2)}, u32[]{:S(2)}) collective-permute-start(bf16[256,2048]{1,0:T(8,128)(2,1)} %get-tuple-element.84.refs_0_), channel_id=1, source_target_pairs={{0,6},{1,7},{2,4},{3,5},{4,2},{5,3},{6,0},{7,1},{8,14},{9,15},{10,... | collective-permute-start | bytes 3145736 | tf_op jit(solution)/shard_map/ppermute | solution.py:90
  417.9 67.8 %collective-permute-start.35 = (bf16[512,2048]{1,0:T(8,128)(2,1)}, bf16[512,2048]{1,0:T(8,128)(2,1)}, u32[]{:S(2)}, u32[]{:S(2)}) collective-permute-start(bf16[512,2048]{1,0:T(8,128)(2,1)} %convert_add_fusion.3), channel_id=1, source_target_pairs={{0,4},{1,3},{2,6},{3,1},{4,0},{5,7},{6,2},{7,5},{8,12},{9,11},{10,... | collective-permute-start | bytes 6291464 | tf_op jit(solution)/shard_map/ppermute | solution.py:54
  490.5 27.1 %collective-permute-start.40 = (bf16[512,2048]{1,0:T(8,128)(2,1)}, bf16[512,2048]{1,0:T(8,128)(2,1)}, u32[]{:S(2)}, u32[]{:S(2)}) collective-permute-start(bf16[512,2048]{1,0:T(8,128)(2,1)} %convolution_convert_fusion.3), channel_id=1, source_target_pairs={{0,1},{1,0},{2,3},{3,2},{4,5},{5,4},{6,7},{7,6},{8,9},{9,8},{10,11... | collective-permute-start | bytes 6291464 | tf_op jit(solution)/shard_map/ppermute | solution.py:58
  496.3 33.0 %collective-permute-start.42 = (bf16[512,2048]{1,0:T(8,128)(2,1)}, bf16[512,2048]{1,0:T(8,128)(2,1)}, u32[]{:S(2)}, u32[]{:S(2)}) collective-permute-start(bf16[512,2048]{1,0:T(8,128)(2,1)} %add_convert_fusion), channel_id=1, source_target_pairs={{0,4},{1,3},{2,6},{3,1},{4,0},{5,7},{6,2},{7,5},{8,12},{9,11},{10,... | collective-permute-start | bytes 6291464 | tf_op jit(solution)/shard_map/ppermute | solution.py:54
  510.7 37.9 %collective-permute-start.36 = (bf16[256,2048]{1,0:T(8,128)(2,1)}, bf16[256,2048]{1,0:T(8,128)(2,1)}, u32[]{:S(2)}, u32[]{:S(2)}) collective-permute-start(bf16[256,2048]{1,0:T(8,128)(2,1)} %slice.167), channel_id=1, source_target_pairs={{0,2},{1,5},{2,0},{3,7},{4,6},{5,1},{6,4},{7,3},{8,10},{9,13},{10,... | collective-permute-start | bytes 3145736 | tf_op jit(solution)/shard_map/ppermute | solution.py:54
  542.7 25.0 %all-to-all-start.5 = ((bf16[8,64,1408]{2,1,0:T(8,128)(2,1)}), bf16[8,64,1408]{2,1,0:T(8,128)(2,1)}, u32[]{:S(2)}, u32[]{:S(2)}) async-start(bf16[8,64,1408]{2,1,0:T(8,128)(2,1)} %bitcast.18), calls=%async_computation.8 | async-start | bytes 2883584 | tf_op jit(solution)/shard_map/all_to_all | solution.py:128
  548.6 39.7 %reduce-scatter.9.cloned.1.call-start = ((), (), s32[]{:S(2)}) async-start(), calls=%async_computation.16 | async-start | bytes 1310720 | tf_op jit(solution)/shard_map/reduce_scatter | solution.py:136
  588.3 21.7 %collective-permute-start.48 = (bf16[64,2048]{1,0:T(8,128)(2,1)}, bf16[64,2048]{1,0:T(8,128)(2,1)S(1)}, u32[]{:S(2)}, u32[]{:S(2)}) collective-permute-start(bf16[64,2048]{1,0:T(8,128)(2,1)} %reduce-scatter.9.cloned.1.call-done), channel_id=1, source_target_pairs={{0,0},{8,1},{16,2},{24,3},{1,4},{9,5},{17,6},{25,7},{2,8},{10,9},{... | collective-permute-start | bytes 786440 | tf_op jit(solution)/shard_map/ppermute | solution.py:1015
  (84 other events, 1090.7 us)
Sparse Core Ops, SparseCore 0:
  34.0 27.5 all-gather.6
  68.5 34.7 all-gather.4
  122.1 105.2 all-gather.8
  228.9 57.2 all-gather.10
  323.8 54.4 reduce-scatter.10
  380.5 102.3 reduce-scatter.4
  517.7 32.4 reduce-scatter.6
  557.8 30.4 reduce-scatter.8
